TPU v7x, 256 devices: a whole 4x4x8 slice. The times are simulated.
256 devices in a mesh: wide: 32 (over z, y_lo, core), narrow: 8 (over y_hi, x).
Axes of the slice: x: 4, y: 4 (y_hi: 2, y_lo: 2; y = y_hi * 2 + y_lo), z: 8, core: 2. Of those that a mesh axis runs over, the one named last changes fastest.
Arguments:
- tokens: bfloat16 [3072, 8192], P('wide', 'narrow')
- grad_out: bfloat16 [3072, 8192], P('wide', 'narrow'), may hold values from -6 to 6
- selected: int32 [384], replicated, may hold values from 0 to 3071, as said below
- gain: float32 [8192], P('narrow'), may hold values from 0.1 to 1.9
- router_weight: float32 [8192], P('narrow'), may hold values from -0.0625 to 0.0625
- w_gate: bfloat16 [8192, 32768], P('narrow', 'wide'), may hold values from -0.0625 to 0.0625
- w_up: bfloat16 [8192, 32768], P('narrow', 'wide'), may hold values from -0.0625 to 0.0625
- w_down: bfloat16 [32768, 8192], P('wide', 'narrow'), may hold values from -0.03125 to 0.03125
Outputs:
- grad_x: bfloat16 [3072, 8192], P('wide', 'narrow')
- grad_gate: bfloat16 [8192, 32768], P('narrow', 'wide')
- grad_up: bfloat16 [8192, 32768], P('narrow', 'wide')
- grad_down: bfloat16 [32768, 8192], P('wide', 'narrow')
- grad_gain: float32 [8192], P('narrow')
- grad_router: float32 [8192], P('narrow')
Inputs may be any that keep to these rules, and one draw needn't show every extreme that they name: The ids rise strictly. Each aligned block of 96 token ids holds at most 24 selected ids, and some block holds exactly 24.
All inputs are finite; a program needn't handle non-finite values.
Results may differ from a plain program's by a relative error of at most 0.008.
Values may be sent and summed in bfloat16 or wider, within the bound.
No kernel may reach another device: no remote copies, remote signals or barrier semaphores. Data moves between devices by JAX's collectives and lax.ppermute only.
A program may use at most 128 MiB of HBM per device.

v0:
```python
import jax
import jax.numpy as jnp
from jax import lax
from jax.sharding import PartitionSpec as P

D = 8192


eps = 1e-06


def slot_rows(selected, block, count, capacity):
    start = block * count
    offset = jnp.sum((selected < start).astype(jnp.int32))
    upto = jnp.sum((selected < start + count).astype(jnp.int32))
    places = offset + jnp.arange(capacity, dtype=jnp.int32)
    valid = places < upto
    picked = jnp.take(selected, jnp.minimum(places, selected.shape[0] - 1)) - start
    return (jnp.where(valid, picked, count), valid)


def local(tokens, grad_out, selected, gain, router_weight, w_gate, w_up, w_down):
    tok_dev = tokens.shape[0]
    capacity = tok_dev // 4
    block = lax.axis_index("wide")
    local_rows, valid = slot_rows(selected, block, tok_dev, capacity)
    safe_rows = jnp.minimum(local_rows, tok_dev - 1)
    x_slots = jnp.where(
        valid[:, None], jnp.take(tokens, safe_rows, axis=0), jnp.zeros((), jnp.bfloat16)
    )
    g_slots = jnp.where(
        valid[:, None], jnp.take(grad_out, safe_rows, axis=0), jnp.zeros((), jnp.bfloat16)
    )
    sel_rows, grad_rows = (
        lax.all_gather(x_slots, "wide", axis=0, tiled=True),
        lax.all_gather(g_slots, "wide", axis=0, tiled=True),
    )
    sel32 = sel_rows.astype(jnp.float32)
    squares, logit = lax.psum(
        (jnp.sum(sel32 * sel32, axis=1), jnp.sum(sel32 * router_weight[None, :], axis=1)), "narrow"
    )
    scales = lax.rsqrt(squares / D + eps)
    normed = (sel32 * scales[:, None] * gain[None, :]).astype(jnp.bfloat16)
    gate, up = lax.psum(
        (
            jnp.dot(normed, w_gate, preferred_element_type=jnp.float32),
            jnp.dot(normed, w_up, preferred_element_type=jnp.float32),
        ),
        "narrow",
    )
    sigma = jax.nn.sigmoid(gate)
    hidden = (gate * sigma * up).astype(jnp.bfloat16)
    back = lax.psum(
        jnp.einsum("rd,fd->rf", grad_rows, w_down, preferred_element_type=jnp.float32), "narrow"
    )
    router_grad = lax.psum(jnp.sum(hidden.astype(jnp.float32) * back, axis=1), "wide")
    d_hidden = logit[:, None] * back
    d_gate = (d_hidden * up * (sigma + gate * sigma * (1.0 - sigma))).astype(jnp.bfloat16)
    d_up = (d_hidden * gate * sigma).astype(jnp.bfloat16)
    d_out = (logit[:, None] * grad_rows.astype(jnp.float32)).astype(jnp.bfloat16)
    grad_down = jnp.einsum("rf,rd->fd", hidden, d_out, preferred_element_type=jnp.float32).astype(
        jnp.bfloat16
    )
    grad_gate = jnp.einsum("rd,rf->df", normed, d_gate, preferred_element_type=jnp.float32).astype(
        jnp.bfloat16
    )
    grad_up = jnp.einsum("rd,rf->df", normed, d_up, preferred_element_type=jnp.float32).astype(
        jnp.bfloat16
    )
    grad_router = jnp.sum(sel32 * router_grad[:, None], axis=0)
    first = jnp.einsum("rf,df->rd", d_gate, w_gate, preferred_element_type=jnp.float32)
    d_normed = lax.psum_scatter(
        first + jnp.einsum("rf,df->rd", d_up, w_up, preferred_element_type=jnp.float32),
        "wide",
        scatter_dimension=0,
        tiled=True,
    )
    own_start = block * capacity
    own_scales = lax.dynamic_slice_in_dim(scales, own_start, capacity, 0)
    own_router = lax.dynamic_slice_in_dim(router_grad, own_start, capacity, 0)
    own_sel = x_slots.astype(jnp.float32)
    dotted = lax.psum(jnp.sum(gain[None, :] * d_normed * own_sel, axis=1), "narrow")
    grad_gain = lax.psum(jnp.sum(d_normed * own_sel * own_scales[:, None], axis=0), "wide")
    cubed = own_scales * own_scales * own_scales
    d_sel = (
        own_scales[:, None] * gain[None, :] * d_normed
        - own_sel * (cubed * dotted / D)[:, None]
        + own_router[:, None] * router_weight[None, :]
    )
    grad_x = (
        grad_out.astype(jnp.float32).at[local_rows].add(d_sel, mode="drop").astype(jnp.bfloat16)
    )
    return (grad_x, grad_gate, grad_up, grad_down, grad_gain, grad_router)


def solution(mesh):
    return jax.shard_map(
        local,
        mesh=mesh,
        in_specs=(
            P("wide", "narrow"),
            P("wide", "narrow"),
            P(),
            P("narrow"),
            P("narrow"),
            P("narrow", "wide"),
            P("narrow", "wide"),
            P("wide", "narrow"),
        ),
        out_specs=(
            P("wide", "narrow"),
            P("narrow", "wide"),
            P("narrow", "wide"),
            P("wide", "narrow"),
            P("narrow"),
            P("narrow"),
        ),
        check_vma=False,
    )
```

profile of v0, /device:TPU:22, one launch (start us, length us, event | category | flops | bytes accessed | tf_op | source)
XLA Modules:
  0.0 660.5 jit_solution(10905773531981987158)
XLA Ops:
  7.2 1.5 convert_reduce_fusion
  12.1 1.6 gather_fusion.1
  13.7 1.6 gather_fusion.2
  16.8 66.1 %all-gather.3.cloned.1.call-done = bf16[768,1024]{1,0:T(8,128)(2,1)} async-done(((bf16[24,1024]{1,0:T(8,128)(2,1)}), bf16[768,1024]{1,0:T(8,128)(2,1)}) %all-gather.3.cloned.1.call-update) | async-done | bytes 1572880 | tf_op jit(solution)/shard_map/all_gather | solution.py:35
  83.0 1.8 fusion
  84.8 18.7 %psum.56 = f32[768]{0:T(1024)S(1)} all-reduce(f32[768]{0:T(1024)S(1)} %fusion), channel_id=1, replica_groups=mesh['wide'=32,'narrow'=8] {'narrow'}, use_global_device_ids=true, to_apply=%region_3.5 | all-reduce | flops 768 | bytes 6144 | tf_op jit(solution)/shard_map/psum | solution.py:39
  103.5 5.1 fusion.29
  108.6 3.5 fusion.31
  112.1 37.4 %all-gather.5.cloned.1.call-done = bf16[768,1024]{1,0:T(8,128)(2,1)} async-done(((bf16[24,1024]{1,0:T(8,128)(2,1)}), bf16[768,1024]{1,0:T(8,128)(2,1)}) %all-gather.5.cloned.1.call-update) | async-done | bytes 1572880 | tf_op jit(solution)/shard_map/all_gather | solution.py:36
  149.4 5.6 fusion.33
  155.1 207.2 %all-reduce.3.cloned.1.call-done = (f32[768,1024]{1,0:T(8,128)}, f32[768,1024]{1,0:T(8,128)}, f32[768,1024]{1,0:T(8,128)}) async-done(((f32[768,1024]{1,0:T(8,128)}, f32[768,1024]{1,0:T(8,128)}, f32[768,1024]{1,0:T(8,128)}), (f32[768,1024]{1,0:T(8,128)}, f32[768,1024]{1,0:T(8,128)}, f32[768,1024]{1,0:T(8,128)})) %all-reduce.3.cloned.1.call-update) | async-done | bytes 9437200 | tf_op jit(solution)/shard_map/psum | solution.py:44
  362.2 5.9 multiply_reduce_fusion
  368.1 57.0 %psum.62 = f32[768]{0:T(1024)S(1)} all-reduce(f32[768]{0:T(1024)S(1)} %get-tuple-element.16), channel_id=1, replica_groups=mesh['wide'=32,'narrow'=8] {'wide'}, use_global_device_ids=true, to_apply=%region_13.15 | all-reduce | flops 768 | bytes 6144 | tf_op jit(solution)/shard_map/psum | solution.py:56
  425.2 2.8 fusion.4
  427.9 19.0 %psum.57 = f32[768]{0:T(1024)S(1)} all-reduce(f32[768]{0:T(1024)S(1)} %get-tuple-element.8), channel_id=1, replica_groups=mesh['wide'=32,'narrow'=8] {'narrow'}, use_global_device_ids=true, to_apply=%region_5.7 | all-reduce | flops 768 | bytes 6144 | tf_op jit(solution)/shard_map/psum | solution.py:39
  446.9 4.7 multiply_convert_fusion.2
  451.6 1.9 fusion.34
  454.3 3.5 convolution_add_fusion
  460.3 5.3 convolution_convert_fusion
  465.5 3.4 convolution_convert_fusion.1
  468.9 3.4 convolution_convert_fusion.2
  472.3 106.1 %reduce-scatter.2.cloned.1.call-done = f32[24,1024]{1,0:T(8,128)} async-done(((f32[768,1024]{1,0:T(8,128)}), f32[24,1024]{1,0:T(8,128)}) %reduce-scatter.2.cloned.1.call-update) | async-done | bytes 98320 | tf_op jit(solution)/shard_map/reduce_scatter | solution.py:72
  579.6 18.7 %psum.61 = f32[24]{0:T(128)S(1)} all-reduce(f32[24]{0:T(128)S(1)} %get-tuple-element.10), channel_id=1, replica_groups=mesh['wide'=32,'narrow'=8] {'narrow'}, use_global_device_ids=true, to_apply=%region_11.13 | all-reduce | flops 24 | bytes 192 | tf_op jit(solution)/shard_map/psum | solution.py:82
  600.4 53.6 %psum.63 = f32[1024]{0:T(1024)} all-reduce(f32[1024]{0:T(1024)S(1)} %get-tuple-element.9), channel_id=1, replica_groups=mesh['wide'=32,'narrow'=8] {'wide'}, use_global_device_ids=true, to_apply=%region_16.18 | all-reduce | flops 1024 | bytes 8192 | tf_op jit(solution)/shard_map/psum | solution.py:83
  (49 shorter events, 11.5 us)
Async XLA Ops:
  7.2 96.3 %copy-start = (bf16[1024,1024]{1,0:T(8,128)(2,1)S(1)}, bf16[1024,1024]{1,0:T(8,128)(2,1)}, u32[]{:S(2)}) copy-start(bf16[1024,1024]{1,0:T(8,128)(2,1)} %param.15) | copy-start | bytes 6291460
  7.2 96.3 %copy-start.10 = (f32[1024]{0:T(1024)S(1)}, f32[1024]{0:T(1024)}, u32[]{:S(2)}) copy-start(f32[1024]{0:T(1024)} %param.13) | copy-start | bytes 12292
  7.2 75.8 %all-gather.3.cloned.1.call-start = ((), (), s32[]{:S(2)}) async-start(), calls=%async_computation.1 | async-start | bytes 1622016 | tf_op jit(solution)/shard_map/all_gather | solution.py:35
  16.0 133.4 %all-gather.5.cloned.1.call-start = ((), (), s32[]{:S(2)}) async-start(), calls=%async_computation.2 | async-start | bytes 1622016 | tf_op jit(solution)/shard_map/all_gather | solution.py:36
  16.8 345.5 %all-reduce.3.cloned.1.call-start = ((), (), s32[]{:S(2)}) async-start(), calls=%async_computation.4 | async-start | bytes 18874368 | tf_op jit(solution)/shard_map/psum | solution.py:44
  103.5 5.1 copy-start.1
  103.5 5.1 copy-start.11
  155.0 423.4 %reduce-scatter.2.cloned.1.call-start = ((), (), s32[]{:S(2)}) async-start(), calls=%async_computation.3 | async-start | bytes 3244032 | tf_op jit(solution)/shard_map/reduce_scatter | solution.py:72
  362.2 62.9 %copy-start.9 = (f32[1024]{0:T(1024)S(1)}, f32[1024]{0:T(1024)}, u32[]{:S(2)}) copy-start(f32[1024]{0:T(1024)} %param.14) | copy-start | bytes 12292
  451.6 1.9 copy-start.4
  451.6 1.9 copy-start.6
  451.6 2.7 copy-start.12
  457.8 0.9 copy-start.3
  460.3 5.3 copy-start.2
  460.3 5.3 copy-start.7
  465.5 3.4 copy-start.5
  468.9 109.5 %copy-start.8 = (bf16[24,1024]{1,0:T(8,128)(2,1)S(1)}, bf16[24,1024]{1,0:T(8,128)(2,1)}, u32[]{:S(2)}) copy-start(bf16[24,1024]{1,0:T(8,128)(2,1)} %get-tuple-element.23) | copy-start | bytes 147460
Sparse Core Ops, SparseCore 0:
  16.2 66.7 all-gather.2
  85.4 63.9 all-gather.4
  155.2 207.0 all-reduce.2
  458.0 120.4 reduce-scatter.1
where the time goes:
time: 668 us; the launch traced here: 661 us
  waiting for transfers between devices  418 us (63%)
  blocking collectives  167 us (25%)
  matrix products  31.5 us (5%)
  other arithmetic  23.8 us (4%)
  between operations  14 us (2%)
    psum x1, waiting for transfers between devices, local(): lax.psum((jnp.dot(normed, w_gate, preferred_element_type=jnp.float32), jn...  207 us
    reduce_scatter x1, waiting for transfers between devices, local(): lax.psum_scatter(first + jnp.einsum('rf,df->rd', d_up, w_up, preferred_el...  106 us
    all_gather x1, waiting for transfers between devices, local(): lax.all_gather(x_slots, 'wide', axis=0, tiled=True)  66.1 us
    psum x1, blocking collectives, local(): lax.psum(jnp.sum(hidden.astype(jnp.float32) * back, axis=1), 'wide')  57 us
    psum x1, blocking collectives, local(): lax.psum(jnp.sum(d_normed * own_sel * own_scales[:, None], axis=0), 'wide')  53.6 us
    psum x2, blocking collectives, local(): lax.psum((jnp.sum(sel32 * sel32, axis=1), jnp.sum(sel32 * router_weight[N...  37.7 us
    all_gather x1, waiting for transfers between devices, local(): lax.all_gather(g_slots, 'wide', axis=0, tiled=True)  37.4 us
    psum x1, blocking collectives, local(): lax.psum(jnp.sum(gain[None, :] * d_normed * own_sel, axis=1), 'narrow')  18.7 us
  transfers between devices with their start and end apart: 4, of which 4 were waited for; matrix products, arithmetic and copies ran while one was open for 4% of the time, Pallas kernels for 0%

commit v1 on v0

v1 whole, which is shorter than its diff:
```python
import jax
import jax.numpy as jnp
from jax import lax
from jax.sharding import PartitionSpec as P

D = 8192
EPS = 1e-06
bf16 = jnp.bfloat16
f32 = jnp.float32
DOWN, UP = 2.0**-20, 2.0**20

WIDE = [(z, y, c) for z in range(8) for y in range(2) for c in range(2)]


def wide_pairs(move):
    def index(z, y, c):
        return (z % 8 * 2 + y) * 2 + c

    return [(index(*t), index(*move(*t))) for t in WIDE]


CORE = wide_pairs(lambda z, y, c: (z, y, 1 - c))
YLO = wide_pairs(lambda z, y, c: (z, 1 - y, c))
ZUP = wide_pairs(lambda z, y, c: (z + 1, y, c))
ZDOWN = wide_pairs(lambda z, y, c: (z + 7, y, c))
ZGROUPS = [[(z * 2 + y) * 2 + c for z in range(8)] for y in range(2) for c in range(2)]


def pieces(value, count):
    out = []
    for _ in range(count):
        head = lax.reduce_precision(value, 8, 7)
        out.append(head.astype(bf16))
        value = jnp.where(jnp.abs(head) < jnp.inf, value - head, 0.0)
    return out


def matmul(a, b, dims, out=f32):
    return lax.dot_general(a, b, (dims, ((), ())), preferred_element_type=out)


def local(tokens, grad_out, selected, gain, router_weight, w_gate, w_up, w_down):
    tok = tokens.shape[0]
    cap = tok // 4
    rows = selected.shape[0]
    w = lax.axis_index("wide")
    z, y, c = w // 4, (w // 2) % 2, w % 2

    def before(ids):
        return jnp.sum((selected[:, None] < ids[None, :]).astype(jnp.int32), axis=0)

    def slot_places(blocks):
        start, end = before(blocks * tok), before((blocks + 1) * tok)
        place = start[:, None] + jnp.arange(cap, dtype=jnp.int32)[None, :]
        return jnp.where(place < end[:, None], place, rows).reshape(-1)

    def onehot(places):
        return (places[:, None] == jnp.arange(rows, dtype=jnp.int32)[None, :]).astype(bf16)

    ids = w * tok + jnp.arange(tok, dtype=jnp.int32)
    first = before(w[None] * tok)
    rank = before(ids) - first
    marked = jnp.sum((selected[:, None] == ids[None, :]).astype(jnp.int32), axis=0) > 0
    pick = (
        (jnp.arange(cap, dtype=jnp.int32)[:, None] == rank[None, :]) & marked[None, :]
    ).astype(bf16)
    mine = jnp.concatenate(
        [
            matmul(pick, tokens, ((1,), (0,)), bf16),
            matmul(pick, grad_out, ((1,), (0,)), bf16),
        ],
        axis=0,
    )[None]

    base = jnp.concatenate([mine, lax.ppermute(mine, "wide", YLO)], axis=0)
    up = [base]
    down = [base]
    for _ in range(3):
        up.append(lax.ppermute(up[-1], "wide", ZUP))
        down.append(lax.ppermute(down[-1], "wide", ZDOWN))
    far_a = lax.ppermute(up[3][:1], "wide", ZUP)
    far_b = lax.ppermute(down[3][1:], "wide", ZDOWN)
    parts = [base] + up[1:] + down[1:] + [far_a, far_b]
    half = jnp.concatenate(parts, axis=0)
    other = lax.ppermute(half, "wide", CORE)
    steps = jnp.array([0, -1, -2, -3, 1, 2, 3, 4], jnp.int32)
    zs = (z + steps + 8) % 8
    chips = ((zs * 2)[:, None] + jnp.stack([y, 1 - y])[None, :]).reshape(-1) * 2
    put = onehot(slot_places(jnp.concatenate([chips + c, chips + 1 - c])))
    slots = jnp.concatenate([half, other], axis=0).reshape(32, 2, cap, -1)
    sel = matmul(put, slots[:, 0].reshape(32 * cap, -1), ((0,), (0,)), bf16)
    gsel = matmul(put, slots[:, 1].reshape(32 * cap, -1), ((0,), (0,)), bf16)

    sel32 = sel.astype(f32)
    squares = jnp.sum(sel32 * sel32, axis=1, keepdims=True)
    logit = jnp.sum(sel32 * router_weight[None, :], axis=1, keepdims=True)
    scaled = (sel32 * (gain * DOWN)[None, :]).astype(bf16)
    extra = jnp.concatenate(
        pieces(squares, 3) + pieces(logit, 3) + [jnp.zeros((rows, 122), bf16)], axis=1
    )
    send = jnp.concatenate(
        [
            matmul(scaled, w_gate, ((1,), (0,))).astype(bf16),
            matmul(scaled, w_up, ((1,), (0,))).astype(bf16),
            matmul(gsel, w_down, ((1,), (1,))).astype(bf16),
            extra,
        ],
        axis=1,
    ).reshape(8, rows // 8, -1)
    got = lax.all_to_all(send, "narrow", 0, 0, tiled=True)
    total = jnp.sum(got.astype(f32), axis=0)
    ff = w_gate.shape[1]
    tail = total[:, 3 * ff :]
    squares = jnp.sum(tail[:, 0:3], axis=1, keepdims=True)
    logit = jnp.sum(tail[:, 3:6], axis=1, keepdims=True)
    scale = lax.rsqrt(squares / D + EPS)
    gate = total[:, :ff] * (scale * UP)
    upv = total[:, ff : 2 * ff] * (scale * UP)
    back = total[:, 2 * ff : 3 * ff]
    sigma = jax.nn.sigmoid(gate)
    hidden = (gate * sigma * upv).astype(bf16)
    d_hidden = logit * back
    d_gate = (d_hidden * upv * (sigma + gate * sigma * (1.0 - sigma))).astype(bf16)
    d_up = (d_hidden * gate * sigma).astype(bf16)
    router_grad = jnp.sum(hidden.astype(f32) * back, axis=1, keepdims=True)
    inner = jnp.sum(d_gate.astype(f32) * gate + d_up.astype(f32) * upv, axis=1, keepdims=True)
    extra = jnp.concatenate(
        pieces(scale, 3)
        + pieces(logit, 3)
        + pieces(router_grad, 3)
        + pieces(inner, 3)
        + [jnp.zeros((rows // 8, 116), bf16)],
        axis=1,
    )
    share = jnp.concatenate([hidden, d_gate, d_up, extra], axis=1)
    gathered = lax.all_to_all(
        jnp.broadcast_to(share[None], (8,) + share.shape), "narrow", 0, 0, tiled=True
    ).reshape(rows, -1)
    hidden, d_gate, d_up = (gathered[:, k * ff : (k + 1) * ff] for k in range(3))
    tail = gathered[:, 3 * ff : 3 * ff + 12].astype(f32)
    scale, logit, router_grad, inner = (
        jnp.sum(tail[:, 3 * k : 3 * k + 3], axis=1, keepdims=True) for k in range(4)
    )

    d_normed = matmul(d_gate, w_gate, ((1,), (1,))) + matmul(d_up, w_up, ((1,), (1,)))
    small = jnp.concatenate(
        [
            jnp.sum(d_normed * sel32 * scale, axis=0, keepdims=True),
            jnp.sum(sel32 * router_grad, axis=0, keepdims=True),
            jnp.concatenate(
                [router_grad[:, 0], inner[:, 0], jnp.zeros((tokens.shape[1] - 2 * rows,), f32)]
            )[None],
        ],
        axis=0,
    )
    rounded = d_normed.astype(bf16)
    zy = jnp.arange(8, dtype=jnp.int32) * 2
    order = (jnp.stack([y, 1 - y])[:, None] + zy[None, :]).reshape(-1) * 2
    theirs = matmul(onehot(slot_places(order + 1 - c)), rounded, ((1,), (0,)), bf16)
    ours = matmul(onehot(slot_places(order + c)), rounded, ((1,), (0,)), bf16)
    part = ours.astype(f32) + lax.ppermute(theirs, "wide", CORE).astype(f32)
    small = small + lax.ppermute(small, "wide", CORE)
    part = part.reshape(2, 8, cap, -1)
    part = part[0] + lax.ppermute(part[1].astype(bf16), "wide", YLO).astype(f32)
    small = small + lax.ppermute(small, "wide", YLO)
    packed = jnp.concatenate(pieces(small, 2) + [jnp.zeros((2, small.shape[1]), bf16)], axis=0)
    message = jnp.concatenate(
        [part.astype(bf16), jnp.broadcast_to(packed[None], (8,) + packed.shape)], axis=1
    )
    message = lax.all_to_all(
        message, "wide", 0, 0, tiled=True, axis_index_groups=ZGROUPS
    )
    message = jnp.sum(message.astype(f32), axis=0)
    own = message[:cap]
    small = message[cap : cap + 3] + message[cap + 3 : cap + 6]

    normed = (sel32 * scale * gain[None, :]).astype(bf16)
    d_out = (logit * gsel.astype(f32)).astype(bf16)
    grad_down = matmul(hidden, d_out, ((0,), (0,))).astype(bf16)
    grad_gate = matmul(normed, d_gate, ((0,), (0,))).astype(bf16)
    grad_up = matmul(normed, d_up, ((0,), (0,))).astype(bf16)

    where = onehot(slot_places(w[None])).astype(f32)
    own_scale = jnp.sum(where * scale[:, 0][None, :], axis=1, keepdims=True)
    own_router = jnp.sum(where * small[2, :rows][None, :], axis=1, keepdims=True)
    own_inner = jnp.sum(where * small[2, rows : 2 * rows][None, :], axis=1, keepdims=True)
    own_sel = mine[0, :cap].astype(f32)
    d_sel = (
        own_scale * gain[None, :] * own
        - own_sel * (own_scale * own_scale * own_inner / D)
        + own_router * router_weight[None, :]
    )
    spread = lax.dot_general(
        pick.astype(f32), d_sel, (((0,), (0,)), ((), ())), precision=lax.Precision.HIGHEST
    )
    grad_x = (grad_out.astype(f32) + spread).astype(bf16)
    return (grad_x, grad_gate, grad_up, grad_down, small[0], small[1])


def solution(mesh):
    return jax.shard_map(
        local,
        mesh=mesh,
        in_specs=(
            P("wide", "narrow"),
            P("wide", "narrow"),
            P(),
            P("narrow"),
            P("narrow"),
            P("narrow", "wide"),
            P("narrow", "wide"),
            P("wide", "narrow"),
        ),
        out_specs=(
            P("wide", "narrow"),
            P("narrow", "wide"),
            P("narrow", "wide"),
            P("wide", "narrow"),
            P("narrow"),
            P("narrow"),
        ),
        check_vma=False,
    )
```

time: 668 us -> 195 us (0.29)
  waiting for transfers between devices: 418 us -> 67.1 us
  blocking collectives: 167 us -> 35.6 us
  starting transfers between devices: 0.16 us -> 34 us
  other arithmetic: 23.8 us -> 8.88 us
  between operations: 14 us -> 1.26 us
  local copies, waits for them, and re-layouts: 6.52 us -> 14.4 us
    psum x1 -> x0, waiting for transfers between devices: 207 us -> none  [local(): lax.psum((jnp.dot(normed, w_gate, preferred_element_type=jnp.float32), jn...]
    psum x5 -> x0, blocking collectives: 167 us -> none  [the longest x1 57 us: local(): lax.psum(jnp.sum(hidden.astype(jnp.float32) * back, axis=1), 'wide')]
    reduce_scatter x1 -> x0, waiting for transfers between devices: 106 us -> none  [local(): lax.psum_scatter(first + jnp.einsum('rf,df->rd', d_up, w_up, preferred_el...]
    all_gather x2 -> x0, waiting for transfers between devices: 104 us -> none  [the longest x1 66.1 us: local(): lax.all_gather(x_slots, 'wide', axis=0, tiled=True)]
    all_to_all x0 -> x2, waiting for transfers between devices: none -> 36.4 us  [the longest x1 31.4 us: local(): lax.all_to_all(jnp.broadcast_to(share[None], (8,) + share.shape), 'narrow...]
    all_to_all x0 -> x1, blocking collectives: none -> 35.6 us  [local(): got = lax.all_to_all(send, 'narrow', 0, 0, tiled=True)]
    ppermute x0 -> x14, waiting for transfers between devices: none -> 30.7 us  [the longest x3 10.1 us: local(): down.append(lax.ppermute(down[-1], 'wide', ZDOWN))]
    ppermute x0 -> x14, starting transfers between devices: none -> 21.9 us  [the longest x3 13.3 us: local(): down.append(lax.ppermute(down[-1], 'wide', ZDOWN))]
  transfers between devices with their start and end apart: 4 -> 16, of which waited for: 4 -> 12; matrix products, arithmetic and copies ran while one was open for 4% -> 9% of each run, Pallas kernels for 0% -> 0%
where the time goes in v1:
time: 195 us; the launch traced here: 194 us
  waiting for transfers between devices  67.1 us (34%)
  blocking collectives  35.6 us (18%)
  starting transfers between devices  34 us (17%)
  matrix products  33 us (17%)
  local copies, waits for them, and re-layouts  14.4 us (7%)
  other arithmetic  8.88 us (5%)
    all_to_all x1, blocking collectives, local(): got = lax.all_to_all(send, 'narrow', 0, 0, tiled=True)  35.6 us
    dot_general x14, matrix products, matmul(): return lax.dot_general(a, b, (dims, ((), ())), preferred_element_type=out)  31.9 us
    all_to_all x1, waiting for transfers between devices, local(): lax.all_to_all(jnp.broadcast_to(share[None], (8,) + share.shape), 'narrow...  31.4 us
    ppermute x3, starting transfers between devices, local(): down.append(lax.ppermute(down[-1], 'wide', ZDOWN))  13.3 us
    ppermute x3, waiting for transfers between devices, local(): down.append(lax.ppermute(down[-1], 'wide', ZDOWN))  10.1 us
    ppermute x1, waiting for transfers between devices, local(): part = part[0] + lax.ppermute(part[1].astype(bf16), 'wide', YLO).astype(f32)  9.02 us
    all_to_all x1, starting transfers between devices, local(): lax.all_to_all(jnp.broadcast_to(share[None], (8,) + share.shape), 'narrow...  8.63 us
    ppermute x1, waiting for transfers between devices, local(): far_a = lax.ppermute(up[3][:1], 'wide', ZUP)  5.72 us
  transfers between devices with their start and end apart: 16, of which 12 were waited for; matrix products, arithmetic and copies ran while one was open for 9% of the time, Pallas kernels for 0%

profile of v1, /device:TPU:22, one launch (start us, length us, event | category | flops | bytes accessed | tf_op | source)
XLA Modules:
  0.0 194.2 jit_solution(16532922595471583505)
XLA Ops:
  10.6 5.9 %collective-permute-start.4 = (bf16[2,48,1024]{2,1,0:T(8,128)(2,1)S(1)}, bf16[2,48,1024]{2,1,0:T(8,128)(2,1)S(1)}, u32[]{:S(2)}, u32[]{:S(2)}) collective-permute-start(bf16[2,48,1024]{2,1,0:T(8,128)(2,1)S(1)} %pad_maximum_fusion.1), channel_id=1, source_target_pairs={{0,224},{8,232},{16,240},{24,248},{32,0},{40,8},{48,16},{56,24},{6... | collective-permute-start | bytes 589832 | tf_op jit(solution)/shard_map/ppermute | solution.py:80
  16.7 3.0 %collective-permute-done.4 = bf16[2,48,1024]{2,1,0:T(8,128)(2,1)S(1)} collective-permute-done((bf16[2,48,1024]{2,1,0:T(8,128)(2,1)S(1)}, bf16[2,48,1024]{2,1,0:T(8,128)(2,1)S(1)}, u32[]{:S(2)}, u32[]{:S(2)}) %collective-permute-start.4) | collective-permute-done | bytes 196640 | tf_op jit(solution)/shard_map/ppermute | solution.py:80
  19.7 3.7 %collective-permute-start.5 = (bf16[2,48,1024]{2,1,0:T(8,128)(2,1)S(1)}, bf16[2,48,1024]{2,1,0:T(8,128)(2,1)S(1)}, u32[]{:S(2)}, u32[]{:S(2)}) collective-permute-start(bf16[2,48,1024]{2,1,0:T(8,128)(2,1)S(1)} %collective-permute-done.4), channel_id=1, source_target_pairs={{0,224},{8,232},{16,240},{24,248},{32,0},{40,8},{48,16},{56,24},{6... | collective-permute-start | bytes 589832 | tf_op jit(solution)/shard_map/ppermute | solution.py:80
  23.4 3.2 %collective-permute-done.5 = bf16[2,48,1024]{2,1,0:T(8,128)(2,1)S(1)} collective-permute-done((bf16[2,48,1024]{2,1,0:T(8,128)(2,1)S(1)}, bf16[2,48,1024]{2,1,0:T(8,128)(2,1)S(1)}, u32[]{:S(2)}, u32[]{:S(2)}) %collective-permute-start.5) | collective-permute-done | bytes 196640 | tf_op jit(solution)/shard_map/ppermute | solution.py:80
  26.6 3.7 %collective-permute-start.6 = (bf16[2,48,1024]{2,1,0:T(8,128)(2,1)S(1)}, bf16[2,48,1024]{2,1,0:T(8,128)(2,1)S(1)}, u32[]{:S(2)}, u32[]{:S(2)}) collective-permute-start(bf16[2,48,1024]{2,1,0:T(8,128)(2,1)S(1)} %collective-permute-done.5), channel_id=1, source_target_pairs={{0,224},{8,232},{16,240},{24,248},{32,0},{40,8},{48,16},{56,24},{6... | collective-permute-start | bytes 589832 | tf_op jit(solution)/shard_map/ppermute | solution.py:80
  30.4 3.9 %collective-permute-done.6 = bf16[2,48,1024]{2,1,0:T(8,128)(2,1)S(1)} collective-permute-done((bf16[2,48,1024]{2,1,0:T(8,128)(2,1)S(1)}, bf16[2,48,1024]{2,1,0:T(8,128)(2,1)S(1)}, u32[]{:S(2)}, u32[]{:S(2)}) %collective-permute-start.6) | collective-permute-done | bytes 196640 | tf_op jit(solution)/shard_map/ppermute | solution.py:80
  34.3 3.8 %collective-permute-start.8 = (bf16[1,48,1024]{2,1,0:T(8,128)(2,1)S(1)}, bf16[1,48,1024]{2,1,0:T(8,128)(2,1)S(1)}, u32[]{:S(2)}, u32[]{:S(2)}) collective-permute-start(bf16[1,48,1024]{2,1,0:T(8,128)(2,1)S(1)} %slice.115), channel_id=1, source_target_pairs={{0,224},{8,232},{16,240},{24,248},{32,0},{40,8},{48,16},{56,24},{6... | collective-permute-start | bytes 294920 | tf_op jit(solution)/shard_map/ppermute | solution.py:82
  38.4 5.7 %collective-permute-done.7 = bf16[1,48,1024]{2,1,0:T(8,128)(2,1)S(1)} collective-permute-done((bf16[1,48,1024]{2,1,0:T(8,128)(2,1)S(1)}, bf16[1,48,1024]{2,1,0:T(8,128)(2,1)S(1)}, u32[]{:S(2)}, u32[]{:S(2)}) %collective-permute-start.7) | collective-permute-done | bytes 98336 | tf_op jit(solution)/shard_map/ppermute | solution.py:81
  44.7 3.2 %collective-permute-done.9 = bf16[16,48,1024]{2,1,0:T(8,128)(2,1)S(1)} collective-permute-done((bf16[16,48,1024]{2,1,0:T(8,128)(2,1)S(1)}, bf16[16,48,1024]{2,1,0:T(8,128)(2,1)S(1)}, u32[]{:S(2)}, u32[]{:S(2)}) %collective-permute-start.9) | collective-permute-done | bytes 1572896 | tf_op jit(solution)/shard_map/ppermute | solution.py:85
  53.7 2.3 %convolution_convert_fusion.4 = bf16[384,1024]{1,0:T(8,128)(2,1)S(1)} fusion(bf16[1024,1024]{1,0:T(8,128)(2,1)S(1)} %copy-done, bf16[384,1024]{1,0:T(8,128)(2,1)} %get-tuple-element.70, f32[1024]{0:T(1024)S(1)} %broadcast_multiply_fusion), kind=kOutput, calls=%fused_computation.22 | convolution fusion | flops 806879232 | bytes 3674112 | tf_op jit(solution)/shard_map/dot_general | solution.py:39
  56.1 1.9 convolution_convert_fusion.5
  57.9 1.9 convolution_convert_fusion.3
  60.5 5.1 %concatenate.92 = bf16[8,48,3200]{2,1,0:T(8,128)(2,1)} concatenate(bf16[8,48,1024]{2,1,0:T(8,128)(2,1)} %bitcast.111, bf16[8,48,1024]{2,1,0:T(8,128)(2,1)S(1)} %bitcast.110, bf16[8,48,1024]{2,1,0:T(8,128)(2,1)} %bitcast.112, bf16[8,48,1]{2,1,0:T(8,128)(2,1)S(1)} %copy.90, bf16[8,48,1]{2,1,0:T(8,128)(2,1)S(1)} %copy.91, bf16[8,48,1]{2,1,0:T(8,128)(2,1)S(1)} %copy.92, ...), dimensions={2} | concatenate | bytes 4915200 | tf_op jit(solution)/shard_map/concatenate | solution.py:101
  65.6 35.6 %all_to_all.15 = bf16[8,48,3200]{2,1,0:T(8,128)(2,1)S(1)} all-to-all(bf16[8,48,3200]{2,1,0:T(8,128)(2,1)} %concatenate.92), channel_id=1, replica_groups=mesh['wide'=32,'narrow'=8] {'narrow'}, dimensions={0} | all-to-all | bytes 4915200 | tf_op jit(solution)/shard_map/all_to_all | solution.py:110
  105.1 8.6 %all-to-all-start.1 = ((bf16[8,48,3200]{2,1,0:T(8,128)(2,1)}), bf16[8,48,3200]{2,1,0:T(8,128)(2,1)}, u32[]{:S(2)}, u32[]{:S(2)}) async-start(bf16[8,48,3200]{2,1,0:T(8,128)(2,1)} %broadcast_in_dim.60), calls=%async_computation.1 | async-start | bytes 4915200 | tf_op jit(solution)/shard_map/all_to_all | solution.py:136
  115.0 31.4 %all-to-all-done.1 = bf16[8,48,3200]{2,1,0:T(8,128)(2,1)} async-done(((bf16[8,48,3200]{2,1,0:T(8,128)(2,1)}), bf16[8,48,3200]{2,1,0:T(8,128)(2,1)}, u32[]{:S(2)}, u32[]{:S(2)}) %all-to-all-start.1) | async-done | bytes 2457632 | tf_op jit(solution)/shard_map/all_to_all | solution.py:136
  147.3 4.0 %fusion.16 = f32[384,1024]{1,0:T(8,128)} fusion(bf16[1024,1024]{1,0:T(8,128)(2,1)} %param.14, bf16[384,3200]{1,0:T(8,128)(2,1)} %bitcast.23), kind=kOutput, calls=%fused_computation.37 | convolution fusion | flops 805306368 | bytes 4456448 | tf_op jit(solution)/shard_map/dot_general | solution.py:39
  151.5 3.1 %fusion.4 = (f32[1024]{0:T(1024)S(1)}, f32[1024]{0:T(1024)S(1)}, bf16[384,1024]{1,0:T(8,128)(2,1)S(1)}) fusion(bf16[384,1024]{1,0:T(8,128)(2,1)} %get-tuple-element.70, f32[384]{0:T(512)S(1)} %get-tuple-element.17, f32[384]{0:T(512)S(1)} %get-tuple-element.16, f32[384,1024]{1,0:T(8,128)} %fusion.16, bf16[1024,1024]{1,0:T(8,128)(2,1)S(1)} %copy-done, ...), kind=kOutput, calls=%fused_computation.14 | convolution fusion | flops 808450048 | bytes 6040576 | tf_op jit(solution)/shard_map/dot_general | solution.py:39
  161.8 9.0 %collective-permute-done.11 = bf16[8,24,1024]{2,1,0:T(8,128)(2,1)S(1)} collective-permute-done((bf16[8,24,1024]{2,1,0:T(8,128)(2,1)S(1)}, bf16[8,24,1024]{2,1,0:T(8,128)(2,1)S(1)}, u32[]{:S(2)}, u32[]{:S(2)}) %collective-permute-start.11) | collective-permute-done | bytes 393248 | tf_op jit(solution)/shard_map/ppermute | solution.py:164
  171.8 3.5 %all-to-all-start.2 = ((bf16[8,32,1024]{2,1,0:T(8,128)(2,1)}), bf16[8,32,1024]{2,1,0:T(8,128)(2,1)S(1)}, u32[]{:S(2)}, u32[]{:S(2)}) async-start(bf16[8,32,1024]{2,1,0:T(8,128)(2,1)} %pad_maximum_fusion), calls=%async_computation.2 | async-start | bytes 1048576 | tf_op jit(solution)/shard_map/all_to_all | solution.py:170
  175.3 4.1 %convolution_convert_fusion = bf16[1024,1024]{1,0:T(8,128)(2,1)} fusion(bf16[384,1024]{1,0:T(8,128)(2,1)} %fusion.8, bf16[384,3200]{1,0:T(8,128)(2,1)} %bitcast.23, f32[384]{0:T(512)S(1)} %get-tuple-element.14), kind=kOutput, calls=%fused_computation.7 | convolution fusion | flops 807534592 | bytes 3671552 | tf_op jit(solution)/shard_map/dot_general | solution.py:39
  179.4 3.8 %convolution_convert_fusion.1 = bf16[1024,1024]{1,0:T(8,128)(2,1)} fusion(bf16[384,3200]{1,0:T(8,128)(2,1)} %bitcast.23, bf16[384,1024]{1,0:T(8,128)(2,1)S(1)} %copy-done.9, f32[1024]{0:T(1024)S(1)} %copy-done.3, f32[384]{0:T(512)S(1)} %get-tuple-element.17), kind=kOutput, calls=%fused_computation.8 | convolution fusion | flops 807927808 | bytes 3675648 | tf_op jit(solution)/shard_map/dot_general | solution.py:39
  183.3 3.9 %convolution_convert_fusion.2 = bf16[1024,1024]{1,0:T(8,128)(2,1)} fusion(bf16[384,3200]{1,0:T(8,128)(2,1)} %bitcast.23, bf16[384,1024]{1,0:T(8,128)(2,1)S(1)} %copy-done.9, f32[1024]{0:T(1024)S(1)} %copy-done.3, f32[384]{0:T(512)S(1)} %get-tuple-element.17), kind=kOutput, calls=%fused_computation.9 | convolution fusion | flops 807927808 | bytes 3675648 | tf_op jit(solution)/shard_map/dot_general | solution.py:39
  187.1 5.0 %all-to-all-done.2 = bf16[8,32,1024]{2,1,0:T(8,128)(2,1)S(1)} async-done(((bf16[8,32,1024]{2,1,0:T(8,128)(2,1)}), bf16[8,32,1024]{2,1,0:T(8,128)(2,1)S(1)}, u32[]{:S(2)}, u32[]{:S(2)}) %all-to-all-start.2) | async-done | bytes 524320 | tf_op jit(solution)/shard_map/all_to_all | solution.py:170
  (161 shorter events, 33.6 us)
Async XLA Ops:
  0.6 53.1 %copy-start = (bf16[1024,1024]{1,0:T(8,128)(2,1)S(1)}, bf16[1024,1024]{1,0:T(8,128)(2,1)}, u32[]{:S(2)}) copy-start(bf16[1024,1024]{1,0:T(8,128)(2,1)} %param.15) | copy-start | bytes 6291460
  5.9 4.7 %collective-permute-start = (bf16[1,48,1024]{2,1,0:T(8,128)(2,1)S(1)}, bf16[1,48,1024]{2,1,0:T(8,128)(2,1)S(1)}, u32[]{:S(2)}, u32[]{:S(2)}) collective-permute-start(bf16[1,48,1024]{2,1,0:T(8,128)(2,1)S(1)} %get-tuple-element.38), channel_id=1, source_target_pairs={{0,16},{8,24},{16,0},{24,8},{32,48},{40,56},{48,32},{56,40},{64,80... | collective-permute-start | bytes 294920 | tf_op jit(solution)/shard_map/ppermute | solution.py:75
  10.6 9.1 %collective-permute-start.4 = (bf16[2,48,1024]{2,1,0:T(8,128)(2,1)S(1)}, bf16[2,48,1024]{2,1,0:T(8,128)(2,1)S(1)}, u32[]{:S(2)}, u32[]{:S(2)}) collective-permute-start(bf16[2,48,1024]{2,1,0:T(8,128)(2,1)S(1)} %pad_maximum_fusion.1), channel_id=1, source_target_pairs={{0,224},{8,232},{16,240},{24,248},{32,0},{40,8},{48,16},{56,24},{6... | collective-permute-start | bytes 589832 | tf_op jit(solution)/shard_map/ppermute | solution.py:80
  16.5 6.9 %collective-permute-start.1 = (bf16[2,48,1024]{2,1,0:T(8,128)(2,1)S(1)}, bf16[2,48,1024]{2,1,0:T(8,128)(2,1)S(1)}, u32[]{:S(2)}, u32[]{:S(2)}) collective-permute-start(bf16[2,48,1024]{2,1,0:T(8,128)(2,1)S(1)} %pad_maximum_fusion.1), channel_id=1, source_target_pairs={{0,32},{8,40},{16,48},{24,56},{32,64},{40,72},{48,80},{56,88},{64,... | collective-permute-start | bytes 589832 | tf_op jit(solution)/shard_map/ppermute | solution.py:79
  19.7 6.9 %collective-permute-start.5 = (bf16[2,48,1024]{2,1,0:T(8,128)(2,1)S(1)}, bf16[2,48,1024]{2,1,0:T(8,128)(2,1)S(1)}, u32[]{:S(2)}, u32[]{:S(2)}) collective-permute-start(bf16[2,48,1024]{2,1,0:T(8,128)(2,1)S(1)} %collective-permute-done.4), channel_id=1, source_target_pairs={{0,224},{8,232},{16,240},{24,248},{32,0},{40,8},{48,16},{56,24},{6... | collective-permute-start | bytes 589832 | tf_op jit(solution)/shard_map/ppermute | solution.py:80
  23.4 6.9 %collective-permute-start.2 = (bf16[2,48,1024]{2,1,0:T(8,128)(2,1)S(1)}, bf16[2,48,1024]{2,1,0:T(8,128)(2,1)S(1)}, u32[]{:S(2)}, u32[]{:S(2)}) collective-permute-start(bf16[2,48,1024]{2,1,0:T(8,128)(2,1)S(1)} %collective-permute-done.1), channel_id=1, source_target_pairs={{0,32},{8,40},{16,48},{24,56},{32,64},{40,72},{48,80},{56,88},{64,... | collective-permute-start | bytes 589832 | tf_op jit(solution)/shard_map/ppermute | solution.py:79
  26.6 7.7 %collective-permute-start.6 = (bf16[2,48,1024]{2,1,0:T(8,128)(2,1)S(1)}, bf16[2,48,1024]{2,1,0:T(8,128)(2,1)S(1)}, u32[]{:S(2)}, u32[]{:S(2)}) collective-permute-start(bf16[2,48,1024]{2,1,0:T(8,128)(2,1)S(1)} %collective-permute-done.5), channel_id=1, source_target_pairs={{0,224},{8,232},{16,240},{24,248},{32,0},{40,8},{48,16},{56,24},{6... | collective-permute-start | bytes 589832 | tf_op jit(solution)/shard_map/ppermute | solution.py:80
  30.3 7.9 %collective-permute-start.3 = (bf16[2,48,1024]{2,1,0:T(8,128)(2,1)S(1)}, bf16[2,48,1024]{2,1,0:T(8,128)(2,1)S(1)}, u32[]{:S(2)}, u32[]{:S(2)}) collective-permute-start(bf16[2,48,1024]{2,1,0:T(8,128)(2,1)S(1)} %collective-permute-done.2), channel_id=1, source_target_pairs={{0,32},{8,40},{16,48},{24,56},{32,64},{40,72},{48,80},{56,88},{64,... | collective-permute-start | bytes 589832 | tf_op jit(solution)/shard_map/ppermute | solution.py:79
  30.3 14.2 %copy-start.3 = (f32[1024]{0:T(1024)S(1)}, f32[1024]{0:T(1024)}, u32[]{:S(2)}) copy-start(f32[1024]{0:T(1024)} %param.12) | copy-start | bytes 12292
  34.3 9.9 %collective-permute-start.8 = (bf16[1,48,1024]{2,1,0:T(8,128)(2,1)S(1)}, bf16[1,48,1024]{2,1,0:T(8,128)(2,1)S(1)}, u32[]{:S(2)}, u32[]{:S(2)}) collective-permute-start(bf16[1,48,1024]{2,1,0:T(8,128)(2,1)S(1)} %slice.115), channel_id=1, source_target_pairs={{0,224},{8,232},{16,240},{24,248},{32,0},{40,8},{48,16},{56,24},{6... | collective-permute-start | bytes 294920 | tf_op jit(solution)/shard_map/ppermute | solution.py:82
  38.3 5.9 %collective-permute-start.7 = (bf16[1,48,1024]{2,1,0:T(8,128)(2,1)S(1)}, bf16[1,48,1024]{2,1,0:T(8,128)(2,1)S(1)}, u32[]{:S(2)}, u32[]{:S(2)}) collective-permute-start(bf16[1,48,1024]{2,1,0:T(8,128)(2,1)S(1)} %slice.114), channel_id=1, source_target_pairs={{0,32},{8,40},{16,48},{24,56},{32,64},{40,72},{48,80},{56,88},{64,... | collective-permute-start | bytes 294920 | tf_op jit(solution)/shard_map/ppermute | solution.py:81
  44.2 3.7 %collective-permute-start.9 = (bf16[16,48,1024]{2,1,0:T(8,128)(2,1)S(1)}, bf16[16,48,1024]{2,1,0:T(8,128)(2,1)S(1)}, u32[]{:S(2)}, u32[]{:S(2)}) collective-permute-start(bf16[16,48,1024]{2,1,0:T(8,128)(2,1)S(1)} %constant_dynamic-update-slice_fusion), channel_id=1, source_target_pairs={{0,8},{8,0},{16,24},{24,16},{32,40},{40,32},{48,56},{56,48},{64,72... | collective-permute-start | bytes 4718600 | tf_op jit(solution)/shard_map/ppermute | solution.py:85
  53.7 2.3 %copy-start.6 = (bf16[1024,1024]{1,0:T(8,128)(2,1)S(1)}, bf16[1024,1024]{1,0:T(8,128)(2,1)}, u32[]{:S(2)}) copy-start(bf16[1024,1024]{1,0:T(8,128)(2,1)} %param.14) | copy-start | bytes 6291460
  53.7 2.3 %copy-start.8 = (bf16[384,1024]{1,0:T(8,128)(2,1)S(1)}, bf16[384,1024]{1,0:T(8,128)(2,1)}, u32[]{:S(2)}) copy-start(bf16[384,1024]{1,0:T(8,128)(2,1)} %get-tuple-element.70) | copy-start | bytes 2359300
  56.0 1.9 copy-start.5
  105.1 9.0 %copy-start.2 = (s32[384]{0:T(512)S(1)}, s32[384]{0:T(512)}, u32[]{:S(2)}) copy-start(s32[384]{0:T(512)} %param.11) | copy-start | bytes 4612
  105.1 41.3 %all-to-all-start.1 = ((bf16[8,48,3200]{2,1,0:T(8,128)(2,1)}), bf16[8,48,3200]{2,1,0:T(8,128)(2,1)}, u32[]{:S(2)}, u32[]{:S(2)}) async-start(bf16[8,48,3200]{2,1,0:T(8,128)(2,1)} %broadcast_in_dim.60), calls=%async_computation.1 | async-start | bytes 4915200 | tf_op jit(solution)/shard_map/all_to_all | solution.py:136
  155.2 4.0 %collective-permute-start.10 = (bf16[384,1024]{1,0:T(8,128)(2,1)S(1)}, bf16[384,1024]{1,0:T(8,128)(2,1)S(1)}, u32[]{:S(2)}, u32[]{:S(2)}) collective-permute-start(bf16[384,1024]{1,0:T(8,128)(2,1)S(1)} %fusion.22), channel_id=1, source_target_pairs={{0,8},{8,0},{16,24},{24,16},{32,40},{40,32},{48,56},{56,48},{64,72... | collective-permute-start | bytes 2359304 | tf_op jit(solution)/shard_map/ppermute | solution.py:161
  155.4 2.2 %collective-permute-start.12 = (f32[3,1024]{1,0:T(4,128)S(1)}, f32[3,1024]{1,0:T(4,128)S(1)}, u32[]{:S(2)}, u32[]{:S(2)}) collective-permute-start(f32[3,1024]{1,0:T(4,128)S(1)} %pad_maximum_fusion.3), channel_id=1, source_target_pairs={{0,8},{8,0},{16,24},{24,16},{32,40},{40,32},{48,56},{56,48},{64,72... | collective-permute-start | bytes 36872 | tf_op jit(solution)/shard_map/ppermute | solution.py:162
  157.6 4.0 %collective-permute-start.13 = (f32[3,1024]{1,0:T(4,128)S(1)}, f32[3,1024]{1,0:T(4,128)S(1)}, u32[]{:S(2)}, u32[]{:S(2)}) collective-permute-start(f32[3,1024]{1,0:T(4,128)S(1)} %fusion.90), channel_id=1, source_target_pairs={{0,16},{8,24},{16,0},{24,8},{32,48},{40,56},{48,32},{56,40},{64,80... | collective-permute-start | bytes 36872 | tf_op jit(solution)/shard_map/ppermute | solution.py:165
  159.9 11.0 %collective-permute-start.11 = (bf16[8,24,1024]{2,1,0:T(8,128)(2,1)S(1)}, bf16[8,24,1024]{2,1,0:T(8,128)(2,1)S(1)}, u32[]{:S(2)}, u32[]{:S(2)}) collective-permute-start(bf16[8,24,1024]{2,1,0:T(8,128)(2,1)S(1)} %bitcast.113), channel_id=1, source_target_pairs={{0,16},{8,24},{16,0},{24,8},{32,48},{40,56},{48,32},{56,40},{64,80... | collective-permute-start | bytes 1179656 | tf_op jit(solution)/shard_map/ppermute | solution.py:164
  171.8 20.3 %all-to-all-start.2 = ((bf16[8,32,1024]{2,1,0:T(8,128)(2,1)}), bf16[8,32,1024]{2,1,0:T(8,128)(2,1)S(1)}, u32[]{:S(2)}, u32[]{:S(2)}) async-start(bf16[8,32,1024]{2,1,0:T(8,128)(2,1)} %pad_maximum_fusion), calls=%async_computation.2 | async-start | bytes 1048576 | tf_op jit(solution)/shard_map/all_to_all | solution.py:170
  175.3 4.1 %copy-start.9 = (bf16[384,1024]{1,0:T(8,128)(2,1)S(1)}, bf16[384,1024]{1,0:T(8,128)(2,1)}, u32[]{:S(2)}) copy-start(bf16[384,1024]{1,0:T(8,128)(2,1)} %get-tuple-element.70) | copy-start | bytes 2359300
  183.3 9.8 %copy-start.1 = (bf16[96,1024]{1,0:T(8,128)(2,1)S(1)}, bf16[96,1024]{1,0:T(8,128)(2,1)}, u32[]{:S(2)}) copy-start(bf16[96,1024]{1,0:T(8,128)(2,1)} %param.10) | copy-start | bytes 589828
  (2 other events, 3.7 us)

commit v2 on v0

v2 whole, which is shorter than its diff:
```python
import jax
import jax.numpy as jnp
import numpy as np
from jax import lax
from jax.experimental import pallas as pl
from jax.experimental.pallas import tpu as pltpu
from jax.sharding import PartitionSpec as P

D = 8192
EPS = 1e-06
bf16 = jnp.bfloat16
f32 = jnp.float32
i32 = jnp.int32
DOWN, UP = 2.0**-20, 2.0**20
TOK = 96
CAP = 24
SEL = 384
W = 1024
TILE = 256

WIDE = [(z, y, c) for z in range(8) for y in range(2) for c in range(2)]


def wide_pairs(move):
    def index(z, y, c):
        return (z % 8 * 2 + y) * 2 + c

    return [(index(*t), index(*move(*t))) for t in WIDE]


CORE = wide_pairs(lambda z, y, c: (z, y, 1 - c))
YLO = wide_pairs(lambda z, y, c: (z, 1 - y, c))
ZUP = wide_pairs(lambda z, y, c: (z + 1, y, c))
ZDOWN = wide_pairs(lambda z, y, c: (z + 7, y, c))
ZFAR = wide_pairs(lambda z, y, c: (z + 1 + 6 * c, y, c))
ZGROUPS = [[(z * 2 + y) * 2 + c for z in range(8)] for y in range(2) for c in range(2)]

GATHER = np.zeros((8, 768), np.int32)
_s = np.arange(768)
GATHER[0] = _s // 48 % 8 - 3
GATHER[1] = _s // 24 % 2
GATHER[2] = _s // 384
GATHER[3] = _s % 24
SPREAD = np.zeros((8, 768), np.int32)
SPREAD[0] = _s // 24 % 8
SPREAD[1] = _s // 192 % 2
SPREAD[2] = 1 - _s // 384
SPREAD[3] = _s % 24

VMEM = pl.BlockSpec(memory_space=pltpu.VMEM)


def params(mib=48):
    return pltpu.CompilerParams(vmem_limit_bytes=mib << 20)


def cost(flops, bytes_):
    return pl.CostEstimate(flops=int(flops), bytes_accessed=int(bytes_), transcendentals=0)


def pieces(value, count):
    out = []
    for _ in range(count):
        head = lax.reduce_precision(value, 8, 7)
        out.append(head.astype(bf16))
        value = jnp.where(jnp.abs(head) < jnp.inf, value - head, 0.0)
    return out


def heads(value, count):
    out = []
    for _ in range(count):
        head = value.astype(bf16).astype(f32)
        out.append(head)
        value = jnp.where(jnp.abs(head) < jnp.inf, value - head, 0.0)
    return out


def lanes_of(columns, rows):
    lane = lax.broadcasted_iota(i32, (rows, 128), 1)
    out = jnp.zeros((rows, 128), f32)
    for k, column in enumerate(columns):
        out = jnp.where(lane == k, column, out)
    return out.astype(bf16)


def mm(a, b, ca, cb):
    return lax.dot_general(a, b, (((ca,), (cb,)), ((), ())), preferred_element_type=f32)


def place_of():
    w = lax.axis_index("wide")
    return w, w // 4, (w // 2) % 2, w % 2


def count_before(sel_col, ids):
    return jnp.sum(jnp.where(sel_col < ids, 1, 0).astype(i32), axis=0, keepdims=True)


def placement(sel_col, z, y, c, zz, yrel, crel, k):
    block = zz * 4 + (y ^ yrel) * 2 + (c ^ crel)
    start = count_before(sel_col, block * TOK)
    end = count_before(sel_col, block * TOK + TOK)
    row = lax.broadcasted_iota(i32, (SEL, k.shape[1]), 0)
    return jnp.where((row == start + k) & (row < end), 1.0, 0.0).astype(bf16)


def pick_of(sel_col, w):
    ids = w * TOK + lax.broadcasted_iota(i32, (1, TOK), 1)
    first = count_before(sel_col, jnp.full((1, 1), w * TOK, i32))
    last = count_before(sel_col, jnp.full((1, 1), w * TOK + TOK, i32))
    rank = count_before(sel_col, ids) - first
    marked = jnp.sum(jnp.where(sel_col == ids, 1, 0).astype(i32), axis=0, keepdims=True) > 0
    k = lax.broadcasted_iota(i32, (CAP, TOK), 0)
    return jnp.where((k == rank) & marked, 1.0, 0.0), first, last


def own_kernel(sel_ref, tok_ref, go_ref, x_ref, g_ref):
    w, _, _, _ = place_of()
    pick = pick_of(sel_ref[...], w)[0].astype(bf16)
    x_ref[...] = mm(pick, tok_ref[...], 1, 0).astype(bf16)
    g_ref[...] = mm(pick, go_ref[...], 1, 0).astype(bf16)


def gate_kernel(*refs):
    pieces_in = refs[:16]
    table, sel_col, gain, rw, wg, wu, put, sel, out, slots, scaled = refs[16:]
    j = pl.program_id(0)

    @pl.when(j == 0)
    def _():
        _, z, y, c = place_of()
        t = table[...]
        zz = (z + t[0:1] + 8) & 7
        put[...] = placement(sel_col[...], z, y, c, zz, t[1:2], t[2:3], t[3:4])
        for p in range(16):
            slots[48 * p : 48 * p + 48, :] = pieces_in[p][...]
        squares = jnp.zeros((SEL, 1), f32)
        logit = jnp.zeros((SEL, 1), f32)
        for k in range(W // TILE):
            cols = slice(k * TILE, (k + 1) * TILE)
            tile = mm(put[...], slots[:, cols], 1, 0)
            sel[:, cols] = tile.astype(bf16)
            squares += jnp.sum(tile * tile, axis=1, keepdims=True)
            logit += jnp.sum(tile * rw[:, cols], axis=1, keepdims=True)
            scaled[:, cols] = (tile * (gain[:, cols] * DOWN)).astype(bf16)
        out[:, 2 * W :] = lanes_of(heads(squares, 3) + heads(logit, 3), SEL)

    at = pl.multiple_of(j * TILE, TILE)
    out[:, pl.ds(at, TILE)] = mm(scaled[...], wg[...], 1, 0).astype(bf16)
    out[:, pl.ds(pl.multiple_of(W + j * TILE, TILE), TILE)] = mm(
        scaled[...], wu[...], 1, 0
    ).astype(bf16)


def back_kernel(*refs):
    pieces_in = refs[:16]
    put, wd, gsel, out, slots = refs[16:]
    j = pl.program_id(0)

    @pl.when(j == 0)
    def _():
        for p in range(16):
            slots[48 * p : 48 * p + 48, :] = pieces_in[p][...]
        for k in range(W // TILE):
            cols = slice(k * TILE, (k + 1) * TILE)
            gsel[:, cols] = mm(put[...], slots[:, cols], 1, 0).astype(bf16)

    out[...] = mm(gsel[...], wd[...], 1, 1).astype(bf16)


def hidden_kernel(gu, bk, d_out, h_out):
    rows = SEL // 8
    tail = jnp.sum(gu[:, :, 2 * W :].astype(f32), axis=0)
    squares = tail[:, 0:1] + tail[:, 1:2] + tail[:, 2:3]
    logit = tail[:, 3:4] + tail[:, 4:5] + tail[:, 5:6]
    scale = lax.rsqrt(squares / D + EPS)
    router_grad = jnp.zeros((rows, 1), f32)
    inner = jnp.zeros((rows, 1), f32)
    for k in range(W // TILE):
        lo, hi = k * TILE, (k + 1) * TILE
        gate = jnp.sum(gu[:, :, lo:hi].astype(f32), axis=0) * (scale * UP)
        upv = jnp.sum(gu[:, :, W + lo : W + hi].astype(f32), axis=0) * (scale * UP)
        back = jnp.sum(bk[:, :, lo:hi].astype(f32), axis=0)
        sigma = jax.nn.sigmoid(gate)
        hidden = (gate * sigma * upv).astype(bf16)
        d_hidden = logit * back
        d_gate = (d_hidden * upv * (sigma + gate * sigma * (1.0 - sigma))).astype(bf16)
        d_up = (d_hidden * gate * sigma).astype(bf16)
        router_grad += jnp.sum(hidden.astype(f32) * back, axis=1, keepdims=True)
        inner += jnp.sum(
            d_gate.astype(f32) * gate + d_up.astype(f32) * upv, axis=1, keepdims=True
        )
        for n in range(8):
            d_out[n, :, lo:hi] = d_gate
            d_out[n, :, W + lo : W + hi] = d_up
            h_out[n, :, lo:hi] = hidden
    extra = lanes_of(
        heads(scale, 3) + heads(logit, 3) + heads(router_grad, 3) + heads(inner, 3), rows
    )
    for n in range(8):
        d_out[n, :, 2 * W :] = extra


def to_row(column):
    eye = lax.broadcasted_iota(i32, (SEL, SEL), 0) == lax.broadcasted_iota(i32, (SEL, SEL), 1)
    return jnp.sum(jnp.where(eye, column, 0.0), axis=0, keepdims=True)


def normed_kernel(table, sel_col, gd, wg, wu, sel, theirs, ours, small, put, cols):
    j = pl.program_id(0)

    @pl.when(j == 0)
    def _():
        _, z, y, c = place_of()
        t = table[...]
        put[...] = placement(sel_col[...], z, y, c, t[0:1], t[1:2], t[2:3], t[3:4])
        tail = gd[:, 2 * W :].astype(f32)
        lane = lax.broadcasted_iota(i32, (SEL, 128), 1)

        def value(k):
            return jnp.sum(
                jnp.where((lane >= 3 * k) & (lane < 3 * k + 3), tail, 0.0), axis=1, keepdims=True
            )

        scale, router_grad, inner = value(0), value(2), value(3)
        cols[...] = jnp.where(lane == 0, scale, router_grad)
        small[...] = jnp.zeros(small.shape, f32)
        small[2:3, 0:SEL] = to_row(router_grad)
        small[2:3, SEL : 2 * SEL] = to_row(inner)
        small[3:4, 0:SEL] = to_row(scale)

    part = mm(gd[:, 0:W], wg[...], 1, 1) + mm(gd[:, W : 2 * W], wu[...], 1, 1)
    sel32 = sel[...].astype(f32)
    at = pl.ds(pl.multiple_of(j * TILE, TILE), TILE)
    small[0:1, at] = jnp.sum(part * sel32 * cols[:, 0:1], axis=0, keepdims=True)
    small[1:2, at] = jnp.sum(sel32 * cols[:, 1:2], axis=0, keepdims=True)
    rounded = part.astype(bf16)
    both = mm(put[...], rounded, 0, 0).astype(bf16)
    theirs[...] = both[:SEL]
    ours[...] = both[SEL:]


def final_kernel(msg, x, go, gain, rw, sel_col, small, grad_x, out_small):
    w, _, _, _ = place_of()
    pick, first, last = pick_of(sel_col[...], w)
    total = jnp.sum(msg[...].astype(f32), axis=0)
    summed = total[CAP : CAP + 3] + total[CAP + 3 : CAP + 6]
    out_small[...] = summed
    own = total[:CAP]
    row = lax.broadcasted_iota(i32, (CAP, SEL), 1)
    k = lax.broadcasted_iota(i32, (CAP, SEL), 0)
    where = (row == first + k) & (row < last)

    def mine(values):
        return jnp.sum(jnp.where(where, values, 0.0), axis=1, keepdims=True)

    scale = mine(small[3:4, 0:SEL])
    router_grad = mine(summed[2:3, 0:SEL])
    inner = mine(summed[2:3, SEL : 2 * SEL])
    d_sel = (
        scale * gain[...] * own
        - x[...].astype(f32) * (scale * scale * inner / D)
        + router_grad * rw[...]
    )
    spread = jnp.zeros((TOK, W), f32)
    for piece in heads(d_sel, 3):
        spread += mm(pick.astype(bf16), piece.astype(bf16), 0, 0)
    grad_x[...] = (go[...].astype(f32) + spread).astype(bf16)


def gather(mine):
    pair = jnp.concatenate([mine, lax.ppermute(mine, "wide", YLO)], axis=0)
    held = {0: pair}
    for k in range(1, 4):
        held[-k] = lax.ppermute(held[1 - k], "wide", ZUP)
        held[k] = lax.ppermute(held[k - 1], "wide", ZDOWN)
    core = lax.axis_index("wide") % 2
    held[4] = lax.ppermute(jnp.where(core == 0, held[-3], held[3]), "wide", ZFAR)
    ours = [held[k] for k in range(-3, 5)]
    return ours + [lax.ppermute(piece, "wide", CORE) for piece in ours]


def local(tokens, grad_out, selected, gain, router_weight, w_gate, w_up, w_down):
    sel_col = selected.reshape(SEL, 1)
    gain = gain.reshape(1, W)
    router_weight = router_weight.reshape(1, W)
    slot = jax.ShapeDtypeStruct((CAP, W), bf16)
    x, g = pl.pallas_call(
        own_kernel,
        out_shape=(slot, slot),
        in_specs=[VMEM] * 3,
        out_specs=(VMEM, VMEM),
        compiler_params=params(16),
        name="own",
    )(sel_col, tokens, grad_out)
    xs = gather(x)
    gs = gather(g)

    full = lambda *shape: pl.BlockSpec(shape, lambda j: (0,) * len(shape))
    put, sel, send = pl.pallas_call(
        gate_kernel,
        grid=(W // TILE,),
        out_shape=(
            jax.ShapeDtypeStruct((SEL, 768), bf16),
            jax.ShapeDtypeStruct((SEL, W), bf16),
            jax.ShapeDtypeStruct((SEL, 2 * W + 128), bf16),
        ),
        in_specs=[full(48, W)] * 16
        + [full(8, 768), full(SEL, 1), full(1, W), full(1, W)]
        + [pl.BlockSpec((W, TILE), lambda j: (0, j))] * 2,
        out_specs=(full(SEL, 768), full(SEL, W), full(SEL, 2 * W + 128)),
        scratch_shapes=[pltpu.VMEM((768, W), bf16), pltpu.VMEM((SEL, W), bf16)],
        compiler_params=params(),
        cost_estimate=cost(2.2e9, 9e6),
        name="gate_up",
    )(*xs, jnp.asarray(GATHER), sel_col, gain, router_weight, w_gate, w_up)
    got_gu = lax.all_to_all(send.reshape(8, SEL // 8, -1), "narrow", 0, 0, tiled=True)
    gsel, send = pl.pallas_call(
        back_kernel,
        grid=(W // TILE,),
        out_shape=(
            jax.ShapeDtypeStruct((SEL, W), bf16),
            jax.ShapeDtypeStruct((SEL, W), bf16),
        ),
        in_specs=[full(48, W)] * 16
        + [full(SEL, 768), pl.BlockSpec((TILE, W), lambda j: (j, 0))],
        out_specs=(full(SEL, W), pl.BlockSpec((SEL, TILE), lambda j: (0, j))),
        scratch_shapes=[pltpu.VMEM((768, W), bf16)],
        compiler_params=params(),
        cost_estimate=cost(1.4e9, 6e6),
        name="back",
    )(*gs, put, w_down)
    got_b = lax.all_to_all(send.reshape(8, SEL // 8, -1), "narrow", 0, 0, tiled=True)

    share_d, share_h = pl.pallas_call(
        hidden_kernel,
        out_shape=(
            jax.ShapeDtypeStruct((8, SEL // 8, 2 * W + 128), bf16),
            jax.ShapeDtypeStruct((8, SEL // 8, W), bf16),
        ),
        in_specs=[VMEM, VMEM],
        out_specs=(VMEM, VMEM),
        compiler_params=params(),
        name="hidden",
    )(got_gu, got_b)
    gd = lax.all_to_all(share_d, "narrow", 0, 0, tiled=True).reshape(SEL, -1)
    gd, share_h = lax.optimization_barrier((gd, share_h))
    hidden = lax.all_to_all(share_h, "narrow", 0, 0, tiled=True).reshape(SEL, W)

    theirs, ours, small = pl.pallas_call(
        normed_kernel,
        grid=(W // TILE,),
        out_shape=(
            jax.ShapeDtypeStruct((SEL, W), bf16),
            jax.ShapeDtypeStruct((SEL, W), bf16),
            jax.ShapeDtypeStruct((8, W), f32),
        ),
        in_specs=[full(8, 768), full(SEL, 1), full(SEL, 2 * W + 128)]
        + [pl.BlockSpec((TILE, W), lambda j: (j, 0))] * 2
        + [pl.BlockSpec((SEL, TILE), lambda j: (0, j))],
        out_specs=(
            pl.BlockSpec((SEL, TILE), lambda j: (0, j)),
            pl.BlockSpec((SEL, TILE), lambda j: (0, j)),
            full(8, W),
        ),
        scratch_shapes=[pltpu.VMEM((SEL, 768), bf16), pltpu.VMEM((SEL, 128), f32)],
        compiler_params=params(),
        cost_estimate=cost(2.4e9, 9e6),
        name="normed",
    )(jnp.asarray(SPREAD), sel_col, gd, w_gate, w_up, sel)

    total = small[:3]
    part = ours.astype(f32) + lax.ppermute(theirs, "wide", CORE).astype(f32)
    total = total + lax.ppermute(total, "wide", CORE)
    part = part.reshape(2, 8, CAP, W)
    part = part[0] + lax.ppermute(part[1].astype(bf16), "wide", YLO).astype(f32)
    total = total + lax.ppermute(total, "wide", YLO)
    packed = jnp.concatenate(pieces(total, 2) + [jnp.zeros((2, W), bf16)], axis=0)
    message = jnp.concatenate(
        [part.astype(bf16), jnp.broadcast_to(packed[None], (8,) + packed.shape)], axis=1
    )
    message = lax.all_to_all(
        message, "wide", 0, 0, tiled=True, axis_index_groups=ZGROUPS
    )

    tail = gd[:, 2 * W :].astype(f32)
    scale = jnp.sum(tail[:, 0:3], axis=1, keepdims=True)
    logit = jnp.sum(tail[:, 3:6], axis=1, keepdims=True)
    normed = (sel.astype(f32) * scale * gain).astype(bf16)
    d_out = (logit * gsel.astype(f32)).astype(bf16)
    grad_gate = mm(normed, gd[:, :W], 0, 0).astype(bf16)
    grad_up = mm(normed, gd[:, W : 2 * W], 0, 0).astype(bf16)
    grad_down = mm(hidden, d_out, 0, 0).astype(bf16)

    grad_x, total = pl.pallas_call(
        final_kernel,
        out_shape=(
            jax.ShapeDtypeStruct((TOK, W), bf16),
            jax.ShapeDtypeStruct((3, W), f32),
        ),
        in_specs=[VMEM] * 7,
        out_specs=(VMEM, VMEM),
        compiler_params=params(16),
        name="final",
    )(message, x, grad_out, gain, router_weight, sel_col, small)
    return (grad_x, grad_gate, grad_up, grad_down, total[0], total[1])


def solution(mesh):
    return jax.shard_map(
        local,
        mesh=mesh,
        in_specs=(
            P("wide", "narrow"),
            P("wide", "narrow"),
            P(),
            P("narrow"),
            P("narrow"),
            P("narrow", "wide"),
            P("narrow", "wide"),
            P("wide", "narrow"),
        ),
        out_specs=(
            P("wide", "narrow"),
            P("narrow", "wide"),
            P("narrow", "wide"),
            P("wide", "narrow"),
            P("narrow"),
            P("narrow"),
        ),
        check_vma=False,
    )
```

time: 668 us -> 186 us (0.28); the launches traced: 661 us -> 186 us
  waiting for transfers between devices: 418 us -> 32.5 us
  blocking collectives: 167 us -> 67.6 us
  starting transfers between devices: 0.16 us -> 48.8 us
  matrix products: 31.5 us -> 9.25 us
  other arithmetic: 23.8 us -> 2.73 us
  Pallas kernels: 0 us -> 19.4 us
  between operations: 14 us -> 0.93 us
    psum x1 -> x0, waiting for transfers between devices: 207 us -> none  [local(): lax.psum((jnp.dot(normed, w_gate, preferred_element_type=jnp.float32), jn...]
    psum x5 -> x0, blocking collectives: 167 us -> none  [the longest x1 57 us: local(): lax.psum(jnp.sum(hidden.astype(jnp.float32) * back, axis=1), 'wide')]
    reduce_scatter x1 -> x0, waiting for transfers between devices: 106 us -> none  [local(): lax.psum_scatter(first + jnp.einsum('rf,df->rd', d_up, w_up, preferred_el...]
    all_gather x2 -> x0, waiting for transfers between devices: 104 us -> none  [the longest x1 66.1 us: local(): lax.all_gather(x_slots, 'wide', axis=0, tiled=True)]
    all_to_all x0 -> x3, blocking collectives: none -> 67.6 us  [the longest x2 42.8 us: local(): lax.all_to_all(send.reshape(8, SEL // 8, -1), 'narrow', 0, 0, tiled=True)]
    ppermute x0 -> x36, starting transfers between devices: none -> 33.6 us  [the longest x6 20.4 us: gather(): held[k] = lax.ppermute(held[k - 1], 'wide', ZDOWN)]
    ppermute x0 -> x36, waiting for transfers between devices: none -> 24.1 us  [the longest x1 8.19 us: local(): part = part[0] + lax.ppermute(part[1].astype(bf16), 'wide', YLO).astype(f32)]
    dot_general x8 -> x3, matrix products: 31.5 us -> 9.25 us  [mm(): lax.dot_general(a, b, (((ca,), (cb,)), ((), ())), preferred_element_type=...]
  transfers between devices with their start and end apart: 4 -> 38, of which waited for: 4 -> 9; matrix products, arithmetic and copies ran while one was open for 4% -> 7% of each run, Pallas kernels for 0% -> 3%
where the time goes in v2:
time: 186 us
  blocking collectives  67.6 us (36%)
  starting transfers between devices  48.8 us (26%)
  waiting for transfers between devices  32.5 us (17%)
  Pallas kernels  19.4 us (10%)
  matrix products  9.25 us (5%)
  local copies, waits for them, and re-layouts  4.39 us (2%)
  other arithmetic  2.73 us (1%)
    all_to_all x2, blocking collectives, local(): lax.all_to_all(send.reshape(8, SEL // 8, -1), 'narrow', 0, 0, tiled=True)  42.8 us
    all_to_all x1, blocking collectives, local(): gd = lax.all_to_all(share_d, 'narrow', 0, 0, tiled=True).reshape(SEL, -1)  24.8 us
    ppermute x6, starting transfers between devices, gather(): held[k] = lax.ppermute(held[k - 1], 'wide', ZDOWN)  20.4 us
    dot_general x3, matrix products, mm(): lax.dot_general(a, b, (((ca,), (cb,)), ((), ())), preferred_element_type=...  9.25 us
    all_to_all x1, waiting for transfers between devices, local(): lax.all_to_all(message, 'wide', 0, 0, tiled=True, axis_index_groups=ZGROUPS)  8.4 us
    all_to_all x1, starting transfers between devices, local(): hidden = lax.all_to_all(share_h, 'narrow', 0, 0, tiled=True).reshape(SEL, W)  8.36 us
    ppermute x1, waiting for transfers between devices, local(): part = part[0] + lax.ppermute(part[1].astype(bf16), 'wide', YLO).astype(f32)  8.19 us
    pallas_call x1, Pallas kernels, local(): pl.pallas_call(normed_kernel, grid=(W // TILE,), out_shape=(jax.ShapeDtyp...  7.82 us
  transfers between devices with their start and end apart: 38, of which 9 were waited for; matrix products, arithmetic and copies ran while one was open for 7% of the time, Pallas kernels for 3%

profile of v2, /device:TPU:22, one launch (start us, length us, event | category | flops | bytes accessed | tf_op | source)
XLA Modules:
  0.0 185.6 jit_solution(1181022922116044897)
XLA Ops:
  5.8 2.4 %collective-permute-done = bf16[24,1024]{1,0:T(8,128)(2,1)S(1)} collective-permute-done((bf16[24,1024]{1,0:T(8,128)(2,1)S(1)}, bf16[24,1024]{1,0:T(8,128)(2,1)S(1)}, u32[]{:S(2)}, u32[]{:S(2)}) %collective-permute-start) | collective-permute-done | bytes 49184 | tf_op jit(solution)/shard_map/ppermute | solution.py:273
  10.1 4.0 %collective-permute-start.4 = (bf16[48,1024]{1,0:T(8,128)(2,1)S(1)}, bf16[48,1024]{1,0:T(8,128)(2,1)S(1)}, u32[]{:S(2)}, u32[]{:S(2)}) collective-permute-start(bf16[48,1024]{1,0:T(8,128)(2,1)S(1)} %constant_dynamic-update-slice_fusion.refs_3_), channel_id=1, source_target_pairs={{0,224},{8,232},{16,240},{24,248},{32,0},{40,8},{48,16},{56,24},{6... | collective-permute-start | bytes 294920 | tf_op jit(solution)/shard_map/ppermute | solution.py:277
  14.2 3.2 %collective-permute-start.20 = (bf16[48,1024]{1,0:T(8,128)(2,1)S(1)}, bf16[48,1024]{1,0:T(8,128)(2,1)S(1)}, u32[]{:S(2)}, u32[]{:S(2)}) collective-permute-start(bf16[48,1024]{1,0:T(8,128)(2,1)S(1)} %constant_dynamic-update-slice_fusion.2.refs_3_), channel_id=1, source_target_pairs={{0,224},{8,232},{16,240},{24,248},{32,0},{40,8},{48,16},{56,24},{6... | collective-permute-start | bytes 294920 | tf_op jit(solution)/shard_map/ppermute | solution.py:277
  17.5 3.5 %collective-permute-start.5 = (bf16[48,1024]{1,0:T(8,128)(2,1)S(1)}, bf16[48,1024]{1,0:T(8,128)(2,1)S(1)}, u32[]{:S(2)}, u32[]{:S(2)}) collective-permute-start(bf16[48,1024]{1,0:T(8,128)(2,1)S(1)} %collective-permute-done.4.refs_4_), channel_id=1, source_target_pairs={{0,224},{8,232},{16,240},{24,248},{32,0},{40,8},{48,16},{56,24},{6... | collective-permute-start | bytes 294920 | tf_op jit(solution)/shard_map/ppermute | solution.py:277
  21.0 3.2 %collective-permute-start.21 = (bf16[48,1024]{1,0:T(8,128)(2,1)S(1)}, bf16[48,1024]{1,0:T(8,128)(2,1)S(1)}, u32[]{:S(2)}, u32[]{:S(2)}) collective-permute-start(bf16[48,1024]{1,0:T(8,128)(2,1)S(1)} %collective-permute-done.20.refs_4_), channel_id=1, source_target_pairs={{0,224},{8,232},{16,240},{24,248},{32,0},{40,8},{48,16},{56,24},{6... | collective-permute-start | bytes 294920 | tf_op jit(solution)/shard_map/ppermute | solution.py:277
  24.2 3.2 %collective-permute-start.6 = (bf16[48,1024]{1,0:T(8,128)(2,1)S(1)}, bf16[48,1024]{1,0:T(8,128)(2,1)S(1)}, u32[]{:S(2)}, u32[]{:S(2)}) collective-permute-start(bf16[48,1024]{1,0:T(8,128)(2,1)S(1)} %collective-permute-done.5.refs_5_), channel_id=1, source_target_pairs={{0,224},{8,232},{16,240},{24,248},{32,0},{40,8},{48,16},{56,24},{6... | collective-permute-start | bytes 294920 | tf_op jit(solution)/shard_map/ppermute | solution.py:277
  28.0 2.0 %collective-permute-done.3.refs_0_ = bf16[48,1024]{1,0:T(8,128)(2,1)S(1)} collective-permute-done((bf16[48,1024]{1,0:T(8,128)(2,1)S(1)}, bf16[48,1024]{1,0:T(8,128)(2,1)S(1)}, u32[]{:S(2)}, u32[]{:S(2)}) %collective-permute-start.3) | collective-permute-done | bytes 98336 | tf_op jit(solution)/shard_map/ppermute | solution.py:276
  30.0 3.2 %collective-permute-start.22 = (bf16[48,1024]{1,0:T(8,128)(2,1)S(1)}, bf16[48,1024]{1,0:T(8,128)(2,1)S(1)}, u32[]{:S(2)}, u32[]{:S(2)}) collective-permute-start(bf16[48,1024]{1,0:T(8,128)(2,1)S(1)} %collective-permute-done.21.refs_5_), channel_id=1, source_target_pairs={{0,224},{8,232},{16,240},{24,248},{32,0},{40,8},{48,16},{56,24},{6... | collective-permute-start | bytes 294920 | tf_op jit(solution)/shard_map/ppermute | solution.py:277
  37.2 2.4 %collective-permute-start.23 = (bf16[48,1024]{1,0:T(8,128)(2,1)S(1)}, bf16[48,1024]{1,0:T(8,128)(2,1)S(1)}, u32[]{:S(2)}, u32[]{:S(2)}) collective-permute-start(bf16[48,1024]{1,0:T(8,128)(2,1)S(1)} %broadcast_select_fusion), channel_id=1, source_target_pairs={{0,32},{8,232},{16,48},{24,248},{32,64},{40,8},{48,80},{56,24},{64... | collective-permute-start | bytes 294920 | tf_op jit(solution)/shard_map/ppermute | solution.py:279
  39.5 2.1 %collective-permute-done.7.refs_7_ = bf16[48,1024]{1,0:T(8,128)(2,1)S(1)} collective-permute-done((bf16[48,1024]{1,0:T(8,128)(2,1)S(1)}, bf16[48,1024]{1,0:T(8,128)(2,1)S(1)}, u32[]{:S(2)}, u32[]{:S(2)}) %collective-permute-start.7) | collective-permute-done | bytes 98336 | tf_op jit(solution)/shard_map/ppermute | solution.py:279
  43.5 6.1 %gate_up.1 = (bf16[384,768]{1,0:T(8,128)(2,1)S(1)}, bf16[384,1024]{1,0:T(8,128)(2,1)S(1)}, bf16[384,2176]{1,0:T(8,128)(2,1)S(1)}) custom-call(bf16[48,1024]{1,0:T(8,128)(2,1)S(1)} %collective-permute-done.3.refs_0_, bf16[48,1024]{1,0:T(8,128)(2,1)S(1)} %collective-permute-done.2.refs_1_, bf16[48,1024]{1,0:T(8,128)(2,1)S(1)} %collective-permute-done.1.refs_2_, ...), custom_call_target="tpu_custom_call" | custom-call | flops 2200000000 | bytes 9000000 | tf_op jit(solution)/shard_map/gate_up/pallas_call | solution.py:301
  49.6 2.6 %back.1 = (bf16[384,1024]{1,0:T(8,128)(2,1)S(1)}, bf16[384,1024]{1,0:T(8,128)(2,1)S(1)}) custom-call(bf16[48,1024]{1,0:T(8,128)(2,1)S(1)} %collective-permute-done.19.refs_0_, bf16[48,1024]{1,0:T(8,128)(2,1)S(1)} %collective-permute-done.18.refs_1_, bf16[48,1024]{1,0:T(8,128)(2,1)S(1)} %collective-permute-done.17.refs_2_, ...), custom_call_target="tpu_custom_call" | custom-call | flops 1400000000 | bytes 6000000 | tf_op jit(solution)/shard_map/back/pallas_call | solution.py:319
  53.1 17.4 %all_to_all.25.bk = bf16[8,48,1024]{2,1,0:T(8,128)(2,1)S(1)} all-to-all(bf16[8,48,1024]{2,1,0:T(8,128)(2,1)S(1)} %bitcast.16), channel_id=1, replica_groups=mesh['wide'=32,'narrow'=8] {'narrow'}, dimensions={0} | all-to-all | bytes 1572864 | tf_op jit(solution)/shard_map/all_to_all | solution.py:334
  70.6 25.3 %all_to_all.26.gu = bf16[8,48,2176]{2,1,0:T(8,128)(2,1)S(1)} all-to-all(bf16[8,48,2176]{2,1,0:T(8,128)(2,1)S(1)} %bitcast.15), channel_id=1, replica_groups=mesh['wide'=32,'narrow'=8] {'narrow'}, dimensions={0} | all-to-all | bytes 3342336 | tf_op jit(solution)/shard_map/all_to_all | solution.py:318
  97.3 24.8 %all_to_all.27 = bf16[8,48,2176]{2,1,0:T(8,128)(2,1)S(1)} all-to-all(bf16[8,48,2176]{2,1,0:T(8,128)(2,1)S(1)} %get-tuple-element.27), channel_id=1, replica_groups=mesh['wide'=32,'narrow'=8] {'narrow'}, dimensions={0} | all-to-all | bytes 3342336 | tf_op jit(solution)/shard_map/all_to_all | solution.py:347
  122.2 7.8 %normed.1 = (bf16[384,1024]{1,0:T(8,128)(2,1)}, bf16[384,1024]{1,0:T(8,128)(2,1)S(1)}, f32[8,1024]{1,0:T(8,128)S(1)}) custom-call(s32[8,768]{1,0:T(8,128)S(1)} %copy-done.6, s32[384,1]{1,0:T(8,128)S(1)} %reshape.50.sel_ref.refs_17_.sel_col, bf16[384,2176]{1,0:T(8,128)(2,1)S(1)} %bitcast.11, bf16[1024,1024]{1,0:T(8,128)(2,1)} %wg.1, bf16[1024,1024]{1,0:T(8,128)(2,1)} %wu.1, ...), custom_call_target="tpu_custom_call" | custom-call | flops 2400000000 | bytes 9000000 | tf_op jit(solution)/shard_map/normed/pallas_call | solution.py:351
  130.9 8.4 %all-to-all-start.4 = ((bf16[8,48,1024]{2,1,0:T(8,128)(2,1)}), bf16[8,48,1024]{2,1,0:T(8,128)(2,1)}, u32[]{:S(2)}, u32[]{:S(2)}) async-start(bf16[8,48,1024]{2,1,0:T(8,128)(2,1)} %get-tuple-element.35), calls=%async_computation.4 | async-start | bytes 1572864 | tf_op jit(solution)/shard_map/all_to_all | solution.py:349
  142.9 7.0 %collective-permute-done.35 = f32[3,1024]{1,0:T(4,128)S(1)} collective-permute-done((f32[3,1024]{1,0:T(4,128)S(1)}, f32[3,1024]{1,0:T(4,128)S(1)}, u32[]{:S(2)}, u32[]{:S(2)}) %collective-permute-start.35) | collective-permute-done | bytes 12320 | tf_op jit(solution)/shard_map/ppermute | solution.py:378
  150.1 8.2 %collective-permute-done.33 = bf16[8,24,1024]{2,1,0:T(8,128)(2,1)S(1)} collective-permute-done((bf16[8,24,1024]{2,1,0:T(8,128)(2,1)S(1)}, bf16[8,24,1024]{2,1,0:T(8,128)(2,1)S(1)}, u32[]{:S(2)}, u32[]{:S(2)}) %collective-permute-start.33) | collective-permute-done | bytes 393248 | tf_op jit(solution)/shard_map/ppermute | solution.py:377
  159.3 6.8 %all-to-all-start.3 = ((bf16[8,32,1024]{2,1,0:T(8,128)(2,1)}), bf16[8,32,1024]{2,1,0:T(8,128)(2,1)S(1)}, u32[]{:S(2)}, u32[]{:S(2)}) async-start(bf16[8,32,1024]{2,1,0:T(8,128)(2,1)} %pad_maximum_fusion), calls=%async_computation.3 | async-start | bytes 1048576 | tf_op jit(solution)/shard_map/all_to_all | solution.py:383
  166.1 2.7 %convolution_convert_fusion.2 = bf16[1024,1024]{1,0:T(8,128)(2,1)} fusion(bf16[384,2176]{1,0:T(8,128)(2,1)S(1)} %bitcast.13, bf16[384,1024]{1,0:T(8,128)(2,1)S(1)} %copy-done.11, f32[1024]{0:T(1024)S(1)} %copy-done.3, f32[384]{0:T(512)S(1)} %get-tuple-element.39), kind=kOutput, calls=%fused_computation.2 | convolution fusion | flops 807927808 | bytes 3676160 | tf_op jit(solution)/shard_map/dot_general | solution.py:88
  168.8 2.7 %convolution_convert_fusion.1 = bf16[1024,1024]{1,0:T(8,128)(2,1)} fusion(bf16[384,2176]{1,0:T(8,128)(2,1)S(1)} %bitcast.14, bf16[384,1024]{1,0:T(8,128)(2,1)S(1)} %copy-done.12, f32[1024]{0:T(1024)S(1)} %copy-done.3, f32[384]{0:T(512)S(1)} %get-tuple-element.39), kind=kOutput, calls=%fused_computation.1 | convolution fusion | flops 807927808 | bytes 3676160 | tf_op jit(solution)/shard_map/dot_general | solution.py:88
  171.5 3.8 %convolution_convert_fusion = bf16[1024,1024]{1,0:T(8,128)(2,1)} fusion(bf16[384,1024]{1,0:T(8,128)(2,1)} %bitcast.7, bf16[384,1024]{1,0:T(8,128)(2,1)S(1)} %copy-done.9, f32[384]{0:T(512)S(1)} %get-tuple-element.38), kind=kOutput, calls=%fused_computation | convolution fusion | flops 807534592 | bytes 3671552 | tf_op jit(solution)/shard_map/dot_general | solution.py:88
  175.4 8.4 %all-to-all-done.3.msg = bf16[8,32,1024]{2,1,0:T(8,128)(2,1)S(1)} async-done(((bf16[8,32,1024]{2,1,0:T(8,128)(2,1)}), bf16[8,32,1024]{2,1,0:T(8,128)(2,1)S(1)}, u32[]{:S(2)}, u32[]{:S(2)}) %all-to-all-start.3) | async-done | bytes 524320 | tf_op jit(solution)/shard_map/all_to_all | solution.py:383
  (112 shorter events, 23.2 us)
Async XLA Ops:
  5.0 9.1 %collective-permute-start.16 = (bf16[24,1024]{1,0:T(8,128)(2,1)S(1)}, bf16[24,1024]{1,0:T(8,128)(2,1)S(1)}, u32[]{:S(2)}, u32[]{:S(2)}) collective-permute-start(bf16[24,1024]{1,0:T(8,128)(2,1)S(1)} %get-tuple-element.24), channel_id=1, source_target_pairs={{0,16},{8,24},{16,0},{24,8},{32,48},{40,56},{48,32},{56,40},{64,80... | collective-permute-start | bytes 147464 | tf_op jit(solution)/shard_map/ppermute | solution.py:273
  8.2 9.3 %collective-permute-start.1 = (bf16[48,1024]{1,0:T(8,128)(2,1)S(1)}, bf16[48,1024]{1,0:T(8,128)(2,1)S(1)}, u32[]{:S(2)}, u32[]{:S(2)}) collective-permute-start(bf16[48,1024]{1,0:T(8,128)(2,1)S(1)} %constant_dynamic-update-slice_fusion.refs_3_), channel_id=1, source_target_pairs={{0,32},{8,40},{16,48},{24,56},{32,64},{40,72},{48,80},{56,88},{64,... | collective-permute-start | bytes 294920 | tf_op jit(solution)/shard_map/ppermute | solution.py:276
  10.1 7.3 %collective-permute-start.4 = (bf16[48,1024]{1,0:T(8,128)(2,1)S(1)}, bf16[48,1024]{1,0:T(8,128)(2,1)S(1)}, u32[]{:S(2)}, u32[]{:S(2)}) collective-permute-start(bf16[48,1024]{1,0:T(8,128)(2,1)S(1)} %constant_dynamic-update-slice_fusion.refs_3_), channel_id=1, source_target_pairs={{0,224},{8,232},{16,240},{24,248},{32,0},{40,8},{48,16},{56,24},{6... | collective-permute-start | bytes 294920 | tf_op jit(solution)/shard_map/ppermute | solution.py:277
  14.2 6.8 %collective-permute-start.17 = (bf16[48,1024]{1,0:T(8,128)(2,1)S(1)}, bf16[48,1024]{1,0:T(8,128)(2,1)S(1)}, u32[]{:S(2)}, u32[]{:S(2)}) collective-permute-start(bf16[48,1024]{1,0:T(8,128)(2,1)S(1)} %constant_dynamic-update-slice_fusion.2.refs_3_), channel_id=1, source_target_pairs={{0,32},{8,40},{16,48},{24,56},{32,64},{40,72},{48,80},{56,88},{64,... | collective-permute-start | bytes 294920 | tf_op jit(solution)/shard_map/ppermute | solution.py:276
  14.2 6.7 %collective-permute-start.20 = (bf16[48,1024]{1,0:T(8,128)(2,1)S(1)}, bf16[48,1024]{1,0:T(8,128)(2,1)S(1)}, u32[]{:S(2)}, u32[]{:S(2)}) collective-permute-start(bf16[48,1024]{1,0:T(8,128)(2,1)S(1)} %constant_dynamic-update-slice_fusion.2.refs_3_), channel_id=1, source_target_pairs={{0,224},{8,232},{16,240},{24,248},{32,0},{40,8},{48,16},{56,24},{6... | collective-permute-start | bytes 294920 | tf_op jit(solution)/shard_map/ppermute | solution.py:277
  17.5 6.7 %collective-permute-start.2 = (bf16[48,1024]{1,0:T(8,128)(2,1)S(1)}, bf16[48,1024]{1,0:T(8,128)(2,1)S(1)}, u32[]{:S(2)}, u32[]{:S(2)}) collective-permute-start(bf16[48,1024]{1,0:T(8,128)(2,1)S(1)} %collective-permute-done.1.refs_2_), channel_id=1, source_target_pairs={{0,32},{8,40},{16,48},{24,56},{32,64},{40,72},{48,80},{56,88},{64,... | collective-permute-start | bytes 294920 | tf_op jit(solution)/shard_map/ppermute | solution.py:276
  17.5 6.7 %collective-permute-start.5 = (bf16[48,1024]{1,0:T(8,128)(2,1)S(1)}, bf16[48,1024]{1,0:T(8,128)(2,1)S(1)}, u32[]{:S(2)}, u32[]{:S(2)}) collective-permute-start(bf16[48,1024]{1,0:T(8,128)(2,1)S(1)} %collective-permute-done.4.refs_4_), channel_id=1, source_target_pairs={{0,224},{8,232},{16,240},{24,248},{32,0},{40,8},{48,16},{56,24},{6... | collective-permute-start | bytes 294920 | tf_op jit(solution)/shard_map/ppermute | solution.py:277
  21.0 6.5 %collective-permute-start.18 = (bf16[48,1024]{1,0:T(8,128)(2,1)S(1)}, bf16[48,1024]{1,0:T(8,128)(2,1)S(1)}, u32[]{:S(2)}, u32[]{:S(2)}) collective-permute-start(bf16[48,1024]{1,0:T(8,128)(2,1)S(1)} %collective-permute-done.17.refs_2_), channel_id=1, source_target_pairs={{0,32},{8,40},{16,48},{24,56},{32,64},{40,72},{48,80},{56,88},{64,... | collective-permute-start | bytes 294920 | tf_op jit(solution)/shard_map/ppermute | solution.py:276
  21.0 7.0 %collective-permute-start.21 = (bf16[48,1024]{1,0:T(8,128)(2,1)S(1)}, bf16[48,1024]{1,0:T(8,128)(2,1)S(1)}, u32[]{:S(2)}, u32[]{:S(2)}) collective-permute-start(bf16[48,1024]{1,0:T(8,128)(2,1)S(1)} %collective-permute-done.20.refs_4_), channel_id=1, source_target_pairs={{0,224},{8,232},{16,240},{24,248},{32,0},{40,8},{48,16},{56,24},{6... | collective-permute-start | bytes 294920 | tf_op jit(solution)/shard_map/ppermute | solution.py:277
  27.4 5.8 %collective-permute-start.11 = (bf16[48,1024]{1,0:T(8,128)(2,1)S(1)}, bf16[48,1024]{1,0:T(8,128)(2,1)S(1)}, u32[]{:S(2)}, u32[]{:S(2)}) collective-permute-start(bf16[48,1024]{1,0:T(8,128)(2,1)S(1)} %constant_dynamic-update-slice_fusion.refs_3_), channel_id=1, source_target_pairs={{0,8},{8,0},{16,24},{24,16},{32,40},{40,32},{48,56},{56,48},{64,72... | collective-permute-start | bytes 294920 | tf_op jit(solution)/shard_map/ppermute | solution.py:281
  27.4 6.0 %collective-permute-start.27 = (bf16[48,1024]{1,0:T(8,128)(2,1)S(1)}, bf16[48,1024]{1,0:T(8,128)(2,1)S(1)}, u32[]{:S(2)}, u32[]{:S(2)}) collective-permute-start(bf16[48,1024]{1,0:T(8,128)(2,1)S(1)} %constant_dynamic-update-slice_fusion.2.refs_3_), channel_id=1, source_target_pairs={{0,8},{8,0},{16,24},{24,16},{32,40},{40,32},{48,56},{56,48},{64,72... | collective-permute-start | bytes 294920 | tf_op jit(solution)/shard_map/ppermute | solution.py:281
  28.0 5.9 %collective-permute-start.10 = (bf16[48,1024]{1,0:T(8,128)(2,1)S(1)}, bf16[48,1024]{1,0:T(8,128)(2,1)S(1)}, u32[]{:S(2)}, u32[]{:S(2)}) collective-permute-start(bf16[48,1024]{1,0:T(8,128)(2,1)S(1)} %collective-permute-done.1.refs_2_), channel_id=1, source_target_pairs={{0,8},{8,0},{16,24},{24,16},{32,40},{40,32},{48,56},{56,48},{64,72... | collective-permute-start | bytes 294920 | tf_op jit(solution)/shard_map/ppermute | solution.py:281
  35.9 5.8 %collective-permute-start.7 = (bf16[48,1024]{1,0:T(8,128)(2,1)S(1)}, bf16[48,1024]{1,0:T(8,128)(2,1)S(1)}, u32[]{:S(2)}, u32[]{:S(2)}) collective-permute-start(bf16[48,1024]{1,0:T(8,128)(2,1)S(1)} %broadcast_select_fusion.1), channel_id=1, source_target_pairs={{0,32},{8,232},{16,48},{24,248},{32,64},{40,8},{48,80},{56,24},{64... | collective-permute-start | bytes 294920 | tf_op jit(solution)/shard_map/ppermute | solution.py:279
  41.7 7.9 %collective-permute-start.25 = (bf16[48,1024]{1,0:T(8,128)(2,1)S(1)}, bf16[48,1024]{1,0:T(8,128)(2,1)S(1)}, u32[]{:S(2)}, u32[]{:S(2)}) collective-permute-start(bf16[48,1024]{1,0:T(8,128)(2,1)S(1)} %collective-permute-done.18.refs_1_), channel_id=1, source_target_pairs={{0,8},{8,0},{16,24},{24,16},{32,40},{40,32},{48,56},{56,48},{64,72... | collective-permute-start | bytes 294920 | tf_op jit(solution)/shard_map/ppermute | solution.py:281
  42.2 7.4 %collective-permute-start.29 = (bf16[48,1024]{1,0:T(8,128)(2,1)S(1)}, bf16[48,1024]{1,0:T(8,128)(2,1)S(1)}, u32[]{:S(2)}, u32[]{:S(2)}) collective-permute-start(bf16[48,1024]{1,0:T(8,128)(2,1)S(1)} %collective-permute-done.21.refs_5_), channel_id=1, source_target_pairs={{0,8},{8,0},{16,24},{24,16},{32,40},{40,32},{48,56},{56,48},{64,72... | collective-permute-start | bytes 294920 | tf_op jit(solution)/shard_map/ppermute | solution.py:281
  42.3 7.3 %collective-permute-start.24 = (bf16[48,1024]{1,0:T(8,128)(2,1)S(1)}, bf16[48,1024]{1,0:T(8,128)(2,1)S(1)}, u32[]{:S(2)}, u32[]{:S(2)}) collective-permute-start(bf16[48,1024]{1,0:T(8,128)(2,1)S(1)} %collective-permute-done.19.refs_0_), channel_id=1, source_target_pairs={{0,8},{8,0},{16,24},{24,16},{32,40},{40,32},{48,56},{56,48},{64,72... | collective-permute-start | bytes 294920 | tf_op jit(solution)/shard_map/ppermute | solution.py:281
  43.0 6.6 %collective-permute-start.30 = (bf16[48,1024]{1,0:T(8,128)(2,1)S(1)}, bf16[48,1024]{1,0:T(8,128)(2,1)S(1)}, u32[]{:S(2)}, u32[]{:S(2)}) collective-permute-start(bf16[48,1024]{1,0:T(8,128)(2,1)S(1)} %collective-permute-done.22.refs_6_), channel_id=1, source_target_pairs={{0,8},{8,0},{16,24},{24,16},{32,40},{40,32},{48,56},{56,48},{64,72... | collective-permute-start | bytes 294920 | tf_op jit(solution)/shard_map/ppermute | solution.py:281
  43.0 6.6 %collective-permute-start.31 = (bf16[48,1024]{1,0:T(8,128)(2,1)S(1)}, bf16[48,1024]{1,0:T(8,128)(2,1)S(1)}, u32[]{:S(2)}, u32[]{:S(2)}) collective-permute-start(bf16[48,1024]{1,0:T(8,128)(2,1)S(1)} %collective-permute-done.23.refs_7_), channel_id=1, source_target_pairs={{0,8},{8,0},{16,24},{24,16},{32,40},{40,32},{48,56},{56,48},{64,72... | collective-permute-start | bytes 294920 | tf_op jit(solution)/shard_map/ppermute | solution.py:281
  130.0 10.5 %collective-permute-start.32 = (bf16[384,1024]{1,0:T(8,128)(2,1)}, bf16[384,1024]{1,0:T(8,128)(2,1)}, u32[]{:S(2)}, u32[]{:S(2)}) collective-permute-start(bf16[384,1024]{1,0:T(8,128)(2,1)} %get-tuple-element.32), channel_id=1, source_target_pairs={{0,8},{8,0},{16,24},{24,16},{32,40},{40,32},{48,56},{56,48},{64,72... | collective-permute-start | bytes 2359304 | tf_op jit(solution)/shard_map/ppermute | solution.py:374
  130.1 9.2 %collective-permute-start.34 = (f32[3,1024]{1,0:T(4,128)S(1)}, f32[3,1024]{1,0:T(4,128)S(1)}, u32[]{:S(2)}, u32[]{:S(2)}) collective-permute-start(f32[3,1024]{1,0:T(4,128)S(1)} %slice.35), channel_id=1, source_target_pairs={{0,8},{8,0},{16,24},{24,16},{32,40},{40,32},{48,56},{56,48},{64,72... | collective-permute-start | bytes 36872 | tf_op jit(solution)/shard_map/ppermute | solution.py:375
  130.9 28.4 %all-to-all-start.4 = ((bf16[8,48,1024]{2,1,0:T(8,128)(2,1)}), bf16[8,48,1024]{2,1,0:T(8,128)(2,1)}, u32[]{:S(2)}, u32[]{:S(2)}) async-start(bf16[8,48,1024]{2,1,0:T(8,128)(2,1)} %get-tuple-element.35), calls=%async_computation.4 | async-start | bytes 1572864 | tf_op jit(solution)/shard_map/all_to_all | solution.py:349
  139.2 10.7 %collective-permute-start.35 = (f32[3,1024]{1,0:T(4,128)S(1)}, f32[3,1024]{1,0:T(4,128)S(1)}, u32[]{:S(2)}, u32[]{:S(2)}) collective-permute-start(f32[3,1024]{1,0:T(4,128)S(1)} %slice_add_fusion), channel_id=1, source_target_pairs={{0,16},{8,24},{16,0},{24,8},{32,48},{40,56},{48,32},{56,40},{64,80... | collective-permute-start | bytes 36872 | tf_op jit(solution)/shard_map/ppermute | solution.py:378
  141.9 16.4 %collective-permute-start.33 = (bf16[8,24,1024]{2,1,0:T(8,128)(2,1)S(1)}, bf16[8,24,1024]{2,1,0:T(8,128)(2,1)S(1)}, u32[]{:S(2)}, u32[]{:S(2)}) collective-permute-start(bf16[8,24,1024]{2,1,0:T(8,128)(2,1)S(1)} %bitcast.22), channel_id=1, source_target_pairs={{0,16},{8,24},{16,0},{24,8},{32,48},{40,56},{48,32},{56,40},{64,80... | collective-permute-start | bytes 1179656 | tf_op jit(solution)/shard_map/ppermute | solution.py:377
  159.3 24.5 %all-to-all-start.3 = ((bf16[8,32,1024]{2,1,0:T(8,128)(2,1)}), bf16[8,32,1024]{2,1,0:T(8,128)(2,1)S(1)}, u32[]{:S(2)}, u32[]{:S(2)}) async-start(bf16[8,32,1024]{2,1,0:T(8,128)(2,1)} %pad_maximum_fusion), calls=%async_computation.3 | async-start | bytes 1048576 | tf_op jit(solution)/shard_map/all_to_all | solution.py:383
  (27 other events, 322.2 us)

commit v3 on v2

v3 whole, which is shorter than its diff:
```python
import jax
import jax.numpy as jnp
from jax import lax
from jax.experimental import pallas as pl
from jax.experimental.pallas import tpu as pltpu
from jax.sharding import PartitionSpec as P

D = 8192
EPS = 1e-06
bf16 = jnp.bfloat16
f32 = jnp.float32
i32 = jnp.int32
DOWN, UP = 2.0**-20, 2.0**20
TOK = 96
CAP = 24
SEL = 384
W = 1024
TILE = 256

WIDE = [(z, y, c) for z in range(8) for y in range(2) for c in range(2)]


def wide_pairs(move):
    def index(z, y, c):
        return (z % 8 * 2 + y) * 2 + c

    return [(index(*t), index(*move(*t))) for t in WIDE]


CORE = wide_pairs(lambda z, y, c: (z, y, 1 - c))
YLO = wide_pairs(lambda z, y, c: (z, 1 - y, c))
ZFAR = wide_pairs(lambda z, y, c: (z + 2 + 4 * c, y, c))


def along(value, step):
    return lax.ppermute(value, "wide", wide_pairs(lambda z, y, c: (z + 8 + step, y, c)))


VMEM = pl.BlockSpec(memory_space=pltpu.VMEM)


def params(mib=24):
    return pltpu.CompilerParams(vmem_limit_bytes=mib << 20)


def cost(flops, bytes_):
    return pl.CostEstimate(flops=int(flops), bytes_accessed=int(bytes_), transcendentals=0)


def heads(value, count):
    out = []
    for _ in range(count):
        head = value.astype(bf16).astype(f32)
        out.append(head)
        value = jnp.where(jnp.abs(head) < jnp.inf, value - head, 0.0)
    return out


def lanes_of(columns, rows):
    lane = lax.broadcasted_iota(i32, (rows, 128), 1)
    out = jnp.zeros((rows, 128), f32)
    for k, column in enumerate(columns):
        out = jnp.where(lane == k, column, out)
    return out.astype(bf16)


def mm(a, b, ca, cb):
    return lax.dot_general(a, b, (((ca,), (cb,)), ((), ())), preferred_element_type=f32)


def place_of():
    w = lax.axis_index("wide")
    return w, w // 4, (w // 2) % 2, w % 2


def count_before(sel_col, ids):
    return jnp.sum(jnp.where(sel_col < ids, 1, 0).astype(i32), axis=0, keepdims=True)


def placement(sel_col):
    _, z, y, c = place_of()
    slot = lax.broadcasted_iota(i32, (1, 2 * SEL), 1)
    n = (slot * 2731) >> 16
    k = slot - n * CAP
    zz = (z + ((n >> 1) & 7) + 5) & 7
    block = zz * 4 + (y ^ (n & 1)) * 2 + (c ^ (n >> 4))
    start = count_before(sel_col, block * TOK)
    end = count_before(sel_col, block * TOK + TOK)
    row = lax.broadcasted_iota(i32, (SEL, 2 * SEL), 0)
    return jnp.where((row == start + k) & (row < end), 1.0, 0.0)


def pick_of(sel_row):
    w, _, _, _ = place_of()

    def before(ids):
        return jnp.sum(jnp.where(sel_row < ids, 1, 0).astype(i32), axis=1, keepdims=True)

    ids = w * TOK + lax.broadcasted_iota(i32, (TOK, 1), 0)
    first = before(jnp.full((1, 1), w * TOK, i32))
    last = before(jnp.full((1, 1), w * TOK + TOK, i32))
    rank = before(ids) - first
    marked = before(ids + 1) - before(ids) > 0
    k = lax.broadcasted_iota(i32, (TOK, CAP), 1)
    return jnp.where((k == rank) & marked, 1.0, 0.0).astype(bf16), first, last


def own_kernel(sel_hbm, tok_hbm, go_hbm, out, row, sel, tok, go, sems):
    copies = [
        pltpu.make_async_copy(tok_hbm, tok, sems.at[0]),
        pltpu.make_async_copy(go_hbm, go, sems.at[1]),
        pltpu.make_async_copy(sel_hbm, sel, sems.at[2]),
    ]
    for copy in copies:
        copy.start()
    copies[2].wait()
    sel_row = sel[...].reshape(1, SEL)
    row[...] = sel_row
    pick = pick_of(sel_row)[0]
    for n, held in enumerate((tok, go)):
        copies[n].wait()
        out[n] = mm(pick, held[...], 0, 0).astype(bf16)


def base_kernel(mine, other, out):
    parts = [mine[0], other[0], mine[1], other[1]]
    out[...] = jnp.concatenate([part.astype(f32) for part in parts], axis=0).astype(bf16)


def onehot_kernel(sel_col, gain, rw, _, put, spread, vectors):
    vectors[0:1, :] = gain[...]
    vectors[1:2, :] = rw[...]
    hot = placement(sel_col[...])
    put[...] = hot.astype(bf16)
    spread[...] = hot.T.astype(bf16)


def forward_kernel(*refs):
    parts = refs[:16]
    put, vectors, wg, wu, wd, sel, gsel, out, slots, scaled = refs[16:]
    j = pl.program_id(0)

    @pl.when(j == 0)
    def _():
        for p in range(16):
            slots[48 * p : 48 * p + 48, 0:W] = parts[p][0:48, :]
            slots[48 * p : 48 * p + 48, W : 2 * W] = parts[p][48:96, :]
        squares = jnp.zeros((SEL, 1), f32)
        logit = jnp.zeros((SEL, 1), f32)
        for k in range(W // TILE):
            cols = slice(k * TILE, (k + 1) * TILE)
            tile = mm(put[...], slots[:, cols], 1, 0)
            sel[:, cols] = tile.astype(bf16)
            squares += jnp.sum(tile * tile, axis=1, keepdims=True)
            logit += jnp.sum(tile * vectors[1:2, cols], axis=1, keepdims=True)
            scaled[:, cols] = (tile * (vectors[0:1, cols] * DOWN)).astype(bf16)
            tile = mm(put[...], slots[:, W + k * TILE : W + (k + 1) * TILE], 1, 0)
            gsel[:, cols] = tile.astype(bf16)
        out[:, 3 * W :] = lanes_of(heads(squares, 3) + heads(logit, 3), SEL)

    def at(start):
        return pl.ds(pl.multiple_of(start + j * TILE, TILE), TILE)

    out[:, at(0)] = mm(scaled[...], wg[...], 1, 0).astype(bf16)
    out[:, at(W)] = mm(scaled[...], wu[...], 1, 0).astype(bf16)
    out[:, at(2 * W)] = mm(gsel[...], wd[...], 1, 1).astype(bf16)


def hidden_kernel(got, d_out, h_out):
    rows = SEL // 8

    def total(lo, hi):
        return jnp.sum(got[:, :, lo:hi].astype(f32), axis=0)

    tail = total(3 * W, 3 * W + 128)
    squares = tail[:, 0:1] + tail[:, 1:2] + tail[:, 2:3]
    logit = tail[:, 3:4] + tail[:, 4:5] + tail[:, 5:6]
    scale = lax.rsqrt(squares / D + EPS)
    router_grad = jnp.zeros((rows, 1), f32)
    inner = jnp.zeros((rows, 1), f32)
    for k in range(W // TILE):
        lo, hi = k * TILE, (k + 1) * TILE
        gate = total(lo, hi) * (scale * UP)
        upv = total(W + lo, W + hi) * (scale * UP)
        back = total(2 * W + lo, 2 * W + hi)
        sigma = jax.nn.sigmoid(gate)
        hidden = (gate * sigma * upv).astype(bf16)
        d_hidden = logit * back
        d_gate = (d_hidden * upv * (sigma + gate * sigma * (1.0 - sigma))).astype(bf16)
        d_up = (d_hidden * gate * sigma).astype(bf16)
        router_grad += jnp.sum(hidden.astype(f32) * back, axis=1, keepdims=True)
        inner += jnp.sum(
            d_gate.astype(f32) * gate + d_up.astype(f32) * upv, axis=1, keepdims=True
        )
        for n in range(8):
            d_out[n, :, lo:hi] = d_gate
            d_out[n, :, W + lo : W + hi] = d_up
            h_out[n, :, lo:hi] = hidden
    extra = lanes_of(
        heads(scale, 3) + heads(logit, 3) + heads(router_grad, 3) + heads(inner, 3), rows
    )
    for n in range(8):
        d_out[n, :, 2 * W :] = extra


def with_small(rows, small):
    return jnp.concatenate([rows] + heads(small, 2), axis=0).astype(bf16)


def apart(ref):
    value = ref[...].astype(f32)
    n = value.shape[0] - 8
    return value[:n], value[n : n + 4] + value[n + 4 : n + 8]


def to_row(column):
    eye = lax.broadcasted_iota(i32, (SEL, SEL), 0) == lax.broadcasted_iota(i32, (SEL, SEL), 1)
    return jnp.sum(jnp.where(eye, column, 0.0), axis=0, keepdims=True)


def normed_kernel(spread, gd, wg, wu, sel, theirs, ours, small, cols):
    j = pl.program_id(0)

    @pl.when(j == 0)
    def _():
        tail = gd[:, 2 * W :].astype(f32)
        lane = lax.broadcasted_iota(i32, (SEL, 128), 1)

        def value(k):
            return jnp.sum(
                jnp.where((lane >= 3 * k) & (lane < 3 * k + 3), tail, 0.0), axis=1, keepdims=True
            )

        scale, router_grad, inner = value(0), value(2), value(3)
        cols[...] = jnp.where(lane == 0, scale, router_grad)
        small[...] = jnp.zeros(small.shape, f32)
        small[2:3, 0:SEL] = to_row(router_grad)
        small[2:3, SEL : 2 * SEL] = to_row(inner)
        small[3:4, 0:SEL] = to_row(scale)

    part = mm(gd[:, 0:W], wg[...], 1, 1) + mm(gd[:, W : 2 * W], wu[...], 1, 1)
    sel32 = sel[...].astype(f32)
    at = pl.ds(pl.multiple_of(j * TILE, TILE), TILE)
    small[0:1, at] = jnp.sum(part * sel32 * cols[:, 0:1], axis=0, keepdims=True)
    small[1:2, at] = jnp.sum(sel32 * cols[:, 1:2], axis=0, keepdims=True)
    rounded = part.astype(bf16)
    ours[...] = mm(spread[:SEL, :], rounded, 1, 0).astype(bf16)
    theirs[...] = with_small(mm(spread[SEL:, :], rounded, 1, 0), small[0:4, at])


def join_kernel(ours, theirs, mine, up3, down3, far, up1, down1, small):
    rows, other = apart(theirs)
    total = mine[0:4, :] + other
    small[...] = total
    for n, out in ((0, down3), (2, down1), (4, up1), (6, up3), (7, far)):
        at = slice(48 * n, 48 * n + 48)
        out[...] = with_small(ours[at, :].astype(f32) + rows[at], total)


def relay_kernel(
    up2, up2_other, from_below, down2, down2_other, from_above, far, small, to_up, to_down
):
    _, _, _, c = place_of()
    rows, one = apart(far)
    for base, other, ref, mask, out in (
        (up2, up2_other, from_below, c == 0, to_up),
        (down2, down2_other, from_above, c == 1, to_down),
    ):
        chunk, two = apart(ref)
        out[...] = with_small(
            base[...].astype(f32) + other[...].astype(f32) + chunk + jnp.where(mask, rows, 0.0),
            small[...] + two + jnp.where(mask, one, 0.0),
        )


def pair_kernel(stay, stay_other, small, a, b, c, d, here, there):
    total, low = stay[...].astype(f32) + stay_other[...].astype(f32), small[...]
    for part in (a, b, c, d):
        rows, other = apart(part)
        total, low = total + rows, low + other
    here[0:CAP, :] = total[:CAP]
    here[CAP : CAP + 4, :] = low
    there[...] = with_small(total[CAP:], low)


def far_kernel(below, above, _, out):
    out[...] = jnp.where(place_of()[3] == 0, below[...], above[...])


def final_kernel(here, there, mine, go, vectors, sel_row, small, grad_x, d_gain, d_router):
    pick, first, last = pick_of(sel_row[...])
    rows, summed = apart(there)
    own = here[0:CAP, :] + rows
    summed = summed + here[CAP : CAP + 4, :]
    d_gain[...] = summed[0:1]
    d_router[...] = summed[1:2]
    row = lax.broadcasted_iota(i32, (CAP, SEL), 1)
    k = lax.broadcasted_iota(i32, (CAP, SEL), 0)
    where = (row == first + k) & (row < last)

    def place(values):
        return jnp.sum(jnp.where(where, values, 0.0), axis=1, keepdims=True)

    scale = place(small[3:4, 0:SEL])
    router_grad = place(summed[2:3, 0:SEL])
    inner = place(summed[2:3, SEL : 2 * SEL])
    d_sel = (
        scale * vectors[0:1, :] * own
        - mine[0].astype(f32) * (scale * scale * inner / D)
        + router_grad * vectors[1:2, :]
    )
    spread = jnp.zeros((TOK, W), f32)
    for piece in heads(d_sel, 3):
        spread += mm(pick, piece.astype(bf16), 1, 0)
    grad_x[...] = (go[...].astype(f32) + spread).astype(bf16)


def gather(pair, after):
    held = {0: pair}
    for k in (2, 1):
        held[-k] = along(pair, k)
        held[k] = along(pair, -k)
    held[-3] = along(held[-2], 1)
    held[3] = along(held[2], -1)
    far = pl.pallas_call(
        far_kernel,
        out_shape=jax.ShapeDtypeStruct(pair.shape, bf16),
        in_specs=[VMEM] * 2 + [pl.BlockSpec(memory_space=pl.ANY)],
        out_specs=VMEM,
        compiler_params=params(16),
        name="far",
    )(held[-2], held[2], after)
    held[4] = lax.ppermute(far, "wide", ZFAR)
    ours = [held[k] for k in range(-3, 5)]
    return ours + [lax.ppermute(piece, "wide", CORE) for piece in ours]


def local(tokens, grad_out, selected, gain, router_weight, w_gate, w_up, w_down):
    sel_col = selected.reshape(SEL, 1)
    gain = gain.reshape(1, W)
    router_weight = router_weight.reshape(1, W)
    anywhere = pl.BlockSpec(memory_space=pl.ANY)
    mine, sel_row = pl.pallas_call(
        own_kernel,
        out_shape=(
            jax.ShapeDtypeStruct((2, CAP, W), bf16),
            jax.ShapeDtypeStruct((1, SEL), i32),
        ),
        in_specs=[anywhere] * 3,
        out_specs=(VMEM, VMEM),
        scratch_shapes=[pltpu.VMEM((SEL,), i32)]
        + [pltpu.VMEM((TOK, W), bf16)] * 2
        + [pltpu.SemaphoreType.DMA((3,))],
        compiler_params=params(60),
        name="own",
    )(selected, tokens, grad_out)
    put, spread, vectors = pl.pallas_call(
        onehot_kernel,
        out_shape=(
            jax.ShapeDtypeStruct((SEL, 2 * SEL), bf16),
            jax.ShapeDtypeStruct((2 * SEL, SEL), bf16),
            jax.ShapeDtypeStruct((2, W), f32),
        ),
        in_specs=[VMEM] * 3 + [pl.BlockSpec(memory_space=pl.ANY)],
        out_specs=(VMEM,) * 3,
        compiler_params=params(24),
        name="onehot",
    )(sel_col, gain, router_weight, mine)
    pair = pl.pallas_call(
        base_kernel,
        out_shape=jax.ShapeDtypeStruct((4 * CAP, W), bf16),
        in_specs=[VMEM] * 2,
        out_specs=VMEM,
        compiler_params=params(16),
        name="base",
    )(mine, lax.ppermute(mine, "wide", YLO))
    parts = gather(pair, put)

    full = lambda *shape: pl.BlockSpec(shape, lambda j: (0,) * len(shape))
    sel, gsel, send = pl.pallas_call(
        forward_kernel,
        grid=(W // TILE,),
        out_shape=(
            jax.ShapeDtypeStruct((SEL, W), bf16),
            jax.ShapeDtypeStruct((SEL, W), bf16),
            jax.ShapeDtypeStruct((SEL, 3 * W + 128), bf16),
        ),
        in_specs=[full(96, W)] * 16
        + [full(SEL, 768), full(2, W)]
        + [pl.BlockSpec((W, TILE), lambda j: (0, j))] * 2
        + [pl.BlockSpec((TILE, W), lambda j: (j, 0))],
        out_specs=(full(SEL, W), full(SEL, W), full(SEL, 3 * W + 128)),
        scratch_shapes=[pltpu.VMEM((768, 2 * W), bf16), pltpu.VMEM((SEL, W), bf16)],
        compiler_params=params(48),
        cost_estimate=cost(3.6e9, 16e6),
        name="forward",
    )(*parts, put, vectors, w_gate, w_up, w_down)
    got = lax.all_to_all(send.reshape(8, SEL // 8, -1), "narrow", 0, 0, tiled=True)

    share_d, share_h = pl.pallas_call(
        hidden_kernel,
        out_shape=(
            jax.ShapeDtypeStruct((8, SEL // 8, 2 * W + 128), bf16),
            jax.ShapeDtypeStruct((8, SEL // 8, W), bf16),
        ),
        in_specs=[VMEM],
        out_specs=(VMEM, VMEM),
        compiler_params=params(),
        name="hidden",
    )(got)
    gd = lax.all_to_all(share_d, "narrow", 0, 0, tiled=True).reshape(SEL, -1)
    gd, share_h = lax.optimization_barrier((gd, share_h))
    hidden = lax.all_to_all(share_h, "narrow", 0, 0, tiled=True).reshape(SEL, W)

    theirs, ours, small = pl.pallas_call(
        normed_kernel,
        grid=(W // TILE,),
        out_shape=(
            jax.ShapeDtypeStruct((SEL + 8, W), bf16),
            jax.ShapeDtypeStruct((SEL, W), bf16),
            jax.ShapeDtypeStruct((8, W), f32),
        ),
        in_specs=[full(768, SEL), full(SEL, 2 * W + 128)]
        + [pl.BlockSpec((TILE, W), lambda j: (j, 0))] * 2
        + [pl.BlockSpec((SEL, TILE), lambda j: (0, j))],
        out_specs=(
            pl.BlockSpec((SEL + 8, TILE), lambda j: (0, j)),
            pl.BlockSpec((SEL, TILE), lambda j: (0, j)),
            full(8, W),
        ),
        scratch_shapes=[pltpu.VMEM((SEL, 128), f32)],
        compiler_params=params(),
        cost_estimate=cost(2.4e9, 9e6),
        name="normed",
    )(spread, gd, w_gate, w_up, sel)

    part = jax.ShapeDtypeStruct((56, W), bf16)
    theirs = lax.ppermute(theirs, "wide", CORE)
    up3, down3, far, up1, down1, total = pl.pallas_call(
        join_kernel,
        out_shape=(part,) * 5 + (jax.ShapeDtypeStruct((4, W), f32),),
        in_specs=[VMEM] * 3,
        out_specs=(VMEM,) * 6,
        compiler_params=params(16),
        name="join",
    )(ours, theirs, small)
    from_below, from_above = along(up3, 1), along(down3, -1)
    far = lax.ppermute(far, "wide", ZFAR)
    near = along(up1, 1), along(down1, -1)

    def chunk(n):
        return pl.BlockSpec((48, W), lambda j: (n, 0))

    up2, down2 = pl.pallas_call(
        relay_kernel,
        grid=(1,),
        out_shape=(part, part),
        in_specs=[chunk(5), chunk(5), full(56, W), chunk(1), chunk(1)]
        + [full(56, W), full(56, W), full(4, W)],
        out_specs=(full(56, W), full(56, W)),
        compiler_params=params(16),
        name="relay",
    )(ours, theirs, from_below, ours, theirs, from_above, far, total)
    here, there = pl.pallas_call(
        pair_kernel,
        grid=(1,),
        out_shape=(
            jax.ShapeDtypeStruct((CAP + 4, W), f32),
            jax.ShapeDtypeStruct((CAP + 8, W), bf16),
        ),
        in_specs=[chunk(3), chunk(3), full(4, W)] + [full(56, W)] * 4,
        out_specs=(full(CAP + 4, W), full(CAP + 8, W)),
        compiler_params=params(16),
        name="pair",
    )(ours, theirs, total, *near, along(up2, 2), along(down2, -2))
    there = lax.ppermute(there, "wide", YLO)

    tail = gd[:, 2 * W :].astype(f32)
    scale = jnp.sum(tail[:, 0:3], axis=1, keepdims=True)
    logit = jnp.sum(tail[:, 3:6], axis=1, keepdims=True)
    normed = (sel.astype(f32) * scale * gain).astype(bf16)
    d_out = (logit * gsel.astype(f32)).astype(bf16)
    grad_gate = mm(normed, gd[:, :W], 0, 0).astype(bf16)
    grad_up = mm(normed, gd[:, W : 2 * W], 0, 0).astype(bf16)
    grad_down = mm(hidden, d_out, 0, 0).astype(bf16)

    vector = jax.ShapeDtypeStruct((1, W), f32)
    grad_x, d_gain, d_router = pl.pallas_call(
        final_kernel,
        out_shape=(jax.ShapeDtypeStruct((TOK, W), bf16), vector, vector),
        in_specs=[VMEM] * 7,
        out_specs=(VMEM,) * 3,
        compiler_params=params(16),
        name="final",
    )(here, there, mine, grad_out, vectors, sel_row, small)
    return (grad_x, grad_gate, grad_up, grad_down, d_gain.reshape(W), d_router.reshape(W))


def solution(mesh):
    return jax.shard_map(
        local,
        mesh=mesh,
        in_specs=(
            P("wide", "narrow"),
            P("wide", "narrow"),
            P(),
            P("narrow"),
            P("narrow"),
            P("narrow", "wide"),
            P("narrow", "wide"),
            P("wide", "narrow"),
        ),
        out_specs=(
            P("wide", "narrow"),
            P("narrow", "wide"),
            P("narrow", "wide"),
            P("wide", "narrow"),
            P("narrow"),
            P("narrow"),
        ),
        check_vma=False,
    )
```

time: 186 us -> 154 us (0.83)
  waiting for transfers between devices: 32.5 us -> 18.5 us
  starting transfers between devices: 48.8 us -> 38.7 us
  blocking collectives: 67.6 us -> 62.1 us
  other arithmetic: 2.73 us -> 0.28 us
    all_to_all x1 -> x0, waiting for transfers between devices: 8.4 us -> none  [local(): lax.all_to_all(message, 'wide', 0, 0, tiled=True, axis_index_groups=ZGROUPS)]
    all_to_all x2 -> x1, blocking collectives: 42.8 us -> 35.7 us  [local(): lax.all_to_all(send.reshape(8, SEL // 8, -1), 'narrow', 0, 0, tiled=True)]
    all_to_all x1 -> x0, starting transfers between devices: 6.82 us -> none  [local(): lax.all_to_all(message, 'wide', 0, 0, tiled=True, axis_index_groups=ZGROUPS)]
    ppermute x20 -> x17, waiting for transfers between devices: 23.9 us -> 17.3 us  [the longest x12 12.3 us: along(): lax.ppermute(value, 'wide', wide_pairs(lambda z, y, c: (z + 8 + step, y,...]
    pallas_call x3 -> x8, Pallas kernels: 8.92 us -> 11.5 us  [the longest x1 8.43 us: local(): pl.pallas_call(forward_kernel, grid=(W // TILE,), out_shape=(jax.ShapeDty...]
    ppermute x16 -> x8, starting transfers between devices: 3.63 us -> 1.3 us  [gather(): return ours + [lax.ppermute(piece, 'wide', CORE) for piece in ours]]
    ppermute x20 -> x17, starting transfers between devices: 30 us -> 29 us  [the longest x12 24 us: along(): lax.ppermute(value, 'wide', wide_pairs(lambda z, y, c: (z + 8 + step, y,...]
  transfers between devices with their start and end apart: 38 -> 26, of which waited for: 9 -> 11; matrix products, arithmetic and copies ran while one was open for 7% -> 7% of each run, Pallas kernels for 3% -> 1%
where the time goes in v3:
time: 154 us
  blocking collectives  62.1 us (40%)
  starting transfers between devices  38.7 us (25%)
  Pallas kernels  19.8 us (13%)
  waiting for transfers between devices  18.5 us (12%)
  matrix products  9.26 us (6%)
  local copies, waits for them, and re-layouts  3.99 us (3%)
    all_to_all x1, blocking collectives, local(): lax.all_to_all(send.reshape(8, SEL // 8, -1), 'narrow', 0, 0, tiled=True)  35.7 us
    all_to_all x1, blocking collectives, local(): gd = lax.all_to_all(share_d, 'narrow', 0, 0, tiled=True).reshape(SEL, -1)  26.5 us
    ppermute x12, starting transfers between devices, along(): lax.ppermute(value, 'wide', wide_pairs(lambda z, y, c: (z + 8 + step, y,...  24 us
    ppermute x12, waiting for transfers between devices, along(): lax.ppermute(value, 'wide', wide_pairs(lambda z, y, c: (z + 8 + step, y,...  12.3 us
    dot_general x3, matrix products, mm(): lax.dot_general(a, b, (((ca,), (cb,)), ((), ())), preferred_element_type=...  9.26 us
    all_to_all x1, starting transfers between devices, local(): hidden = lax.all_to_all(share_h, 'narrow', 0, 0, tiled=True).reshape(SEL, W)  8.48 us
    pallas_call x1, Pallas kernels, local(): pl.pallas_call(forward_kernel, grid=(W // TILE,), out_shape=(jax.ShapeDty...  8.43 us
    pallas_call x1, Pallas kernels, local(): pl.pallas_call(normed_kernel, grid=(W // TILE,), out_shape=(jax.ShapeDtyp...  6.33 us
  transfers between devices with their start and end apart: 26, of which 11 were waited for; matrix products, arithmetic and copies ran while one was open for 7% of the time, Pallas kernels for 1%

profile of v3, /device:TPU:22, one launch (start us, length us, event | category | flops | bytes accessed | tf_op | source)
XLA Modules:
  0.0 153.6 jit_solution(7130349617205572579)
XLA Ops:
  0.6 2.0 %own.1 = (bf16[2,24,1024]{2,1,0:T(8,128)(2,1)}, s32[1,384]{1,0:T(1,128)}) custom-call(s32[384]{0:T(512)} %sel_hbm.1, bf16[96,1024]{1,0:T(8,128)(2,1)} %tok_hbm.1, bf16[96,1024]{1,0:T(8,128)(2,1)} %go.1), custom_call_target="tpu_custom_call" | custom-call | tf_op jit(solution)/shard_map/own/pallas_call | solution.py:343
  4.0 3.5 %collective-permute-done.other = bf16[2,24,1024]{2,1,0:T(8,128)(2,1)S(1)} collective-permute-done((bf16[2,24,1024]{2,1,0:T(8,128)(2,1)}, bf16[2,24,1024]{2,1,0:T(8,128)(2,1)S(1)}, u32[]{:S(2)}, u32[]{:S(2)}) %collective-permute-start) | collective-permute-done | bytes 98336 | tf_op jit(solution)/shard_map/ppermute | solution.py:376
  8.5 3.4 %collective-permute-start.1 = (bf16[96,1024]{1,0:T(8,128)(2,1)S(1)}, bf16[96,1024]{1,0:T(8,128)(2,1)S(1)}, u32[]{:S(2)}, u32[]{:S(2)}) collective-permute-start(bf16[96,1024]{1,0:T(8,128)(2,1)S(1)} %base.1.refs_3_), channel_id=1, source_target_pairs={{0,64},{8,72},{16,80},{24,88},{32,96},{40,104},{48,112},{56,120},{... | collective-permute-start | bytes 589832 | tf_op jit(solution)/shard_map/ppermute | solution.py:36
  11.8 3.1 %collective-permute-start.5 = (bf16[96,1024]{1,0:T(8,128)(2,1)S(1)}, bf16[96,1024]{1,0:T(8,128)(2,1)S(1)}, u32[]{:S(2)}, u32[]{:S(2)}) collective-permute-start(bf16[96,1024]{1,0:T(8,128)(2,1)S(1)} %base.1.refs_3_), channel_id=1, source_target_pairs={{0,192},{8,200},{16,208},{24,216},{32,224},{40,232},{48,240},{56,2... | collective-permute-start | bytes 589832 | tf_op jit(solution)/shard_map/ppermute | solution.py:36
  16.0 2.2 %collective-permute-start.4 = (bf16[96,1024]{1,0:T(8,128)(2,1)S(1)}, bf16[96,1024]{1,0:T(8,128)(2,1)S(1)}, u32[]{:S(2)}, u32[]{:S(2)}) collective-permute-start(bf16[96,1024]{1,0:T(8,128)(2,1)S(1)} %base.1.refs_3_), channel_id=1, source_target_pairs={{0,224},{8,232},{16,240},{24,248},{32,0},{40,8},{48,16},{56,24},{6... | collective-permute-start | bytes 589832 | tf_op jit(solution)/shard_map/ppermute | solution.py:36
  21.9 2.7 %collective-permute-done.1.below.refs_1_ = bf16[96,1024]{1,0:T(8,128)(2,1)S(1)} collective-permute-done((bf16[96,1024]{1,0:T(8,128)(2,1)S(1)}, bf16[96,1024]{1,0:T(8,128)(2,1)S(1)}, u32[]{:S(2)}, u32[]{:S(2)}) %collective-permute-start.1) | collective-permute-done | bytes 196640 | tf_op jit(solution)/shard_map/ppermute | solution.py:36
  24.6 3.5 %collective-permute-start.6 = (bf16[96,1024]{1,0:T(8,128)(2,1)S(1)}, bf16[96,1024]{1,0:T(8,128)(2,1)S(1)}, u32[]{:S(2)}, u32[]{:S(2)}) collective-permute-start(bf16[96,1024]{1,0:T(8,128)(2,1)S(1)} %collective-permute-done.5.above.refs_5_), channel_id=1, source_target_pairs={{0,224},{8,232},{16,240},{24,248},{32,0},{40,8},{48,16},{56,24},{6... | collective-permute-start | bytes 589832 | tf_op jit(solution)/shard_map/ppermute | solution.py:36
  31.5 4.2 %collective-permute-done.6.refs_6_ = bf16[96,1024]{1,0:T(8,128)(2,1)S(1)} collective-permute-done((bf16[96,1024]{1,0:T(8,128)(2,1)S(1)}, bf16[96,1024]{1,0:T(8,128)(2,1)S(1)}, u32[]{:S(2)}, u32[]{:S(2)}) %collective-permute-start.6) | collective-permute-done | bytes 196640 | tf_op jit(solution)/shard_map/ppermute | solution.py:36
  35.7 1.4 collective-permute-done.7.refs_7_
  39.1 8.4 %forward.1 = (bf16[384,1024]{1,0:T(8,128)(2,1)S(1)}, bf16[384,1024]{1,0:T(8,128)(2,1)S(1)}, bf16[384,3200]{1,0:T(8,128)(2,1)}) custom-call(bf16[96,1024]{1,0:T(8,128)(2,1)S(1)} %collective-permute-done.2.refs_0_, bf16[96,1024]{1,0:T(8,128)(2,1)S(1)} %collective-permute-done.1.below.refs_1_, bf16[96,1024]{1,0:T(8,128)(2,1)S(1)} %collective-permute-done.3.refs_2_, ...), custom_call_target="tpu_custom_call" | custom-call | flops 3600000000 | bytes 16000000 | tf_op jit(solution)/shard_map/forward/pallas_call | solution.py:380
  47.6 35.7 %all_to_all.15.got = bf16[8,48,3200]{2,1,0:T(8,128)(2,1)S(1)} all-to-all(bf16[8,48,3200]{2,1,0:T(8,128)(2,1)} %bitcast.14), channel_id=1, replica_groups=mesh['wide'=32,'narrow'=8] {'narrow'}, dimensions={0} | all-to-all | bytes 4915200 | tf_op jit(solution)/shard_map/all_to_all | solution.py:398
  84.0 26.5 %all_to_all.16 = bf16[8,48,2176]{2,1,0:T(8,128)(2,1)S(1)} all-to-all(bf16[8,48,2176]{2,1,0:T(8,128)(2,1)S(1)} %get-tuple-element.39), channel_id=1, replica_groups=mesh['wide'=32,'narrow'=8] {'narrow'}, dimensions={0} | all-to-all | bytes 3342336 | tf_op jit(solution)/shard_map/all_to_all | solution.py:411
  110.5 6.3 %normed.1 = (bf16[392,1024]{1,0:T(8,128)(2,1)}, bf16[384,1024]{1,0:T(8,128)(2,1)S(1)}, f32[8,1024]{1,0:T(8,128)S(1)}) custom-call(bf16[768,384]{1,0:T(8,128)(2,1)S(1)} %get-tuple-element.35.spread, bf16[384,2176]{1,0:T(8,128)(2,1)S(1)} %bitcast.8, bf16[1024,1024]{1,0:T(8,128)(2,1)S(1)} %copy-done.9, bf16[1024,1024]{1,0:T(8,128)(2,1)S(1)} %copy-done.10, ...), custom_call_target="tpu_custom_call" | custom-call | flops 2400000000 | bytes 9000000 | tf_op jit(solution)/shard_map/normed/pallas_call | solution.py:415
  116.9 8.5 %all-to-all-start.2 = ((bf16[8,48,1024]{2,1,0:T(8,128)(2,1)}), bf16[8,48,1024]{2,1,0:T(8,128)(2,1)}, u32[]{:S(2)}, u32[]{:S(2)}) async-start(bf16[8,48,1024]{2,1,0:T(8,128)(2,1)} %copy-done.4), calls=%async_computation.2 | async-start | bytes 1572864 | tf_op jit(solution)/shard_map/all_to_all | solution.py:413
  126.2 2.9 %collective-permute-start.20 = (bf16[56,1024]{1,0:T(8,128)(2,1)S(1)}, bf16[56,1024]{1,0:T(8,128)(2,1)S(1)}, u32[]{:S(2)}, u32[]{:S(2)}) collective-permute-start(bf16[56,1024]{1,0:T(8,128)(2,1)S(1)} %get-tuple-element.50), channel_id=1, source_target_pairs={{0,224},{8,232},{16,240},{24,248},{32,0},{40,8},{48,16},{56,24},{6... | collective-permute-start | bytes 344072 | tf_op jit(solution)/shard_map/ppermute | solution.py:36
  130.2 2.7 %convolution_convert_fusion.2 = bf16[1024,1024]{1,0:T(8,128)(2,1)} fusion(bf16[384,2176]{1,0:T(8,128)(2,1)S(1)} %bitcast.10, bf16[384,1024]{1,0:T(8,128)(2,1)S(1)} %copy-done.14, f32[1024]{0:T(1024)S(1)} %copy-done.7, f32[384]{0:T(512)S(1)} %get-tuple-element.63), kind=kOutput, calls=%fused_computation.2 | convolution fusion | flops 807927808 | bytes 3676160 | tf_op jit(solution)/shard_map/dot_general | solution.py:68
  132.9 1.9 %collective-permute-start.17 = (bf16[56,1024]{1,0:T(8,128)(2,1)S(1)}, bf16[56,1024]{1,0:T(8,128)(2,1)S(1)}, u32[]{:S(2)}, u32[]{:S(2)}) collective-permute-start(bf16[56,1024]{1,0:T(8,128)(2,1)S(1)} %get-tuple-element.47), channel_id=1, source_target_pairs={{0,32},{8,40},{16,48},{24,56},{32,64},{40,72},{48,80},{56,88},{64,... | collective-permute-start | bytes 344072 | tf_op jit(solution)/shard_map/ppermute | solution.py:36
  134.8 1.4 collective-permute-start.18
  136.3 3.0 %collective-permute-start.22 = (bf16[56,1024]{1,0:T(8,128)(2,1)S(1)}, bf16[56,1024]{1,0:T(8,128)(2,1)S(1)}, u32[]{:S(2)}, u32[]{:S(2)}) collective-permute-start(bf16[56,1024]{1,0:T(8,128)(2,1)S(1)} %get-tuple-element.52), channel_id=1, source_target_pairs={{0,64},{8,72},{16,80},{24,88},{32,96},{40,104},{48,112},{56,120},{... | collective-permute-start | bytes 344072 | tf_op jit(solution)/shard_map/ppermute | solution.py:36
  140.6 2.7 %convolution_convert_fusion.1 = bf16[1024,1024]{1,0:T(8,128)(2,1)} fusion(bf16[384,2176]{1,0:T(8,128)(2,1)S(1)} %bitcast.11, bf16[384,1024]{1,0:T(8,128)(2,1)S(1)} %copy-done.14, f32[1024]{0:T(1024)S(1)} %copy-done.7, f32[384]{0:T(512)S(1)} %get-tuple-element.63), kind=kOutput, calls=%fused_computation.1 | convolution fusion | flops 807927808 | bytes 3676160 | tf_op jit(solution)/shard_map/dot_general | solution.py:68
  143.3 2.1 %collective-permute-done.22.c = bf16[56,1024]{1,0:T(8,128)(2,1)S(1)} collective-permute-done((bf16[56,1024]{1,0:T(8,128)(2,1)S(1)}, bf16[56,1024]{1,0:T(8,128)(2,1)S(1)}, u32[]{:S(2)}, u32[]{:S(2)}) %collective-permute-start.22) | collective-permute-done | bytes 114720 | tf_op jit(solution)/shard_map/ppermute | solution.py:36
  145.4 1.6 %collective-permute-done.23.d = bf16[56,1024]{1,0:T(8,128)(2,1)S(1)} collective-permute-done((bf16[56,1024]{1,0:T(8,128)(2,1)S(1)}, bf16[56,1024]{1,0:T(8,128)(2,1)S(1)}, u32[]{:S(2)}, u32[]{:S(2)}) %collective-permute-start.23) | collective-permute-done | bytes 114720 | tf_op jit(solution)/shard_map/ppermute | solution.py:36
  147.1 1.4 collective-permute-start.24
  148.5 3.8 %convolution_convert_fusion = bf16[1024,1024]{1,0:T(8,128)(2,1)} fusion(bf16[384,1024]{1,0:T(8,128)(2,1)} %bitcast.4, bf16[384,1024]{1,0:T(8,128)(2,1)S(1)} %copy-done.12, f32[384]{0:T(512)S(1)} %get-tuple-element.62), kind=kOutput, calls=%fused_computation | convolution fusion | flops 807534592 | bytes 3671552 | tf_op jit(solution)/shard_map/dot_general | solution.py:68
  (77 shorter events, 17.8 us)
Async XLA Ops:
  2.7 4.9 %collective-permute-start = (bf16[2,24,1024]{2,1,0:T(8,128)(2,1)}, bf16[2,24,1024]{2,1,0:T(8,128)(2,1)S(1)}, u32[]{:S(2)}, u32[]{:S(2)}) collective-permute-start(bf16[2,24,1024]{2,1,0:T(8,128)(2,1)} %get-tuple-element.34._.mine), channel_id=1, source_target_pairs={{0,16},{8,24},{16,0},{24,8},{32,48},{40,56},{48,32},{56,40},{64,80... | collective-permute-start | bytes 294920 | tf_op jit(solution)/shard_map/ppermute | solution.py:376
  8.5 16.1 %collective-permute-start.1 = (bf16[96,1024]{1,0:T(8,128)(2,1)S(1)}, bf16[96,1024]{1,0:T(8,128)(2,1)S(1)}, u32[]{:S(2)}, u32[]{:S(2)}) collective-permute-start(bf16[96,1024]{1,0:T(8,128)(2,1)S(1)} %base.1.refs_3_), channel_id=1, source_target_pairs={{0,64},{8,72},{16,80},{24,88},{32,96},{40,104},{48,112},{56,120},{... | collective-permute-start | bytes 589832 | tf_op jit(solution)/shard_map/ppermute | solution.py:36
  11.8 12.7 %collective-permute-start.5 = (bf16[96,1024]{1,0:T(8,128)(2,1)S(1)}, bf16[96,1024]{1,0:T(8,128)(2,1)S(1)}, u32[]{:S(2)}, u32[]{:S(2)}) collective-permute-start(bf16[96,1024]{1,0:T(8,128)(2,1)S(1)} %base.1.refs_3_), channel_id=1, source_target_pairs={{0,192},{8,200},{16,208},{24,216},{32,224},{40,232},{48,240},{56,2... | collective-permute-start | bytes 589832 | tf_op jit(solution)/shard_map/ppermute | solution.py:36
  15.0 13.2 %collective-permute-start.3 = (bf16[96,1024]{1,0:T(8,128)(2,1)S(1)}, bf16[96,1024]{1,0:T(8,128)(2,1)S(1)}, u32[]{:S(2)}, u32[]{:S(2)}) collective-permute-start(bf16[96,1024]{1,0:T(8,128)(2,1)S(1)} %base.1.refs_3_), channel_id=1, source_target_pairs={{0,32},{8,40},{16,48},{24,56},{32,64},{40,72},{48,80},{56,88},{64,... | collective-permute-start | bytes 589832 | tf_op jit(solution)/shard_map/ppermute | solution.py:36
  16.0 13.7 %collective-permute-start.4 = (bf16[96,1024]{1,0:T(8,128)(2,1)S(1)}, bf16[96,1024]{1,0:T(8,128)(2,1)S(1)}, u32[]{:S(2)}, u32[]{:S(2)}) collective-permute-start(bf16[96,1024]{1,0:T(8,128)(2,1)S(1)} %base.1.refs_3_), channel_id=1, source_target_pairs={{0,224},{8,232},{16,240},{24,248},{32,0},{40,8},{48,16},{56,24},{6... | collective-permute-start | bytes 589832 | tf_op jit(solution)/shard_map/ppermute | solution.py:36
  18.2 11.5 %collective-permute-start.11 = (bf16[96,1024]{1,0:T(8,128)(2,1)S(1)}, bf16[96,1024]{1,0:T(8,128)(2,1)S(1)}, u32[]{:S(2)}, u32[]{:S(2)}) collective-permute-start(bf16[96,1024]{1,0:T(8,128)(2,1)S(1)} %base.1.refs_3_), channel_id=1, source_target_pairs={{0,8},{8,0},{16,24},{24,16},{32,40},{40,32},{48,56},{56,48},{64,72... | collective-permute-start | bytes 589832 | tf_op jit(solution)/shard_map/ppermute | solution.py:335
  24.6 6.9 %collective-permute-start.2 = (bf16[96,1024]{1,0:T(8,128)(2,1)S(1)}, bf16[96,1024]{1,0:T(8,128)(2,1)S(1)}, u32[]{:S(2)}, u32[]{:S(2)}) collective-permute-start(bf16[96,1024]{1,0:T(8,128)(2,1)S(1)} %collective-permute-done.1.below.refs_1_), channel_id=1, source_target_pairs={{0,32},{8,40},{16,48},{24,56},{32,64},{40,72},{48,80},{56,88},{64,... | collective-permute-start | bytes 589832 | tf_op jit(solution)/shard_map/ppermute | solution.py:36
  24.6 11.1 %collective-permute-start.6 = (bf16[96,1024]{1,0:T(8,128)(2,1)S(1)}, bf16[96,1024]{1,0:T(8,128)(2,1)S(1)}, u32[]{:S(2)}, u32[]{:S(2)}) collective-permute-start(bf16[96,1024]{1,0:T(8,128)(2,1)S(1)} %collective-permute-done.5.above.refs_5_), channel_id=1, source_target_pairs={{0,224},{8,232},{16,240},{24,248},{32,0},{40,8},{48,16},{56,24},{6... | collective-permute-start | bytes 589832 | tf_op jit(solution)/shard_map/ppermute | solution.py:36
  28.2 9.0 %collective-permute-start.7 = (bf16[96,1024]{1,0:T(8,128)(2,1)S(1)}, bf16[96,1024]{1,0:T(8,128)(2,1)S(1)}, u32[]{:S(2)}, u32[]{:S(2)}) collective-permute-start(bf16[96,1024]{1,0:T(8,128)(2,1)S(1)} %far.1), channel_id=1, source_target_pairs={{0,64},{8,200},{16,80},{24,216},{32,96},{40,232},{48,112},{56,248}... | collective-permute-start | bytes 589832 | tf_op jit(solution)/shard_map/ppermute | solution.py:333
  29.7 7.5 %collective-permute-start.9 = (bf16[96,1024]{1,0:T(8,128)(2,1)S(1)}, bf16[96,1024]{1,0:T(8,128)(2,1)S(1)}, u32[]{:S(2)}, u32[]{:S(2)}) collective-permute-start(bf16[96,1024]{1,0:T(8,128)(2,1)S(1)} %collective-permute-done.1.below.refs_1_), channel_id=1, source_target_pairs={{0,8},{8,0},{16,24},{24,16},{32,40},{40,32},{48,56},{56,48},{64,72... | collective-permute-start | bytes 589832 | tf_op jit(solution)/shard_map/ppermute | solution.py:335
  29.7 8.0 %collective-permute-start.10 = (bf16[96,1024]{1,0:T(8,128)(2,1)S(1)}, bf16[96,1024]{1,0:T(8,128)(2,1)S(1)}, u32[]{:S(2)}, u32[]{:S(2)}) collective-permute-start(bf16[96,1024]{1,0:T(8,128)(2,1)S(1)} %collective-permute-done.3.refs_2_), channel_id=1, source_target_pairs={{0,8},{8,0},{16,24},{24,16},{32,40},{40,32},{48,56},{56,48},{64,72... | collective-permute-start | bytes 589832 | tf_op jit(solution)/shard_map/ppermute | solution.py:335
  31.5 6.4 %collective-permute-start.13 = (bf16[96,1024]{1,0:T(8,128)(2,1)S(1)}, bf16[96,1024]{1,0:T(8,128)(2,1)S(1)}, u32[]{:S(2)}, u32[]{:S(2)}) collective-permute-start(bf16[96,1024]{1,0:T(8,128)(2,1)S(1)} %collective-permute-done.5.above.refs_5_), channel_id=1, source_target_pairs={{0,8},{8,0},{16,24},{24,16},{32,40},{40,32},{48,56},{56,48},{64,72... | collective-permute-start | bytes 589832 | tf_op jit(solution)/shard_map/ppermute | solution.py:335
  35.7 2.2 %collective-permute-start.12 = (bf16[96,1024]{1,0:T(8,128)(2,1)S(1)}, bf16[96,1024]{1,0:T(8,128)(2,1)S(1)}, u32[]{:S(2)}, u32[]{:S(2)}) collective-permute-start(bf16[96,1024]{1,0:T(8,128)(2,1)S(1)} %collective-permute-done.4.refs_4_), channel_id=1, source_target_pairs={{0,8},{8,0},{16,24},{24,16},{32,40},{40,32},{48,56},{56,48},{64,72... | collective-permute-start | bytes 589832 | tf_op jit(solution)/shard_map/ppermute | solution.py:335
  37.1 1.7 %collective-permute-start.14 = (bf16[96,1024]{1,0:T(8,128)(2,1)S(1)}, bf16[96,1024]{1,0:T(8,128)(2,1)S(1)}, u32[]{:S(2)}, u32[]{:S(2)}) collective-permute-start(bf16[96,1024]{1,0:T(8,128)(2,1)S(1)} %collective-permute-done.6.refs_6_), channel_id=1, source_target_pairs={{0,8},{8,0},{16,24},{24,16},{32,40},{40,32},{48,56},{56,48},{64,72... | collective-permute-start | bytes 589832 | tf_op jit(solution)/shard_map/ppermute | solution.py:335
  116.8 8.8 %collective-permute-start.16 = (bf16[392,1024]{1,0:T(8,128)(2,1)}, bf16[392,1024]{1,0:T(8,128)(2,1)S(1)}, u32[]{:S(2)}, u32[]{:S(2)}) collective-permute-start(bf16[392,1024]{1,0:T(8,128)(2,1)} %get-tuple-element.44), channel_id=1, source_target_pairs={{0,8},{8,0},{16,24},{24,16},{32,40},{40,32},{48,56},{56,48},{64,72... | collective-permute-start | bytes 2408456 | tf_op jit(solution)/shard_map/ppermute | solution.py:438
  116.9 31.6 %all-to-all-start.2 = ((bf16[8,48,1024]{2,1,0:T(8,128)(2,1)}), bf16[8,48,1024]{2,1,0:T(8,128)(2,1)}, u32[]{:S(2)}, u32[]{:S(2)}) async-start(bf16[8,48,1024]{2,1,0:T(8,128)(2,1)} %copy-done.4), calls=%async_computation.2 | async-start | bytes 1572864 | tf_op jit(solution)/shard_map/all_to_all | solution.py:413
  125.8 10.4 %collective-permute-start.19 = (bf16[56,1024]{1,0:T(8,128)(2,1)S(1)}, bf16[56,1024]{1,0:T(8,128)(2,1)S(1)}, u32[]{:S(2)}, u32[]{:S(2)}) collective-permute-start(bf16[56,1024]{1,0:T(8,128)(2,1)S(1)} %get-tuple-element.49), channel_id=1, source_target_pairs={{0,32},{8,40},{16,48},{24,56},{32,64},{40,72},{48,80},{56,88},{64,... | collective-permute-start | bytes 344072 | tf_op jit(solution)/shard_map/ppermute | solution.py:36
  126.2 10.0 %collective-permute-start.20 = (bf16[56,1024]{1,0:T(8,128)(2,1)S(1)}, bf16[56,1024]{1,0:T(8,128)(2,1)S(1)}, u32[]{:S(2)}, u32[]{:S(2)}) collective-permute-start(bf16[56,1024]{1,0:T(8,128)(2,1)S(1)} %get-tuple-element.50), channel_id=1, source_target_pairs={{0,224},{8,232},{16,240},{24,248},{32,0},{40,8},{48,16},{56,24},{6... | collective-permute-start | bytes 344072 | tf_op jit(solution)/shard_map/ppermute | solution.py:36
  129.1 7.1 %collective-permute-start.21 = (bf16[56,1024]{1,0:T(8,128)(2,1)S(1)}, bf16[56,1024]{1,0:T(8,128)(2,1)S(1)}, u32[]{:S(2)}, u32[]{:S(2)}) collective-permute-start(bf16[56,1024]{1,0:T(8,128)(2,1)S(1)} %get-tuple-element.51), channel_id=1, source_target_pairs={{0,64},{8,200},{16,80},{24,216},{32,96},{40,232},{48,112},{56,248}... | collective-permute-start | bytes 344072 | tf_op jit(solution)/shard_map/ppermute | solution.py:448
  132.9 10.3 %collective-permute-start.17 = (bf16[56,1024]{1,0:T(8,128)(2,1)S(1)}, bf16[56,1024]{1,0:T(8,128)(2,1)S(1)}, u32[]{:S(2)}, u32[]{:S(2)}) collective-permute-start(bf16[56,1024]{1,0:T(8,128)(2,1)S(1)} %get-tuple-element.47), channel_id=1, source_target_pairs={{0,32},{8,40},{16,48},{24,56},{32,64},{40,72},{48,80},{56,88},{64,... | collective-permute-start | bytes 344072 | tf_op jit(solution)/shard_map/ppermute | solution.py:36
  134.8 8.5 %collective-permute-start.18 = (bf16[56,1024]{1,0:T(8,128)(2,1)S(1)}, bf16[56,1024]{1,0:T(8,128)(2,1)S(1)}, u32[]{:S(2)}, u32[]{:S(2)}) collective-permute-start(bf16[56,1024]{1,0:T(8,128)(2,1)S(1)} %get-tuple-element.48), channel_id=1, source_target_pairs={{0,224},{8,232},{16,240},{24,248},{32,0},{40,8},{48,16},{56,24},{6... | collective-permute-start | bytes 344072 | tf_op jit(solution)/shard_map/ppermute | solution.py:36
  136.3 9.1 %collective-permute-start.22 = (bf16[56,1024]{1,0:T(8,128)(2,1)S(1)}, bf16[56,1024]{1,0:T(8,128)(2,1)S(1)}, u32[]{:S(2)}, u32[]{:S(2)}) collective-permute-start(bf16[56,1024]{1,0:T(8,128)(2,1)S(1)} %get-tuple-element.52), channel_id=1, source_target_pairs={{0,64},{8,72},{16,80},{24,88},{32,96},{40,104},{48,112},{56,120},{... | collective-permute-start | bytes 344072 | tf_op jit(solution)/shard_map/ppermute | solution.py:36
  139.3 7.7 %collective-permute-start.23 = (bf16[56,1024]{1,0:T(8,128)(2,1)S(1)}, bf16[56,1024]{1,0:T(8,128)(2,1)S(1)}, u32[]{:S(2)}, u32[]{:S(2)}) collective-permute-start(bf16[56,1024]{1,0:T(8,128)(2,1)S(1)} %get-tuple-element.53), channel_id=1, source_target_pairs={{0,192},{8,200},{16,208},{24,216},{32,224},{40,232},{48,240},{56,2... | collective-permute-start | bytes 344072 | tf_op jit(solution)/shard_map/ppermute | solution.py:36
  147.1 5.3 %collective-permute-start.24 = (bf16[32,1024]{1,0:T(8,128)(2,1)S(1)}, bf16[32,1024]{1,0:T(8,128)(2,1)S(1)}, u32[]{:S(2)}, u32[]{:S(2)}) collective-permute-start(bf16[32,1024]{1,0:T(8,128)(2,1)S(1)} %get-tuple-element.55), channel_id=1, source_target_pairs={{0,16},{8,24},{16,0},{24,8},{32,48},{40,56},{48,32},{56,40},{64,80... | collective-permute-start | bytes 196616 | tf_op jit(solution)/shard_map/ppermute | solution.py:476
  (17 other events, 220.1 us)

commit v4 on v3

--- a/solution.py
+++ b/solution.py
@@ -29,6 +29,11 @@
 
 CORE = wide_pairs(lambda z, y, c: (z, y, 1 - c))
 YLO = wide_pairs(lambda z, y, c: (z, 1 - y, c))
+XUP = [(n, n // 4 * 4 + (n + 1) % 4) for n in range(8)]
+XDOWN = [(n, n // 4 * 4 + (n + 3) % 4) for n in range(8)]
+XFAR = [(n, n // 4 * 4 + (n + 2) % 4) for n in range(8)]
+YHI = [(n, (n + 4) % 8) for n in range(8)]
+ROW = 3 * 1024 + 128
 ZFAR = wide_pairs(lambda z, y, c: (z + 2 + 4 * c, y, c))
 
 
@@ -75,6 +80,13 @@
 
 def count_before(sel_col, ids):
     return jnp.sum(jnp.where(sel_col < ids, 1, 0).astype(i32), axis=0, keepdims=True)
+
+
+def compact_of(i):
+    n = lax.axis_index("narrow")
+    r = (i * 1366) >> 16
+    block = (r & 4 ^ n & 4) | ((r + n) & 3)
+    return i + (block - r) * 48
 
 
 def placement(sel_col):
@@ -86,7 +98,7 @@
     block = zz * 4 + (y ^ (n & 1)) * 2 + (c ^ (n >> 4))
     start = count_before(sel_col, block * TOK)
     end = count_before(sel_col, block * TOK + TOK)
-    row = lax.broadcasted_iota(i32, (SEL, 2 * SEL), 0)
+    row = compact_of(lax.broadcasted_iota(i32, (SEL, 1), 0))
     return jnp.where((row == start + k) & (row < end), 1.0, 0.0)
 
 
@@ -119,12 +131,7 @@
     pick = pick_of(sel_row)[0]
     for n, held in enumerate((tok, go)):
         copies[n].wait()
-        out[n] = mm(pick, held[...], 0, 0).astype(bf16)
-
-
-def base_kernel(mine, other, out):
-    parts = [mine[0], other[0], mine[1], other[1]]
-    out[...] = jnp.concatenate([part.astype(f32) for part in parts], axis=0).astype(bf16)
+        out[:, n * W : n * W + W] = mm(pick, held[...], 0, 0).astype(bf16)
 
 
 def onehot_kernel(sel_col, gain, rw, _, put, spread, vectors):
@@ -137,52 +144,97 @@
 
 def forward_kernel(*refs):
     parts = refs[:16]
-    put, vectors, wg, wu, wd, sel, gsel, out, slots, scaled = refs[16:]
+    put, vectors, wg, wu, wd, sel, gsel, keep, to_up, to_down, to_y, slots, scaled = refs[16:]
     j = pl.program_id(0)
+
+    def write(cols, value):
+        value = value.astype(bf16)
+        for r, (out, at) in enumerate(
+            (
+                (keep, 0),
+                (to_up, 48),
+                (keep, 96),
+                (to_down, 48),
+                (keep, 48),
+                (to_up, 0),
+                (to_y, 0),
+                (to_down, 0),
+            )
+        ):
+            out[at : at + 48, cols] = value[48 * r : 48 * r + 48]
 
     @pl.when(j == 0)
     def _():
         for p in range(16):
-            slots[48 * p : 48 * p + 48, 0:W] = parts[p][0:48, :]
-            slots[48 * p : 48 * p + 48, W : 2 * W] = parts[p][48:96, :]
-        squares = jnp.zeros((SEL, 1), f32)
-        logit = jnp.zeros((SEL, 1), f32)
+            slots[48 * p : 48 * p + 48, :] = parts[p][...]
+        squares = jnp.zeros((SEL, 128), f32)
+        logit = jnp.zeros((SEL, 128), f32)
         for k in range(W // TILE):
             cols = slice(k * TILE, (k + 1) * TILE)
             tile = mm(put[...], slots[:, cols], 1, 0)
             sel[:, cols] = tile.astype(bf16)
-            squares += jnp.sum(tile * tile, axis=1, keepdims=True)
-            logit += jnp.sum(tile * vectors[1:2, cols], axis=1, keepdims=True)
+            for m in range(TILE // 128):
+                lanes = tile[:, 128 * m : 128 * m + 128]
+                squares += lanes * lanes
+                logit += lanes * vectors[1:2, k * TILE + 128 * m : k * TILE + 128 * m + 128]
             scaled[:, cols] = (tile * (vectors[0:1, cols] * DOWN)).astype(bf16)
             tile = mm(put[...], slots[:, W + k * TILE : W + (k + 1) * TILE], 1, 0)
             gsel[:, cols] = tile.astype(bf16)
-        out[:, 3 * W :] = lanes_of(heads(squares, 3) + heads(logit, 3), SEL)
+        squares = jnp.sum(squares, axis=1, keepdims=True)
+        logit = jnp.sum(logit, axis=1, keepdims=True)
+        write(slice(3 * W, ROW), lanes_of(heads(squares, 3) + heads(logit, 3), SEL))
 
     def at(start):
         return pl.ds(pl.multiple_of(start + j * TILE, TILE), TILE)
 
-    out[:, at(0)] = mm(scaled[...], wg[...], 1, 0).astype(bf16)
-    out[:, at(W)] = mm(scaled[...], wu[...], 1, 0).astype(bf16)
-    out[:, at(2 * W)] = mm(gsel[...], wd[...], 1, 1).astype(bf16)
-
-
-def hidden_kernel(got, d_out, h_out):
+    write(at(0), mm(scaled[...], wg[...], 1, 0))
+    write(at(W), mm(scaled[...], wu[...], 1, 0))
+    write(at(2 * W), mm(gsel[...], wd[...], 1, 1))
+
+
+def stats(refs):
+    tail = 0.0
+    for ref in refs:
+        tail = tail + ref[:, 3 * W :].astype(f32)
+    return (
+        tail[:, 0:1] + tail[:, 1:2] + tail[:, 2:3],
+        tail[:, 3:4] + tail[:, 4:5] + tail[:, 5:6],
+    )
+
+
+def sum_kernel(keep, from_below, from_above, from_y, to_y, to_far):
+    for out, refs in (
+        (to_y, (keep.at[48:96], from_below.at[0:48], from_above.at[0:48])),
+        (to_far, (keep.at[96:144], from_y)),
+    ):
+        for k in range(3 * W // TILE):
+            cols = slice(k * TILE, (k + 1) * TILE)
+            total = refs[0][:, cols].astype(f32)
+            for ref in refs[1:]:
+                total = total + ref[:, cols].astype(f32)
+            out[:, cols] = total.astype(bf16)
+        squares, logit = stats(refs)
+        out[:, 3 * W :] = lanes_of(heads(squares, 3) + heads(logit, 3), SEL // 8)
+
+
+def hidden_kernel(keep, from_below, from_above, from_y, from_far, out):
     rows = SEL // 8
-
-    def total(lo, hi):
-        return jnp.sum(got[:, :, lo:hi].astype(f32), axis=0)
-
-    tail = total(3 * W, 3 * W + 128)
-    squares = tail[:, 0:1] + tail[:, 1:2] + tail[:, 2:3]
-    logit = tail[:, 3:4] + tail[:, 4:5] + tail[:, 5:6]
+    refs = (keep.at[0:48], from_below.at[48:96], from_above.at[48:96], from_y, from_far)
+
+    def total(start):
+        value = refs[0][:, start : start + TILE].astype(f32)
+        for ref in refs[1:]:
+            value = value + ref[:, start : start + TILE].astype(f32)
+        return value
+
+    squares, logit = stats(refs)
     scale = lax.rsqrt(squares / D + EPS)
     router_grad = jnp.zeros((rows, 1), f32)
     inner = jnp.zeros((rows, 1), f32)
-    for k in range(W // TILE):
-        lo, hi = k * TILE, (k + 1) * TILE
-        gate = total(lo, hi) * (scale * UP)
-        upv = total(W + lo, W + hi) * (scale * UP)
-        back = total(2 * W + lo, 2 * W + hi)
+    for lo in range(0, W, TILE):
+        gate = total(lo) * (scale * UP)
+        upv = total(W + lo) * (scale * UP)
+        back = total(2 * W + lo)
         sigma = jax.nn.sigmoid(gate)
         hidden = (gate * sigma * upv).astype(bf16)
         d_hidden = logit * back
@@ -192,15 +244,12 @@
         inner += jnp.sum(
             d_gate.astype(f32) * gate + d_up.astype(f32) * upv, axis=1, keepdims=True
         )
-        for n in range(8):
-            d_out[n, :, lo:hi] = d_gate
-            d_out[n, :, W + lo : W + hi] = d_up
-            h_out[n, :, lo:hi] = hidden
-    extra = lanes_of(
+        out[:, lo : lo + TILE] = d_gate
+        out[:, W + lo : W + lo + TILE] = d_up
+        out[:, 2 * W + lo : 2 * W + lo + TILE] = hidden
+    out[:, 3 * W :] = lanes_of(
         heads(scale, 3) + heads(logit, 3) + heads(router_grad, 3) + heads(inner, 3), rows
     )
-    for n in range(8):
-        d_out[n, :, 2 * W :] = extra
 
 
 def with_small(rows, small):
@@ -218,12 +267,29 @@
     return jnp.sum(jnp.where(eye, column, 0.0), axis=0, keepdims=True)
 
 
-def normed_kernel(spread, gd, wg, wu, sel, theirs, ours, small, cols):
+def normed_kernel(
+    spread, own, above, b2, below, b4, b6, wg, wu, sel, theirs, ours, small, gd, cols
+):
     j = pl.program_id(0)
 
     @pl.when(j == 0)
     def _():
-        tail = gd[:, 2 * W :].astype(f32)
+        tail = []
+        for r, (ref, at) in enumerate(
+            (
+                (own, 0),
+                (above, 0),
+                (b2, 0),
+                (below, 0),
+                (b4, 0),
+                (above, 48),
+                (b6, 0),
+                (below, 48),
+            )
+        ):
+            gd[48 * r : 48 * r + 48, :] = ref[at : at + 48, 0 : 2 * W]
+            tail.append(ref[at : at + 48, 3 * W :].astype(f32))
+        tail = jnp.concatenate(tail, axis=0)
         lane = lax.broadcasted_iota(i32, (SEL, 128), 1)
 
         def value(k):
@@ -294,7 +360,7 @@
     summed = summed + here[CAP : CAP + 4, :]
     d_gain[...] = summed[0:1]
     d_router[...] = summed[1:2]
-    row = lax.broadcasted_iota(i32, (CAP, SEL), 1)
+    row = compact_of(lax.broadcasted_iota(i32, (1, SEL), 1))
     k = lax.broadcasted_iota(i32, (CAP, SEL), 0)
     where = (row == first + k) & (row < last)
 
@@ -306,7 +372,7 @@
     inner = place(summed[2:3, SEL : 2 * SEL])
     d_sel = (
         scale * vectors[0:1, :] * own
-        - mine[0].astype(f32) * (scale * scale * inner / D)
+        - mine[:, 0:W].astype(f32) * (scale * scale * inner / D)
         + router_grad * vectors[1:2, :]
     )
     spread = jnp.zeros((TOK, W), f32)
@@ -343,7 +409,7 @@
     mine, sel_row = pl.pallas_call(
         own_kernel,
         out_shape=(
-            jax.ShapeDtypeStruct((2, CAP, W), bf16),
+            jax.ShapeDtypeStruct((CAP, 2 * W), bf16),
             jax.ShapeDtypeStruct((1, SEL), i32),
         ),
         in_specs=[anywhere] * 3,
@@ -366,51 +432,63 @@
         compiler_params=params(24),
         name="onehot",
     )(sel_col, gain, router_weight, mine)
-    pair = pl.pallas_call(
-        base_kernel,
-        out_shape=jax.ShapeDtypeStruct((4 * CAP, W), bf16),
-        in_specs=[VMEM] * 2,
-        out_specs=VMEM,
-        compiler_params=params(16),
-        name="base",
-    )(mine, lax.ppermute(mine, "wide", YLO))
+    pair = jnp.concatenate([mine, lax.ppermute(mine, "wide", YLO)], axis=0)
     parts = gather(pair, put)
 
     full = lambda *shape: pl.BlockSpec(shape, lambda j: (0,) * len(shape))
-    sel, gsel, send = pl.pallas_call(
+    block = jax.ShapeDtypeStruct((48, ROW), bf16)
+    blocks = jax.ShapeDtypeStruct((96, ROW), bf16)
+    sel, gsel, keep, to_up, to_down, to_y = pl.pallas_call(
         forward_kernel,
         grid=(W // TILE,),
         out_shape=(
             jax.ShapeDtypeStruct((SEL, W), bf16),
             jax.ShapeDtypeStruct((SEL, W), bf16),
-            jax.ShapeDtypeStruct((SEL, 3 * W + 128), bf16),
-        ),
-        in_specs=[full(96, W)] * 16
+            jax.ShapeDtypeStruct((144, ROW), bf16),
+            blocks,
+            blocks,
+            block,
+        ),
+        in_specs=[full(48, 2 * W)] * 16
         + [full(SEL, 768), full(2, W)]
         + [pl.BlockSpec((W, TILE), lambda j: (0, j))] * 2
         + [pl.BlockSpec((TILE, W), lambda j: (j, 0))],
-        out_specs=(full(SEL, W), full(SEL, W), full(SEL, 3 * W + 128)),
+        out_specs=(full(SEL, W), full(SEL, W), full(144, ROW))
+        + (full(96, ROW), full(96, ROW), full(48, ROW)),
         scratch_shapes=[pltpu.VMEM((768, 2 * W), bf16), pltpu.VMEM((SEL, W), bf16)],
         compiler_params=params(48),
         cost_estimate=cost(3.6e9, 16e6),
         name="forward",
     )(*parts, put, vectors, w_gate, w_up, w_down)
-    got = lax.all_to_all(send.reshape(8, SEL // 8, -1), "narrow", 0, 0, tiled=True)
-
-    share_d, share_h = pl.pallas_call(
-        hidden_kernel,
-        out_shape=(
-            jax.ShapeDtypeStruct((8, SEL // 8, 2 * W + 128), bf16),
-            jax.ShapeDtypeStruct((8, SEL // 8, W), bf16),
-        ),
-        in_specs=[VMEM],
+
+    from_below = lax.ppermute(to_up, "narrow", XUP)
+    from_above = lax.ppermute(to_down, "narrow", XDOWN)
+    from_y = lax.ppermute(to_y, "narrow", YHI)
+    to_y, to_far = pl.pallas_call(
+        sum_kernel,
+        out_shape=(block, block),
+        in_specs=[VMEM] * 4,
         out_specs=(VMEM, VMEM),
         compiler_params=params(),
+        name="sum",
+    )(keep, from_below, from_above, from_y)
+    from_far = lax.ppermute(to_far, "narrow", XFAR)
+    from_y = lax.ppermute(to_y, "narrow", YHI)
+    own = pl.pallas_call(
+        hidden_kernel,
+        out_shape=block,
+        in_specs=[VMEM] * 5,
+        out_specs=VMEM,
+        compiler_params=params(),
         name="hidden",
-    )(got)
-    gd = lax.all_to_all(share_d, "narrow", 0, 0, tiled=True).reshape(SEL, -1)
-    gd, share_h = lax.optimization_barrier((gd, share_h))
-    hidden = lax.all_to_all(share_h, "narrow", 0, 0, tiled=True).reshape(SEL, W)
+    )(keep, from_below, from_above, from_y, from_far)
+
+    b2 = lax.ppermute(own, "narrow", XFAR)
+    b4 = lax.ppermute(own, "narrow", YHI)
+    column = jnp.concatenate([own, b4], axis=0)
+    below = lax.ppermute(column, "narrow", XUP)
+    above = lax.ppermute(column, "narrow", XDOWN)
+    b6 = lax.ppermute(b2, "narrow", YHI)
 
     theirs, ours, small = pl.pallas_call(
         normed_kernel,
@@ -420,7 +498,8 @@
             jax.ShapeDtypeStruct((SEL, W), bf16),
             jax.ShapeDtypeStruct((8, W), f32),
         ),
-        in_specs=[full(768, SEL), full(SEL, 2 * W + 128)]
+        in_specs=[full(768, SEL), full(48, ROW), full(96, ROW), full(48, ROW), full(96, ROW)]
+        + [full(48, ROW)] * 2
         + [pl.BlockSpec((TILE, W), lambda j: (j, 0))] * 2
         + [pl.BlockSpec((SEL, TILE), lambda j: (0, j))],
         out_specs=(
@@ -428,11 +507,11 @@
             pl.BlockSpec((SEL, TILE), lambda j: (0, j)),
             full(8, W),
         ),
-        scratch_shapes=[pltpu.VMEM((SEL, 128), f32)],
+        scratch_shapes=[pltpu.VMEM((SEL, 2 * W), bf16), pltpu.VMEM((SEL, 128), f32)],
         compiler_params=params(),
         cost_estimate=cost(2.4e9, 9e6),
         name="normed",
-    )(spread, gd, w_gate, w_up, sel)
+    )(spread, own, above, b2, below, b4, b6, w_gate, w_up, sel)
 
     part = jax.ShapeDtypeStruct((56, W), bf16)
     theirs = lax.ppermute(theirs, "wide", CORE)
@@ -475,14 +554,15 @@
     )(ours, theirs, total, *near, along(up2, 2), along(down2, -2))
     there = lax.ppermute(there, "wide", YLO)
 
-    tail = gd[:, 2 * W :].astype(f32)
+    rows = jnp.concatenate([own, above[:48], b2, below[:48], b4, above[48:], b6, below[48:]])
+    tail = rows[:, 3 * W :].astype(f32)
     scale = jnp.sum(tail[:, 0:3], axis=1, keepdims=True)
     logit = jnp.sum(tail[:, 3:6], axis=1, keepdims=True)
     normed = (sel.astype(f32) * scale * gain).astype(bf16)
     d_out = (logit * gsel.astype(f32)).astype(bf16)
-    grad_gate = mm(normed, gd[:, :W], 0, 0).astype(bf16)
-    grad_up = mm(normed, gd[:, W : 2 * W], 0, 0).astype(bf16)
-    grad_down = mm(hidden, d_out, 0, 0).astype(bf16)
+    grad_gate = mm(normed, rows[:, :W], 0, 0).astype(bf16)
+    grad_up = mm(normed, rows[:, W : 2 * W], 0, 0).astype(bf16)
+    grad_down = mm(rows[:, 2 * W : 3 * W], d_out, 0, 0).astype(bf16)
 
     vector = jax.ShapeDtypeStruct((1, W), f32)
     grad_x, d_gain, d_router = pl.pallas_call(

time: 154 us -> 141 us (0.916)
  blocking collectives: 62.1 us -> 0 us
  waiting for transfers between devices: 18.5 us -> 65.6 us
  starting transfers between devices: 38.7 us -> 40.5 us
    all_to_all x2 -> x0, blocking collectives: 62.1 us -> none  [the longest x1 35.7 us: local(): lax.all_to_all(send.reshape(8, SEL // 8, -1), 'narrow', 0, 0, tiled=True)]
    ppermute x1 -> x11, waiting for transfers between devices: 3.54 us -> 44.3 us  [the longest x2 18.3 us: local(): from_y = lax.ppermute(to_y, 'narrow', YHI)]
    ppermute x1 -> x11, starting transfers between devices: 1.37 us -> 12.3 us  [the longest x1 3.22 us: local(): b4 = lax.ppermute(own, 'narrow', YHI)]
    all_to_all x1 -> x0, starting transfers between devices: 8.48 us -> none  [local(): hidden = lax.all_to_all(share_h, 'narrow', 0, 0, tiled=True).reshape(SEL, W)]
    ppermute x12, waiting for transfers between devices: 12.3 us -> 16.6 us  [along(): lax.ppermute(value, 'wide', wide_pairs(lambda z, y, c: (z + 8 + step, y,...]
    ppermute x1, waiting for transfers between devices: 0.01 us -> 1.76 us  [local(): theirs = lax.ppermute(theirs, 'wide', CORE)]
  transfers between devices with their start and end apart: 26 -> 35, of which waited for: 11 -> 22; matrix products, arithmetic and copies ran while one was open for 7% -> 7% of each run, Pallas kernels for 1% -> 1%
where the time goes in v4:
time: 141 us; the launch traced here: 140 us
  waiting for transfers between devices  65.6 us (47%)
  starting transfers between devices  40.5 us (29%)
  Pallas kernels  18.8 us (13%)
  matrix products  8.08 us (6%)
  local copies, waits for them, and re-layouts  5.43 us (4%)
    ppermute x12, starting transfers between devices, along(): lax.ppermute(value, 'wide', wide_pairs(lambda z, y, c: (z + 8 + step, y,...  23.6 us
    ppermute x2, waiting for transfers between devices, local(): from_y = lax.ppermute(to_y, 'narrow', YHI)  18.3 us
    ppermute x12, waiting for transfers between devices, along(): lax.ppermute(value, 'wide', wide_pairs(lambda z, y, c: (z + 8 + step, y,...  16.6 us
    dot_general x3, matrix products, mm(): lax.dot_general(a, b, (((ca,), (cb,)), ((), ())), preferred_element_type=...  8.08 us
    ppermute x1, waiting for transfers between devices, local(): b6 = lax.ppermute(b2, 'narrow', YHI)  7.91 us
    pallas_call x1, Pallas kernels, local(): pl.pallas_call(forward_kernel, grid=(W // TILE,), out_shape=(jax.ShapeDty...  7.8 us
    pallas_call x1, Pallas kernels, local(): pl.pallas_call(normed_kernel, grid=(W // TILE,), out_shape=(jax.ShapeDtyp...  5.79 us
    unnamed x30, local copies, waits for them, and re-layouts  4.61 us
  transfers between devices with their start and end apart: 35, of which 22 were waited for; matrix products, arithmetic and copies ran while one was open for 7% of the time, Pallas kernels for 1%

profile of v4, /device:TPU:22, one launch (start us, length us, event | category | flops | bytes accessed | tf_op | source)
XLA Modules:
  0.0 139.6 jit_solution(7843076762597019587)
XLA Ops:
  0.6 2.0 %own.1 = (bf16[24,2048]{1,0:T(8,128)(2,1)}, s32[1,384]{1,0:T(1,128)}) custom-call(s32[384]{0:T(512)} %sel_hbm.1, bf16[96,1024]{1,0:T(8,128)(2,1)} %tok_hbm.1, bf16[96,1024]{1,0:T(8,128)(2,1)} %go.1), custom_call_target="tpu_custom_call" | custom-call | tf_op jit(solution)/shard_map/own/pallas_call | solution.py:409
  5.0 2.6 %collective-permute-done = bf16[24,2048]{1,0:T(8,128)(2,1)S(1)} collective-permute-done((bf16[24,2048]{1,0:T(8,128)(2,1)}, bf16[24,2048]{1,0:T(8,128)(2,1)S(1)}, u32[]{:S(2)}, u32[]{:S(2)}) %collective-permute-start) | collective-permute-done | bytes 98336 | tf_op jit(solution)/shard_map/ppermute | solution.py:435
  7.6 6.4 %collective-permute-start.5 = (bf16[48,2048]{1,0:T(8,128)(2,1)S(1)}, bf16[48,2048]{1,0:T(8,128)(2,1)S(1)}, u32[]{:S(2)}, u32[]{:S(2)}) collective-permute-start(bf16[48,2048]{1,0:T(8,128)(2,1)S(1)} %constant_dynamic-update-slice_fusion.refs_3_), channel_id=1, source_target_pairs={{0,192},{8,200},{16,208},{24,216},{32,224},{40,232},{48,240},{56,2... | collective-permute-start | bytes 589832 | tf_op jit(solution)/shard_map/ppermute | solution.py:41
  20.2 2.8 %collective-permute-done.5.above.refs_5_ = bf16[48,2048]{1,0:T(8,128)(2,1)S(1)} collective-permute-done((bf16[48,2048]{1,0:T(8,128)(2,1)S(1)}, bf16[48,2048]{1,0:T(8,128)(2,1)S(1)}, u32[]{:S(2)}, u32[]{:S(2)}) %collective-permute-start.5) | collective-permute-done | bytes 196640 | tf_op jit(solution)/shard_map/ppermute | solution.py:41
  23.0 2.4 %collective-permute-done.4.refs_4_ = bf16[48,2048]{1,0:T(8,128)(2,1)S(1)} collective-permute-done((bf16[48,2048]{1,0:T(8,128)(2,1)S(1)}, bf16[48,2048]{1,0:T(8,128)(2,1)S(1)}, u32[]{:S(2)}, u32[]{:S(2)}) %collective-permute-start.4) | collective-permute-done | bytes 196640 | tf_op jit(solution)/shard_map/ppermute | solution.py:41
  25.4 3.7 %collective-permute-start.6 = (bf16[48,2048]{1,0:T(8,128)(2,1)S(1)}, bf16[48,2048]{1,0:T(8,128)(2,1)S(1)}, u32[]{:S(2)}, u32[]{:S(2)}) collective-permute-start(bf16[48,2048]{1,0:T(8,128)(2,1)S(1)} %collective-permute-done.5.above.refs_5_), channel_id=1, source_target_pairs={{0,224},{8,232},{16,240},{24,248},{32,0},{40,8},{48,16},{56,24},{6... | collective-permute-start | bytes 589832 | tf_op jit(solution)/shard_map/ppermute | solution.py:41
  30.7 2.9 %collective-permute-done.6.refs_6_ = bf16[48,2048]{1,0:T(8,128)(2,1)S(1)} collective-permute-done((bf16[48,2048]{1,0:T(8,128)(2,1)S(1)}, bf16[48,2048]{1,0:T(8,128)(2,1)S(1)}, u32[]{:S(2)}, u32[]{:S(2)}) %collective-permute-start.6) | collective-permute-done | bytes 196640 | tf_op jit(solution)/shard_map/ppermute | solution.py:41
  34.1 5.8 %collective-permute-done.2.refs_0_ = bf16[48,2048]{1,0:T(8,128)(2,1)S(1)} collective-permute-done((bf16[48,2048]{1,0:T(8,128)(2,1)S(1)}, bf16[48,2048]{1,0:T(8,128)(2,1)S(1)}, u32[]{:S(2)}, u32[]{:S(2)}) %collective-permute-start.2) | collective-permute-done | bytes 196640 | tf_op jit(solution)/shard_map/ppermute | solution.py:41
  41.6 7.8 %forward.1 = (bf16[384,1024]{1,0:T(8,128)(2,1)S(1)}, bf16[384,1024]{1,0:T(8,128)(2,1)}, bf16[144,3200]{1,0:T(8,128)(2,1)}, bf16[96,3200]{1,0:T(8,128)(2,1)S(1)},...) custom-call(bf16[48,2048]{1,0:T(8,128)(2,1)S(1)} %collective-permute-done.2.refs_0_, ...), custom_call_target="tpu_custom_call" | custom-call | flops 3600000000 | bytes 16000000 | tf_op jit(solution)/shard_map/forward/pallas_call | solution.py:441
  51.8 10.0 %collective-permute-done.18.from_y = bf16[48,3200]{1,0:T(8,128)(2,1)S(1)} collective-permute-done((bf16[48,3200]{1,0:T(8,128)(2,1)S(1)}, bf16[48,3200]{1,0:T(8,128)(2,1)S(1)}, u32[]{:S(2)}, u32[]{:S(2)}) %collective-permute-start.18) | collective-permute-done | bytes 307232 | tf_op jit(solution)/shard_map/ppermute | solution.py:466
  61.8 3.6 %collective-permute-done.16.from_below = bf16[96,3200]{1,0:T(8,128)(2,1)S(1)} collective-permute-done((bf16[96,3200]{1,0:T(8,128)(2,1)S(1)}, bf16[96,3200]{1,0:T(8,128)(2,1)S(1)}, u32[]{:S(2)}, u32[]{:S(2)}) %collective-permute-start.16) | collective-permute-done | bytes 614432 | tf_op jit(solution)/shard_map/ppermute | solution.py:464
  69.9 8.2 %collective-permute-done.19.from_y = bf16[48,3200]{1,0:T(8,128)(2,1)S(1)} collective-permute-done((bf16[48,3200]{1,0:T(8,128)(2,1)S(1)}, bf16[48,3200]{1,0:T(8,128)(2,1)S(1)}, u32[]{:S(2)}, u32[]{:S(2)}) %collective-permute-start.19) | collective-permute-done | bytes 307232 | tf_op jit(solution)/shard_map/ppermute | solution.py:476
  78.9 3.2 %collective-permute-start.21 = (bf16[48,3200]{1,0:T(8,128)(2,1)S(1)}, bf16[48,3200]{1,0:T(8,128)(2,1)S(1)}, u32[]{:S(2)}, u32[]{:S(2)}) collective-permute-start(bf16[48,3200]{1,0:T(8,128)(2,1)S(1)} %hidden.1.own), channel_id=1, source_target_pairs={{0,4},{1,5},{2,6},{3,7},{4,0},{5,1},{6,2},{7,3},{8,12},{9,13},{10,... | collective-permute-start | bytes 921608 | tf_op jit(solution)/shard_map/ppermute | solution.py:487
  83.3 4.4 %collective-permute-done.21.b4 = bf16[48,3200]{1,0:T(8,128)(2,1)S(1)} collective-permute-done((bf16[48,3200]{1,0:T(8,128)(2,1)S(1)}, bf16[48,3200]{1,0:T(8,128)(2,1)S(1)}, u32[]{:S(2)}, u32[]{:S(2)}) %collective-permute-start.21) | collective-permute-done | bytes 307232 | tf_op jit(solution)/shard_map/ppermute | solution.py:487
  89.8 2.5 %collective-permute-done.23.b2 = bf16[48,3200]{1,0:T(8,128)(2,1)S(1)} collective-permute-done((bf16[48,3200]{1,0:T(8,128)(2,1)S(1)}, bf16[48,3200]{1,0:T(8,128)(2,1)S(1)}, u32[]{:S(2)}, u32[]{:S(2)}) %collective-permute-start.23) | collective-permute-done | bytes 307232 | tf_op jit(solution)/shard_map/ppermute | solution.py:486
  92.8 7.9 %collective-permute-done.25.b6 = bf16[48,3200]{1,0:T(8,128)(2,1)S(1)} collective-permute-done((bf16[48,3200]{1,0:T(8,128)(2,1)S(1)}, bf16[48,3200]{1,0:T(8,128)(2,1)S(1)}, u32[]{:S(2)}, u32[]{:S(2)}) %collective-permute-start.25) | collective-permute-done | bytes 307232 | tf_op jit(solution)/shard_map/ppermute | solution.py:491
  101.8 2.4 %collective-permute-done.22.above = bf16[96,3200]{1,0:T(8,128)(2,1)S(1)} collective-permute-done((bf16[96,3200]{1,0:T(8,128)(2,1)S(1)}, bf16[96,3200]{1,0:T(8,128)(2,1)S(1)}, u32[]{:S(2)}, u32[]{:S(2)}) %collective-permute-start.22) | collective-permute-done | bytes 614432 | tf_op jit(solution)/shard_map/ppermute | solution.py:490
  104.2 5.8 %normed.1 = (bf16[392,1024]{1,0:T(8,128)(2,1)S(1)}, bf16[384,1024]{1,0:T(8,128)(2,1)S(1)}, f32[8,1024]{1,0:T(8,128)S(1)}) custom-call(bf16[768,384]{1,0:T(8,128)(2,1)S(1)} %get-tuple-element.36.spread, bf16[48,3200]{1,0:T(8,128)(2,1)S(1)} %hidden.1.own, bf16[96,3200]{1,0:T(8,128)(2,1)S(1)} %collective-permute-done.22.above, ...), custom_call_target="tpu_custom_call" | custom-call | flops 2400000000 | bytes 9000000 | tf_op jit(solution)/shard_map/normed/pallas_call | solution.py:493
  112.6 3.4 %collective-permute-start.29 = (bf16[56,1024]{1,0:T(8,128)(2,1)S(1)}, bf16[56,1024]{1,0:T(8,128)(2,1)S(1)}, u32[]{:S(2)}, u32[]{:S(2)}) collective-permute-start(bf16[56,1024]{1,0:T(8,128)(2,1)S(1)} %get-tuple-element.52), channel_id=1, source_target_pairs={{0,32},{8,40},{16,48},{24,56},{32,64},{40,72},{48,80},{56,88},{64,... | collective-permute-start | bytes 344072 | tf_op jit(solution)/shard_map/ppermute | solution.py:41
  117.5 2.7 %convolution_convert_fusion.1 = bf16[1024,1024]{1,0:T(8,128)(2,1)} fusion(bf16[384,3200]{1,0:T(8,128)(2,1)S(1)} %slice_dynamic-update-slice_fusion, bf16[384,1024]{1,0:T(8,128)(2,1)S(1)} %get-tuple-element.45.sel, f32[1024]{0:T(1024)S(1)} %copy-done.6, f32[384]{0:T(512)S(1)} %get-tuple-element.65), kind=kOutput, calls=%fused_computation.1 | convolution fusion | flops 807927808 | bytes 3676160 | tf_op jit(solution)/shard_map/dot_general | solution.py:73
  120.7 2.8 %collective-permute-start.28 = (bf16[56,1024]{1,0:T(8,128)(2,1)S(1)}, bf16[56,1024]{1,0:T(8,128)(2,1)S(1)}, u32[]{:S(2)}, u32[]{:S(2)}) collective-permute-start(bf16[56,1024]{1,0:T(8,128)(2,1)S(1)} %get-tuple-element.51), channel_id=1, source_target_pairs={{0,224},{8,232},{16,240},{24,248},{32,0},{40,8},{48,16},{56,24},{6... | collective-permute-start | bytes 344072 | tf_op jit(solution)/shard_map/ppermute | solution.py:41
  125.1 4.1 %collective-permute-start.33 = (bf16[56,1024]{1,0:T(8,128)(2,1)S(1)}, bf16[56,1024]{1,0:T(8,128)(2,1)S(1)}, u32[]{:S(2)}, u32[]{:S(2)}) collective-permute-start(bf16[56,1024]{1,0:T(8,128)(2,1)S(1)} %get-tuple-element.56), channel_id=1, source_target_pairs={{0,192},{8,200},{16,208},{24,216},{32,224},{40,232},{48,240},{56,2... | collective-permute-start | bytes 344072 | tf_op jit(solution)/shard_map/ppermute | solution.py:41
  129.2 2.7 %convolution_convert_fusion.2 = bf16[1024,1024]{1,0:T(8,128)(2,1)} fusion(bf16[384,3200]{1,0:T(8,128)(2,1)S(1)} %slice_dynamic-update-slice_fusion, bf16[384,1024]{1,0:T(8,128)(2,1)S(1)} %get-tuple-element.45.sel, f32[1024]{0:T(1024)S(1)} %copy-done.6, f32[384]{0:T(512)S(1)} %get-tuple-element.65), kind=kOutput, calls=%fused_computation.2 | convolution fusion | flops 807927808 | bytes 3676160 | tf_op jit(solution)/shard_map/dot_general | solution.py:73
  135.5 2.7 %convolution_convert_fusion = bf16[1024,1024]{1,0:T(8,128)(2,1)} fusion(bf16[384,1024]{1,0:T(8,128)(2,1)S(1)} %copy-done.10, bf16[384,3200]{1,0:T(8,128)(2,1)S(1)} %slice_dynamic-update-slice_fusion, f32[384]{0:T(512)S(1)} %get-tuple-element.64), kind=kOutput, calls=%fused_computation | convolution fusion | flops 807534592 | bytes 3672064 | tf_op jit(solution)/shard_map/dot_general | solution.py:73
  (96 shorter events, 35.9 us)
Async XLA Ops:
  7.6 15.4 %collective-permute-start.5 = (bf16[48,2048]{1,0:T(8,128)(2,1)S(1)}, bf16[48,2048]{1,0:T(8,128)(2,1)S(1)}, u32[]{:S(2)}, u32[]{:S(2)}) collective-permute-start(bf16[48,2048]{1,0:T(8,128)(2,1)S(1)} %constant_dynamic-update-slice_fusion.refs_3_), channel_id=1, source_target_pairs={{0,192},{8,200},{16,208},{24,216},{32,224},{40,232},{48,240},{56,2... | collective-permute-start | bytes 589832 | tf_op jit(solution)/shard_map/ppermute | solution.py:41
  14.0 11.4 %collective-permute-start.4 = (bf16[48,2048]{1,0:T(8,128)(2,1)S(1)}, bf16[48,2048]{1,0:T(8,128)(2,1)S(1)}, u32[]{:S(2)}, u32[]{:S(2)}) collective-permute-start(bf16[48,2048]{1,0:T(8,128)(2,1)S(1)} %constant_dynamic-update-slice_fusion.refs_3_), channel_id=1, source_target_pairs={{0,224},{8,232},{16,240},{24,248},{32,0},{40,8},{48,16},{56,24},{6... | collective-permute-start | bytes 589832 | tf_op jit(solution)/shard_map/ppermute | solution.py:41
  15.0 14.1 %collective-permute-start.1 = (bf16[48,2048]{1,0:T(8,128)(2,1)S(1)}, bf16[48,2048]{1,0:T(8,128)(2,1)S(1)}, u32[]{:S(2)}, u32[]{:S(2)}) collective-permute-start(bf16[48,2048]{1,0:T(8,128)(2,1)S(1)} %constant_dynamic-update-slice_fusion.refs_3_), channel_id=1, source_target_pairs={{0,64},{8,72},{16,80},{24,88},{32,96},{40,104},{48,112},{56,120},{... | collective-permute-start | bytes 589832 | tf_op jit(solution)/shard_map/ppermute | solution.py:41
  16.5 12.7 %collective-permute-start.11 = (bf16[48,2048]{1,0:T(8,128)(2,1)S(1)}, bf16[48,2048]{1,0:T(8,128)(2,1)S(1)}, u32[]{:S(2)}, u32[]{:S(2)}) collective-permute-start(bf16[48,2048]{1,0:T(8,128)(2,1)S(1)} %constant_dynamic-update-slice_fusion.refs_3_), channel_id=1, source_target_pairs={{0,8},{8,0},{16,24},{24,16},{32,40},{40,32},{48,56},{56,48},{64,72... | collective-permute-start | bytes 589832 | tf_op jit(solution)/shard_map/ppermute | solution.py:401
  16.5 13.6 %collective-permute-start.3 = (bf16[48,2048]{1,0:T(8,128)(2,1)S(1)}, bf16[48,2048]{1,0:T(8,128)(2,1)S(1)}, u32[]{:S(2)}, u32[]{:S(2)}) collective-permute-start(bf16[48,2048]{1,0:T(8,128)(2,1)S(1)} %constant_dynamic-update-slice_fusion.refs_3_), channel_id=1, source_target_pairs={{0,32},{8,40},{16,48},{24,56},{32,64},{40,72},{48,80},{56,88},{64,... | collective-permute-start | bytes 589832 | tf_op jit(solution)/shard_map/ppermute | solution.py:41
  29.2 10.7 %collective-permute-start.2 = (bf16[48,2048]{1,0:T(8,128)(2,1)S(1)}, bf16[48,2048]{1,0:T(8,128)(2,1)S(1)}, u32[]{:S(2)}, u32[]{:S(2)}) collective-permute-start(bf16[48,2048]{1,0:T(8,128)(2,1)S(1)} %collective-permute-done.1.below.refs_1_), channel_id=1, source_target_pairs={{0,32},{8,40},{16,48},{24,56},{32,64},{40,72},{48,80},{56,88},{64,... | collective-permute-start | bytes 589832 | tf_op jit(solution)/shard_map/ppermute | solution.py:41
  30.0 9.9 %collective-permute-start.7 = (bf16[48,2048]{1,0:T(8,128)(2,1)S(1)}, bf16[48,2048]{1,0:T(8,128)(2,1)S(1)}, u32[]{:S(2)}, u32[]{:S(2)}) collective-permute-start(bf16[48,2048]{1,0:T(8,128)(2,1)S(1)} %far.1), channel_id=1, source_target_pairs={{0,64},{8,200},{16,80},{24,216},{32,96},{40,232},{48,112},{56,248}... | collective-permute-start | bytes 589832 | tf_op jit(solution)/shard_map/ppermute | solution.py:399
  30.0 10.4 %collective-permute-start.9 = (bf16[48,2048]{1,0:T(8,128)(2,1)S(1)}, bf16[48,2048]{1,0:T(8,128)(2,1)S(1)}, u32[]{:S(2)}, u32[]{:S(2)}) collective-permute-start(bf16[48,2048]{1,0:T(8,128)(2,1)S(1)} %collective-permute-done.1.below.refs_1_), channel_id=1, source_target_pairs={{0,8},{8,0},{16,24},{24,16},{32,40},{40,32},{48,56},{56,48},{64,72... | collective-permute-start | bytes 589832 | tf_op jit(solution)/shard_map/ppermute | solution.py:401
  49.4 16.0 %collective-permute-start.16 = (bf16[96,3200]{1,0:T(8,128)(2,1)S(1)}, bf16[96,3200]{1,0:T(8,128)(2,1)S(1)}, u32[]{:S(2)}, u32[]{:S(2)}) collective-permute-start(bf16[96,3200]{1,0:T(8,128)(2,1)S(1)} %get-tuple-element.40), channel_id=1, source_target_pairs={{0,1},{1,2},{2,3},{3,0},{4,5},{5,6},{6,7},{7,4},{8,9},{9,10},{10,1... | collective-permute-start | bytes 1843208 | tf_op jit(solution)/shard_map/ppermute | solution.py:464
  49.9 16.9 %collective-permute-start.17 = (bf16[96,3200]{1,0:T(8,128)(2,1)S(1)}, bf16[96,3200]{1,0:T(8,128)(2,1)S(1)}, u32[]{:S(2)}, u32[]{:S(2)}) collective-permute-start(bf16[96,3200]{1,0:T(8,128)(2,1)S(1)} %get-tuple-element.41), channel_id=1, source_target_pairs={{0,3},{1,0},{2,1},{3,2},{4,7},{5,4},{6,5},{7,6},{8,11},{9,8},{10,9... | collective-permute-start | bytes 1843208 | tf_op jit(solution)/shard_map/ppermute | solution.py:465
  51.4 10.4 %collective-permute-start.18 = (bf16[48,3200]{1,0:T(8,128)(2,1)S(1)}, bf16[48,3200]{1,0:T(8,128)(2,1)S(1)}, u32[]{:S(2)}, u32[]{:S(2)}) collective-permute-start(bf16[48,3200]{1,0:T(8,128)(2,1)S(1)} %get-tuple-element.42), channel_id=1, source_target_pairs={{0,4},{1,5},{2,6},{3,7},{4,0},{5,1},{6,2},{7,3},{8,12},{9,13},{10,... | collective-permute-start | bytes 921608 | tf_op jit(solution)/shard_map/ppermute | solution.py:466
  68.3 9.9 %collective-permute-start.19 = (bf16[48,3200]{1,0:T(8,128)(2,1)S(1)}, bf16[48,3200]{1,0:T(8,128)(2,1)S(1)}, u32[]{:S(2)}, u32[]{:S(2)}) collective-permute-start(bf16[48,3200]{1,0:T(8,128)(2,1)S(1)} %get-tuple-element.43), channel_id=1, source_target_pairs={{0,4},{1,5},{2,6},{3,7},{4,0},{5,1},{6,2},{7,3},{8,12},{9,13},{10,... | collective-permute-start | bytes 921608 | tf_op jit(solution)/shard_map/ppermute | solution.py:476
  68.7 9.6 %collective-permute-start.20 = (bf16[48,3200]{1,0:T(8,128)(2,1)S(1)}, bf16[48,3200]{1,0:T(8,128)(2,1)S(1)}, u32[]{:S(2)}, u32[]{:S(2)}) collective-permute-start(bf16[48,3200]{1,0:T(8,128)(2,1)S(1)} %get-tuple-element.44), channel_id=1, source_target_pairs={{0,2},{1,3},{2,0},{3,1},{4,6},{5,7},{6,4},{7,5},{8,10},{9,11},{10,... | collective-permute-start | bytes 921608 | tf_op jit(solution)/shard_map/ppermute | solution.py:475
  78.9 8.8 %collective-permute-start.21 = (bf16[48,3200]{1,0:T(8,128)(2,1)S(1)}, bf16[48,3200]{1,0:T(8,128)(2,1)S(1)}, u32[]{:S(2)}, u32[]{:S(2)}) collective-permute-start(bf16[48,3200]{1,0:T(8,128)(2,1)S(1)} %hidden.1.own), channel_id=1, source_target_pairs={{0,4},{1,5},{2,6},{3,7},{4,0},{5,1},{6,2},{7,3},{8,12},{9,13},{10,... | collective-permute-start | bytes 921608 | tf_op jit(solution)/shard_map/ppermute | solution.py:487
  82.1 10.3 %collective-permute-start.23 = (bf16[48,3200]{1,0:T(8,128)(2,1)S(1)}, bf16[48,3200]{1,0:T(8,128)(2,1)S(1)}, u32[]{:S(2)}, u32[]{:S(2)}) collective-permute-start(bf16[48,3200]{1,0:T(8,128)(2,1)S(1)} %hidden.1.own), channel_id=1, source_target_pairs={{0,2},{1,3},{2,0},{3,1},{4,6},{5,7},{6,4},{7,5},{8,10},{9,11},{10,... | collective-permute-start | bytes 921608 | tf_op jit(solution)/shard_map/ppermute | solution.py:486
  87.7 14.1 %collective-permute-start.24 = (bf16[96,3200]{1,0:T(8,128)(2,1)S(1)}, bf16[96,3200]{1,0:T(8,128)(2,1)S(1)}, u32[]{:S(2)}, u32[]{:S(2)}) collective-permute-start(bf16[96,3200]{1,0:T(8,128)(2,1)S(1)} %pad_maximum_fusion), channel_id=1, source_target_pairs={{0,1},{1,2},{2,3},{3,0},{4,5},{5,6},{6,7},{7,4},{8,9},{9,10},{10,1... | collective-permute-start | bytes 1843208 | tf_op jit(solution)/shard_map/ppermute | solution.py:489
  88.7 15.5 %collective-permute-start.22 = (bf16[96,3200]{1,0:T(8,128)(2,1)S(1)}, bf16[96,3200]{1,0:T(8,128)(2,1)S(1)}, u32[]{:S(2)}, u32[]{:S(2)}) collective-permute-start(bf16[96,3200]{1,0:T(8,128)(2,1)S(1)} %pad_maximum_fusion), channel_id=1, source_target_pairs={{0,3},{1,0},{2,1},{3,2},{4,7},{5,4},{6,5},{7,6},{8,11},{9,8},{10,9... | collective-permute-start | bytes 1843208 | tf_op jit(solution)/shard_map/ppermute | solution.py:490
  92.4 8.4 %collective-permute-start.25 = (bf16[48,3200]{1,0:T(8,128)(2,1)S(1)}, bf16[48,3200]{1,0:T(8,128)(2,1)S(1)}, u32[]{:S(2)}, u32[]{:S(2)}) collective-permute-start(bf16[48,3200]{1,0:T(8,128)(2,1)S(1)} %collective-permute-done.23.b2), channel_id=1, source_target_pairs={{0,4},{1,5},{2,6},{3,7},{4,0},{5,1},{6,2},{7,3},{8,12},{9,13},{10,... | collective-permute-start | bytes 921608 | tf_op jit(solution)/shard_map/ppermute | solution.py:491
  112.6 10.9 %collective-permute-start.29 = (bf16[56,1024]{1,0:T(8,128)(2,1)S(1)}, bf16[56,1024]{1,0:T(8,128)(2,1)S(1)}, u32[]{:S(2)}, u32[]{:S(2)}) collective-permute-start(bf16[56,1024]{1,0:T(8,128)(2,1)S(1)} %get-tuple-element.52), channel_id=1, source_target_pairs={{0,32},{8,40},{16,48},{24,56},{32,64},{40,72},{48,80},{56,88},{64,... | collective-permute-start | bytes 344072 | tf_op jit(solution)/shard_map/ppermute | solution.py:41
  116.1 8.7 %collective-permute-start.31 = (bf16[56,1024]{1,0:T(8,128)(2,1)S(1)}, bf16[56,1024]{1,0:T(8,128)(2,1)S(1)}, u32[]{:S(2)}, u32[]{:S(2)}) collective-permute-start(bf16[56,1024]{1,0:T(8,128)(2,1)S(1)} %get-tuple-element.54), channel_id=1, source_target_pairs={{0,64},{8,200},{16,80},{24,216},{32,96},{40,232},{48,112},{56,248}... | collective-permute-start | bytes 344072 | tf_op jit(solution)/shard_map/ppermute | solution.py:527
  120.2 11.7 %collective-permute-start.27 = (bf16[56,1024]{1,0:T(8,128)(2,1)S(1)}, bf16[56,1024]{1,0:T(8,128)(2,1)S(1)}, u32[]{:S(2)}, u32[]{:S(2)}) collective-permute-start(bf16[56,1024]{1,0:T(8,128)(2,1)S(1)} %get-tuple-element.50), channel_id=1, source_target_pairs={{0,32},{8,40},{16,48},{24,56},{32,64},{40,72},{48,80},{56,88},{64,... | collective-permute-start | bytes 344072 | tf_op jit(solution)/shard_map/ppermute | solution.py:41
  120.7 11.2 %collective-permute-start.28 = (bf16[56,1024]{1,0:T(8,128)(2,1)S(1)}, bf16[56,1024]{1,0:T(8,128)(2,1)S(1)}, u32[]{:S(2)}, u32[]{:S(2)}) collective-permute-start(bf16[56,1024]{1,0:T(8,128)(2,1)S(1)} %get-tuple-element.51), channel_id=1, source_target_pairs={{0,224},{8,232},{16,240},{24,248},{32,0},{40,8},{48,16},{56,24},{6... | collective-permute-start | bytes 344072 | tf_op jit(solution)/shard_map/ppermute | solution.py:41
  125.0 8.9 %collective-permute-start.32 = (bf16[56,1024]{1,0:T(8,128)(2,1)S(1)}, bf16[56,1024]{1,0:T(8,128)(2,1)S(1)}, u32[]{:S(2)}, u32[]{:S(2)}) collective-permute-start(bf16[56,1024]{1,0:T(8,128)(2,1)S(1)} %get-tuple-element.55), channel_id=1, source_target_pairs={{0,64},{8,72},{16,80},{24,88},{32,96},{40,104},{48,112},{56,120},{... | collective-permute-start | bytes 344072 | tf_op jit(solution)/shard_map/ppermute | solution.py:41
  125.1 8.8 %collective-permute-start.33 = (bf16[56,1024]{1,0:T(8,128)(2,1)S(1)}, bf16[56,1024]{1,0:T(8,128)(2,1)S(1)}, u32[]{:S(2)}, u32[]{:S(2)}) collective-permute-start(bf16[56,1024]{1,0:T(8,128)(2,1)S(1)} %get-tuple-element.56), channel_id=1, source_target_pairs={{0,192},{8,200},{16,208},{24,216},{32,224},{40,232},{48,240},{56,2... | collective-permute-start | bytes 344072 | tf_op jit(solution)/shard_map/ppermute | solution.py:41
  (22 other events, 160.9 us)
